TPU v7x, 256 devices: a whole 4x4x8 slice. The times are simulated.
256 devices in a mesh: dp: 8 (over x_hi, y), feat: 32 (over z, x_lo, core).
Axes of the slice: x: 4 (x_hi: 2, x_lo: 2; x = x_hi * 2 + x_lo), y: 4, z: 8, core: 2. Of those that a mesh axis runs over, the one named last changes fastest.
Arguments:
- view_a: bfloat16 [3072, 1536], P('dp'), may hold values from -24 to 24
- view_b: bfloat16 [3072, 1536], P('dp'), may hold values from -24 to 24
- proj_weight: bfloat16 [1536, 8192], P(None, 'feat'), may hold values from -0.15625 to 0.15625
Outputs:
- grad_a: float32 [3072, 8192], P('dp', 'feat')
- grad_b: float32 [3072, 8192], P('dp', 'feat')
All inputs are finite; a program needn't handle non-finite values.
Results may differ from a plain program's by a relative error of at most 0.0023.
Values may be sent and summed in bfloat16 or wider, within the bound.
No kernel may reach another device: no remote copies, remote signals or barrier semaphores. Data moves between devices by JAX's collectives and lax.ppermute only.
A program may use at most 128 MiB of HBM per device.

v0:
```python
import jax
import jax.numpy as jnp
from jax import lax
from jax.sharding import PartitionSpec as P

off_weight = 0.5


def local(view_a, view_b, proj_weight):
    rows = view_a.shape[0]
    block = proj_weight.shape[1]
    groups = lax.axis_size("dp")
    total = rows * groups
    proj_a = jnp.dot(view_a, proj_weight, preferred_element_type=jnp.float32)
    proj_b = jnp.dot(view_b, proj_weight, preferred_element_type=jnp.float32)
    sum_a, square_a, sum_b, square_b = lax.psum(
        (
            jnp.sum(proj_a, axis=0),
            jnp.sum(proj_a * proj_a, axis=0),
            jnp.sum(proj_b, axis=0),
            jnp.sum(proj_b * proj_b, axis=0),
        ),
        "dp",
    )
    mean_a = sum_a / total
    mean_b = sum_b / total
    norm_a = ((proj_a - mean_a) * lax.rsqrt(square_a / total - mean_a * mean_a + 1e-05)).astype(
        jnp.bfloat16
    )
    norm_b = ((proj_b - mean_b) * lax.rsqrt(square_b / total - mean_b * mean_b + 1e-05)).astype(
        jnp.bfloat16
    )
    whole_b = lax.all_gather(norm_b, "feat", axis=1, tiled=True)
    partial_value = (
        lax.dot_general(
            norm_a, whole_b, (((0,), (0,)), ((), ())), preferred_element_type=jnp.float32
        )
        / total
    )
    row_ids = lax.axis_index("feat") * block + jnp.arange(block, dtype=jnp.int32)[:, None]
    tile = lax.psum_scatter(partial_value, "dp", scatter_dimension=1, tiled=True)
    span = tile.shape[1]
    col_ids = lax.axis_index("dp") * span + jnp.arange(span, dtype=jnp.int32)[None, :]
    grad_tile = jnp.where(row_ids == col_ids, -2.0 * (1.0 - tile), 2.0 * off_weight * tile).astype(
        jnp.bfloat16
    )
    grad_block = lax.all_gather(grad_tile, "dp", axis=1, tiled=True)
    grad_a = lax.dot_general(
        whole_b, grad_block, (((1,), (1,)), ((), ())), preferred_element_type=jnp.float32
    )
    grad_b_rows = lax.psum_scatter(
        lax.dot_general(
            grad_block, norm_a, (((0,), (1,)), ((), ())), preferred_element_type=jnp.float32
        ),
        "feat",
        scatter_dimension=0,
        tiled=True,
    )
    grad_b = grad_b_rows.T
    return (grad_a, grad_b)


def solution(mesh):
    return jax.shard_map(
        local,
        mesh=mesh,
        in_specs=(P("dp", None), P("dp", None), P(None, "feat")),
        out_specs=(P("dp", "feat"), P("dp", "feat")),
        check_vma=False,
    )
```

profile of v0, /device:TPU:1, one launch (start us, length us, event | category | flops | bytes accessed | tf_op | source)
XLA Modules:
  0.0 484.5 jit_solution(6950234468098165803)
XLA Ops:
  7.2 0.0 copy-start
  7.2 0.0 all-gather.3.cloned.1.call-start
  7.2 1.2 copy-done
  8.4 1.6 fusion.1
  10.1 2.0 fusion.2
  12.0 21.5 %all-reduce = (f32[256]{0:T(256)S(1)}, f32[256]{0:T(256)S(1)}, f32[256]{0:T(256)S(1)}, f32[256]{0:T(256)S(1)}) all-reduce(f32[256]{0:T(256)S(1)} %get-tuple-element.7, f32[256]{0:T(256)S(1)} %get-tuple-element.6, f32[256]{0:T(256)S(1)} %get-tuple-element.5, f32[256]{0:T(256)S(1)} %get-tuple-element.4), channel_id=1, replica_groups=mesh['dp'=8,'feat'=32] {'dp'}, use_global_device_ids=true, to_apply=%region_3.0 | all-reduce | flops 1024 | bytes 8192 | tf_op jit(solution)/shard_map/psum | solution.py:16
  33.6 0.7 multiply_convert_fusion.1
  34.3 0.0 all-gather.3.cloned.1.call-update
  34.3 0.0 reduce-scatter.3.cloned.1.call-start
  34.4 83.3 %all-gather.3.cloned.1.call-done = bf16[384,8192]{1,0:T(8,128)(2,1)} async-done(((bf16[384,256]{1,0:T(8,128)(2,1)}), bf16[384,8192]{1,0:T(8,128)(2,1)}) %all-gather.3.cloned.1.call-update) | async-done | bytes 6291472 | tf_op jit(solution)/shard_map/all_gather | solution.py:33
  117.6 8.4 %convolution_multiply_fusion = f32[256,8192]{1,0:T(8,128)} fusion(bf16[384,8192]{1,0:T(8,128)(2,1)} %all-gather.3.cloned.1.call-done, f32[384,256]{1,0:T(8,128)S(1)} %get-tuple-element.17, f32[256]{0:T(256)S(1)} %get-tuple-element.13, f32[256]{0:T(256)S(1)} %get-tuple-element.12), kind=kOutput, calls=%fused_computation | convolution fusion | flops 1613004800 | bytes 15075328 | tf_op jit(solution)/shard_map/dot_general | solution.py:35
  126.0 0.0 reduce-scatter.3.cloned.1.call-update
  126.0 0.0 all-gather.5.cloned.1.call-start
  126.1 117.0 %reduce-scatter.3.cloned.1.call-done = f32[256,1024]{1,0:T(8,128)} async-done(((f32[256,8192]{1,0:T(8,128)}), f32[256,1024]{1,0:T(8,128)}) %reduce-scatter.3.cloned.1.call-update) | async-done | bytes 1048592 | tf_op jit(solution)/shard_map/reduce_scatter | solution.py:41
  243.1 2.2 select_convert_fusion
  245.3 0.0 all-gather.5.cloned.1.call-update
  245.3 0.0 reduce-scatter.5.cloned.1.call-start
  245.4 75.2 %all-gather.5.cloned.1.call-done = bf16[256,8192]{1,0:T(8,128)(2,1)} async-done(((bf16[256,1024]{1,0:T(8,128)(2,1)}), bf16[256,8192]{1,0:T(8,128)(2,1)}) %all-gather.5.cloned.1.call-update) | async-done | bytes 4194320 | tf_op jit(solution)/shard_map/all_gather | solution.py:47
  320.6 9.2 %fusion = f32[8192,384]{1,0:T(8,128)} fusion(bf16[256,8192]{1,0:T(8,128)(2,1)} %all-gather.5.cloned.1.call-done, f32[384,256]{1,0:T(8,128)S(1)} %get-tuple-element.17, f32[256]{0:T(256)S(1)} %get-tuple-element.13, f32[256]{0:T(256)S(1)} %get-tuple-element.12), kind=kOutput, calls=%fused_computation.6 | convolution fusion | flops 1610907648 | bytes 17172480 | tf_op jit(solution)/shard_map/dot_general | solution.py:52
  329.8 0.0 reduce-scatter.5.cloned.1.call-update
  329.8 6.6 %fusion.3 = f32[384,256]{1,0:T(8,128)} fusion(bf16[384,8192]{1,0:T(8,128)(2,1)} %all-gather.3.cloned.1.call-done, bf16[256,8192]{1,0:T(8,128)(2,1)} %all-gather.5.cloned.1.call-done), kind=kOutput, calls=%fused_computation.15 | convolution fusion | flops 1610612736 | bytes 10878976 | tf_op jit(solution)/shard_map/dot_general | solution.py:48
  336.4 139.7 %reduce-scatter.5.cloned.1.call-done = f32[256,384]{1,0:T(8,128)} async-done(((f32[8192,384]{1,0:T(8,128)}), f32[256,384]{1,0:T(8,128)}) %reduce-scatter.5.cloned.1.call-update) | async-done | bytes 393232 | tf_op jit(solution)/shard_map/reduce_scatter | solution.py:51
  476.0 1.9 copy.5
  (4 shorter events, 0.0 us)
Async XLA Ops:
  7.2 1.3 copy-start
  7.2 110.4 %all-gather.3.cloned.1.call-start = ((), (), s32[]{:S(2)}) async-start(), calls=%async_computation.2 | async-start | bytes 6488064 | tf_op jit(solution)/shard_map/all_gather | solution.py:33
  34.3 208.8 %reduce-scatter.3.cloned.1.call-start = ((), (), s32[]{:S(2)}) async-start(), calls=%async_computation.3 | async-start | bytes 9437184 | tf_op jit(solution)/shard_map/reduce_scatter | solution.py:41
  126.0 194.6 %all-gather.5.cloned.1.call-start = ((), (), s32[]{:S(2)}) async-start(), calls=%async_computation.4 | async-start | bytes 4718592 | tf_op jit(solution)/shard_map/all_gather | solution.py:47
  245.3 230.7 %reduce-scatter.5.cloned.1.call-start = ((), (), s32[]{:S(2)}) async-start(), calls=%async_computation.5 | async-start | bytes 12976128 | tf_op jit(solution)/shard_map/reduce_scatter | solution.py:51
Sparse Core Ops, SparseCore 0:
  34.4 83.1 all-gather.2
  126.2 116.8 reduce-scatter.2
  246.0 74.5 all-gather.4
  329.9 146.0 reduce-scatter.4
where the time goes:
time: 485 us; the launch traced here: 484 us
  waiting for transfers between devices  415 us (86%)
  matrix products  27.7 us (6%)
  blocking collectives  21.5 us (4%)
  between operations  13.8 us (3%)
    reduce_scatter x1, waiting for transfers between devices, local(): lax.psum_scatter(lax.dot_general(grad_block, norm_a, (((0,), (1,)), ((),...  140 us
    reduce_scatter x1, waiting for transfers between devices, local(): lax.psum_scatter(partial_value, 'dp', scatter_dimension=1, tiled=True)  117 us
    all_gather x1, waiting for transfers between devices, local(): whole_b = lax.all_gather(norm_b, 'feat', axis=1, tiled=True)  83.3 us
    all_gather x1, waiting for transfers between devices, local(): grad_block = lax.all_gather(grad_tile, 'dp', axis=1, tiled=True)  75.2 us
    psum x1, blocking collectives, local(): lax.psum((jnp.sum(proj_a, axis=0), jnp.sum(proj_a * proj_a, axis=0), jnp....  21.5 us
  transfers between devices with their start and end apart: 4, of which 4 were waited for; matrix products, arithmetic and copies ran while one was open for 1% of the time, Pallas kernels for 0%

commit v1 on v0

v1 whole, which is shorter than its diff:
```python
import jax
import jax.numpy as jnp
import numpy as np
from jax import lax
from jax.experimental import pallas as pl
from jax.experimental.pallas import tpu as pltpu
from jax.sharding import Mesh, PartitionSpec as P

DP = ("xh", "y")
FEAT = ("z", "xl", "c")
PARTS = {"xh": 2, "y": 4, "z": 8, "xl": 2, "c": 2}
SWAP = [(0, 1), (1, 0)]
U_SCALE = 1024.0
EPS = 1e-05
f32, bf16, f16 = jnp.float32, jnp.bfloat16, jnp.float16

ROWS = 384
TOTAL = 3072
DEPTH = 1536
BLOCK = 256
QUARTER = ROWS // 4
PIECE = (48, 768)
SHARE = DEPTH // 4
VMEM = pl.BlockSpec(memory_space=pltpu.VMEM)
SMEM = pl.BlockSpec(memory_space=pltpu.SMEM)


def exchange(blocks, axes):
    return lax.all_to_all(blocks, axes, split_axis=0, concat_axis=0, tiled=True)


def dot(a, b, ca, cb):
    return lax.dot_general(a, b, (((ca,), (cb,)), ((), ())), preferred_element_type=f32)


def call(body, out, n_in, flops, nbytes, scratch=(), smem=False, name=None, vmem=60):
    return pl.pallas_call(
        body,
        out_shape=out,
        in_specs=([SMEM] if smem else []) + [VMEM] * n_in,
        out_specs=jax.tree.map(lambda _: VMEM, out),
        scratch_shapes=scratch,
        compiler_params=pltpu.CompilerParams(vmem_limit_bytes=vmem * 2**20),
        cost_estimate=pl.CostEstimate(flops=flops, bytes_accessed=nbytes, transcendentals=0),
        name=name,
    )


def project(va, vb, w, pa, pb, sums):
    a = dot(va[...], w[...], 1, 0)
    b = dot(vb[...], w[...], 1, 0)
    pa[...] = a
    pb[...] = b
    col = [jnp.sum(t, axis=0, keepdims=True) for t in (a, a * a, b, b * b, a * b)]
    own = jnp.concatenate(col + [jnp.zeros((3, BLOCK), f32)], axis=0)
    sums[...] = jnp.broadcast_to(own[None], sums.shape)


def moments(sums, q):
    t = sums[q]
    for d in range(1, 8):
        t = t + sums[4 * d + q]
    t = t * (1.0 / TOTAL)
    ma, mb = t[0:1], t[2:3]
    ra = lax.rsqrt(t[1:2] - ma * ma + EPS)
    rb = lax.rsqrt(t[3:4] - mb * mb + EPS)
    return ma, ra, mb, rb, (t[4:5] - ma * mb) * ra * rb


def embed(place, sums, va, vb, w0, w1, w2, w3, y, na, nb):
    q = place[0]
    at = pl.ds(pl.multiple_of(q * QUARTER, 32), QUARTER)
    v = jnp.concatenate([va[at, :], vb[at, :]], axis=0)
    ws = (w0, w1, w2, w3)
    for j, wj in enumerate(ws):
        ma, ra, mb, rb, _ = moments(sums, q ^ j)
        p = dot(v, wj[...], 1, 0)
        cols = slice(j * BLOCK, (j + 1) * BLOCK)
        na[:, cols] = ((p[:QUARTER] - ma) * (ra * ra)).astype(bf16)
        nb[:, cols] = ((p[QUARTER:] - mb) * (rb * rb)).astype(bf16)
    n = jnp.concatenate([na[...], nb[...]], axis=0)
    for k in range(6):
        rows = slice(k * 256, (k + 1) * 256)
        acc = dot(n[:, :BLOCK], w0[rows, :], 1, 1)
        for j in range(1, 4):
            acc = acc + dot(n[:, j * BLOCK : (j + 1) * BLOCK], ws[j][rows, :], 1, 1)
        acc = acc.astype(bf16)
        for i in range(4):
            y[2 * i + k // 3, :, (k % 3) * 256 : (k % 3 + 1) * 256] = acc[48 * i : 48 * i + 48]


def add_copies(parts, out):
    total = parts[0].astype(f32)
    for d in range(1, 8):
        total = total + parts[d].astype(f32)
    out[...] = jnp.broadcast_to(total.astype(bf16)[None], out.shape)


def turn(va, vb, ta, tb):
    for view, out in ((va, ta), (vb, tb)):
        v = view[...]
        centre = jnp.sum(v.astype(f32), axis=0, keepdims=True) * (1.0 / ROWS)
        centre = jnp.concatenate([centre, jnp.zeros((15, DEPTH), f32)], axis=0).astype(bf16)
        out[...] = jnp.concatenate([v, centre, jnp.zeros((112, DEPTH), bf16)], axis=0).T


def correlate(place, sums, pa, pb, ta, tb, u):
    q, yy = place[0], place[1]
    ma, ra, mb, rb, _ = moments(sums, q)
    for first, p, m, s, t in ((0, pa, ma, ra, tb), (BLOCK, pb, mb, rb, ta)):
        n = (p[...] - m) * s
        rounded = n.astype(bf16)
        excess = jnp.sum(n - rounded.astype(f32), axis=0, keepdims=True)
        excess = jnp.concatenate([excess, jnp.zeros((15, BLOCK), f32)], axis=0).astype(bf16)
        n = jnp.concatenate([rounded, excess, jnp.zeros((112, BLOCK), bf16)], axis=0)
        for b in range(4):
            part = dot(t[b * SHARE : (b + 1) * SHARE, :], n, 1, 0)
            u[b ^ yy, :, first : first + BLOCK] = part * (U_SCALE / TOTAL)


def combine(place, sums, pa, pb, y0, y1, y2, y3, u, out_a, out_b, ya, yb):
    q = place[0]
    for j, yj in enumerate((y0, y1, y2, y3)):
        for i in range(4):
            at = pl.multiple_of((q ^ j) * QUARTER + (i & 1) * 48, 16)
            for h in range(2):
                (ya if i < 2 else yb)[pl.ds(at, 48), h * 768 : (h + 1) * 768] = yj[2 * i + h]
    ma, ra, mb, rb, corr = moments(sums, q)
    for first, y, p, m, s, out in (
        (0, yb, pb, mb, rb, out_a),
        (BLOCK, ya, pa, ma, ra, out_b),
    ):
        acc = (p[...] - m) * (s * (corr - 2.0))
        cols = slice(first, first + BLOCK)
        out[...] = acc + (dot(y[...], u[:DEPTH, cols], 1, 0) + dot(y[...], u[DEPTH:, cols], 1, 0))


def mark(arrived, out):
    out[...] = jnp.zeros(out.shape, f32)


def after(arrived, waiting):
    done = pl.pallas_call(
        mark,
        out_shape=jax.ShapeDtypeStruct((8, 128), f32),
        in_specs=[pl.BlockSpec(memory_space=pl.ANY)],
        out_specs=VMEM,
        cost_estimate=pl.CostEstimate(flops=10**11, bytes_accessed=10**8, transcendentals=0),
        name="mark",
    )(arrived)
    return lax.optimization_barrier((waiting, done))[0]


def split(place, u0, u1, u2, u3, u):
    yy = place[1]
    for s, us in enumerate((u0, u1, u2, u3)):
        x = us[...] * (1.0 / U_SCALE)
        high = x.astype(bf16)
        at = pl.multiple_of((yy ^ s) * SHARE, 128)
        u[pl.ds(at, SHARE), :] = high
        u[pl.ds(DEPTH + at, SHARE), :] = (x - high.astype(f32)).astype(bf16)


def local(va, vb, w):
    q = lax.axis_index("xl") * 2 + lax.axis_index("c")
    place = jnp.stack([q, lax.axis_index("y")]).astype(jnp.int32)
    shape = jax.ShapeDtypeStruct
    tie = lax.optimization_barrier

    w_x = lax.ppermute(w, "xl", SWAP)
    w_c = lax.ppermute(w, "c", SWAP)

    pa, pb, own = call(
        project,
        (shape((ROWS, BLOCK), f32), shape((ROWS, BLOCK), f32), shape((32, 8, BLOCK), f32)),
        3,
        4 * ROWS * DEPTH * BLOCK,
        4 * 2**20,
        name="project",
    )(va, vb, w)
    sums = exchange(own, ("xh", "y", "xl", "c"))
    va_, vb_, _ = tie((va, vb, own))
    ta, tb = call(
        turn, (shape((DEPTH, 512), bf16),) * 2, 2, 10 * 2**20, 6 * 2**20, name="turn"
    )(va_, vb_)
    sums, w_x, w_c, ta, tb = tie((sums, w_x, w_c, ta, tb))
    w_xc = lax.ppermute(w_x, "c", SWAP)

    u_parts = call(
        correlate,
        shape((4, SHARE, 2 * BLOCK), f32),
        5,
        4 * ROWS * DEPTH * BLOCK,
        6 * 2**20,
        smem=True,
        name="correlate",
    )(place, sums, pa, pb, ta, tb)

    def along_y(t, s):
        return lax.ppermute(t, "y", [(i, i ^ s) for i in range(4)])

    u_send = [u_parts[s].astype(f16) for s in (1, 2, 3)]
    sums_, *u_send = tie((sums, *u_send))
    u_recv = [along_y(t, s) for s, t in enumerate(u_send, 1)]

    y_part = call(
        embed,
        shape((8,) + PIECE, bf16),
        7,
        16 * ROWS * DEPTH * BLOCK // 2,
        7 * 2**20,
        [pltpu.VMEM((QUARTER, 4 * BLOCK), bf16)] * 2,
        smem=True,
        name="embed",
    )(place, sums_, va, vb, w, w_c, w_x, w_xc)
    y_parts = exchange(y_part, "z")

    u = u_parts[0]
    for t in u_recv:
        u = u + t.astype(f32)
    u = u.astype(f16)
    u_far = lax.ppermute(u, "xh", SWAP)

    y_parts = after(u, y_parts)
    y_copies = call(
        add_copies, shape((8,) + PIECE, bf16), 1, 10 * 2**20, 2**20, name="add_copies"
    )(y_parts)
    y0 = exchange(y_copies, "z")

    u = (u.astype(f32) + u_far.astype(f32)).astype(f16)
    us = [u] + [along_y(u, s) for s in (1, 2, 3)]
    u = call(
        split,
        shape((2 * DEPTH, 2 * BLOCK), bf16),
        4,
        10**11,
        10**8,
        smem=True,
        name="split",
    )(place, *[t.astype(f32) for t in us])

    y0 = after(u, y0)
    y2 = lax.ppermute(y0, "xl", SWAP)
    y1 = lax.ppermute(y0, "c", SWAP)
    y3 = lax.ppermute(y2, "c", SWAP)

    return call(
        combine,
        (shape((ROWS, BLOCK), f32),) * 2,
        8,
        8 * ROWS * DEPTH * BLOCK,
        8 * 2**20,
        [pltpu.VMEM((ROWS, DEPTH), bf16)] * 2,
        smem=True,
        name="combine",
    )(place, sums, pa, pb, y0, y1, y2, y3, u)


def solution(mesh):
    fine = Mesh(np.asarray(mesh.devices).reshape(tuple(PARTS.values())), tuple(PARTS))
    return jax.shard_map(
        local,
        mesh=fine,
        in_specs=(P(DP, None), P(DP, None), P(None, FEAT)),
        out_specs=(P(DP, FEAT), P(DP, FEAT)),
        check_vma=False,
    )
```

time: 485 us -> 133 us (0.27)
  waiting for transfers between devices: 415 us -> 57.8 us
  starting transfers between devices: 0.16 us -> 33.2 us
  Pallas kernels: 0 us -> 29.1 us
  matrix products: 27.7 us -> 0 us
  blocking collectives: 21.5 us -> 0 us
  between operations: 13.8 us -> 0.75 us
  other arithmetic: 2.94 us -> 8.34 us
    reduce_scatter x2 -> x0, waiting for transfers between devices: 257 us -> none  [the longest x1 140 us: local(): lax.psum_scatter(lax.dot_general(grad_block, norm_a, (((0,), (1,)), ((),...]
    all_gather x2 -> x0, waiting for transfers between devices: 158 us -> none  [the longest x1 83.3 us: local(): whole_b = lax.all_gather(norm_b, 'feat', axis=1, tiled=True)]
    all_to_all x0 -> x3, waiting for transfers between devices: none -> 43.1 us  [exchange(): return lax.all_to_all(blocks, axes, split_axis=0, concat_axis=0, tiled=True)]
    pallas_call x0 -> x7, Pallas kernels: none -> 29.1 us  [the longest x1 5.34 us: local(): call(combine, (shape((ROWS, BLOCK), f32),) * 2, 8, 8 * ROWS * DEPTH * BLO...]
    dot_general x5 -> x0, matrix products: 27.7 us -> none  [the longest x1 9.16 us: local(): lax.dot_general(grad_block, norm_a, (((0,), (1,)), ((), ())), preferred_e...]
    psum x1 -> x0, blocking collectives: 21.5 us -> none  [local(): lax.psum((jnp.sum(proj_a, axis=0), jnp.sum(proj_a * proj_a, axis=0), jnp....]
    all_to_all x0 -> x3, starting transfers between devices: none -> 18.3 us  [exchange(): return lax.all_to_all(blocks, axes, split_axis=0, concat_axis=0, tiled=True)]
    ppermute x0 -> x13, starting transfers between devices: none -> 14.9 us  [the longest x6 7.72 us: along_y(): return lax.ppermute(t, 'y', [(i, i ^ s) for i in range(4)])]
  transfers between devices with their start and end apart: 4 -> 16, of which waited for: 4 -> 6; matrix products, arithmetic and copies ran while one was open for 1% -> 6% of each run, Pallas kernels for 0% -> 14%
where the time goes in v1:
time: 133 us
  waiting for transfers between devices  57.8 us (43%)
  starting transfers between devices  33.2 us (25%)
  Pallas kernels  29.1 us (22%)
  other arithmetic  8.34 us (6%)
  local copies, waits for them, and re-layouts  3.61 us (3%)
    all_to_all x3, waiting for transfers between devices, exchange(): return lax.all_to_all(blocks, axes, split_axis=0, concat_axis=0, tiled=True)  43.1 us
    all_to_all x3, starting transfers between devices, exchange(): return lax.all_to_all(blocks, axes, split_axis=0, concat_axis=0, tiled=True)  18.3 us
    ppermute x6, waiting for transfers between devices, along_y(): return lax.ppermute(t, 'y', [(i, i ^ s) for i in range(4)])  14.7 us
    ppermute x6, starting transfers between devices, along_y(): return lax.ppermute(t, 'y', [(i, i ^ s) for i in range(4)])  7.72 us
    pallas_call x1, Pallas kernels, local(): call(combine, (shape((ROWS, BLOCK), f32),) * 2, 8, 8 * ROWS * DEPTH * BLO...  5.34 us
    pallas_call x1, Pallas kernels, local(): call(embed, shape((8,) + PIECE, bf16), 7, 16 * ROWS * DEPTH * BLOCK // 2,...  5.25 us
    pallas_call x1, Pallas kernels, local(): call(correlate, shape((4, SHARE, 2 * BLOCK), f32), 5, 4 * ROWS * DEPTH *...  5.05 us
    pallas_call x1, Pallas kernels, local(): call(split, shape((2 * DEPTH, 2 * BLOCK), bf16), 4, 10 ** 11, 10 ** 8, sm...  4.19 us
  transfers between devices with their start and end apart: 16, of which 6 were waited for; matrix products, arithmetic and copies ran while one was open for 6% of the time, Pallas kernels for 14%

profile of v1, /device:TPU:1, one launch (start us, length us, event | category | flops | bytes accessed | tf_op | source)
XLA Modules:
  0.0 132.9 jit_solution(1395852119037437889)
XLA Ops:
  0.6 2.1 %collective-permute-start = (bf16[1536,256]{1,0:T(8,128)(2,1)}, bf16[1536,256]{1,0:T(8,128)(2,1)S(1)}, u32[]{:S(2)}, u32[]{:S(2)}) collective-permute-start(bf16[1536,256]{1,0:T(8,128)(2,1)} %w0.1), channel_id=1, source_target_pairs={{0,2},{2,0},{1,3},{3,1},{4,6},{6,4},{5,7},{7,5},{8,10},{10,8},{9,1... | collective-permute-start | bytes 2359304 | tf_op jit(solution)/shard_map/ppermute | solution.py:170
  2.8 1.3 collective-permute-start.1
  4.1 3.6 %project.1 = (f32[384,256]{1,0:T(8,128)}, f32[384,256]{1,0:T(8,128)}, f32[32,8,256]{2,1,0:T(8,128)}) custom-call(bf16[384,1536]{1,0:T(8,128)(2,1)} %va.4, bf16[384,1536]{1,0:T(8,128)(2,1)} %vb.4, bf16[1536,256]{1,0:T(8,128)(2,1)} %w0.1), custom_call_target="tpu_custom_call" | custom-call | flops 603979776 | bytes 4194304 | tf_op jit(solution)/shard_map/project/pallas_call | solution.py:173
  7.6 6.6 %all-to-all-start = ((f32[32,8,256]{2,1,0:T(8,128)}), f32[32,8,256]{2,1,0:T(8,128)S(1)}, u32[]{:S(2)}, u32[]{:S(2)}) async-start(f32[32,8,256]{2,1,0:T(8,128)} %get-tuple-element.18), calls=%async_computation | async-start | bytes 524288 | tf_op jit(solution)/shard_map/all_to_all | solution.py:29
  14.2 3.8 %turn.1 = (bf16[1536,512]{1,0:T(8,128)(2,1)}, bf16[1536,512]{1,0:T(8,128)(2,1)}) custom-call(bf16[384,1536]{1,0:T(8,128)(2,1)} %va.4, bf16[384,1536]{1,0:T(8,128)(2,1)} %vb.4), custom_call_target="tpu_custom_call" | custom-call | flops 10485760 | bytes 6291456 | tf_op jit(solution)/shard_map/turn/pallas_call | solution.py:183
  18.0 10.3 %all-to-all-done.sums = f32[32,8,256]{2,1,0:T(8,128)S(1)} async-done(((f32[32,8,256]{2,1,0:T(8,128)}), f32[32,8,256]{2,1,0:T(8,128)S(1)}, u32[]{:S(2)}, u32[]{:S(2)}) %all-to-all-start) | async-done | bytes 262176 | tf_op jit(solution)/shard_map/all_to_all | solution.py:29
  29.8 5.1 %correlate.1 = f32[4,384,512]{2,1,0:T(8,128)} custom-call(s32[2]{0:T(128)} %pad_add_fusion.place, f32[32,8,256]{2,1,0:T(8,128)} %copy-done, f32[384,256]{1,0:T(8,128)} %get-tuple-element.24.pa, f32[384,256]{1,0:T(8,128)} %get-tuple-element.25.pb, bf16[1536,512]{1,0:T(8,128)(2,1)} %get-tuple-element.26.ta, bf16[1536,512]{1,0:T(8,128)(2,1)} %get-tuple-element.27.tb), custom_call_target="tpu_custom_call" | custom-call | flops 603979776 | bytes 6291456 | tf_op jit(solution)/shard_map/correlate/pallas_call | solution.py:189
  34.9 2.3 %convert.5 = f16[4,384,512]{2,1,0:T(8,128)(2,1)S(1)} convert(f32[4,384,512]{2,1,0:T(8,128)} %correlate.1) | non-fusion elementwise | flops 786432 | bytes 4718592 | tf_op jit(solution)/shard_map/convert.2
  38.3 5.2 %embed.1 = bf16[8,48,768]{2,1,0:T(8,128)(2,1)} custom-call(s32[2]{0:T(128)} %pad_add_fusion.place, f32[32,8,256]{2,1,0:T(8,128)} %copy-done, bf16[384,1536]{1,0:T(8,128)(2,1)} %va.4, bf16[384,1536]{1,0:T(8,128)(2,1)} %vb.4, bf16[1536,256]{1,0:T(8,128)(2,1)} %w0.1, bf16[1536,256]{1,0:T(8,128)(2,1)} %copy-done.4, bf16[1536,256]{1,0:T(8,128)(2,1)} %copy-done.3, ...), custom_call_target="tpu_custom_call" | custom-call | flops 1207959552 | bytes 7340032 | tf_op jit(solution)/shard_map/embed/pallas_call | solution.py:206
  43.6 8.2 %all-to-all-start.1 = ((bf16[8,48,768]{2,1,0:T(8,128)(2,1)}), bf16[8,48,768]{2,1,0:T(8,128)(2,1)S(1)}, u32[]{:S(2)}, u32[]{:S(2)}) async-start(bf16[8,48,768]{2,1,0:T(8,128)(2,1)} %embed.1), calls=%async_computation.1 | async-start | bytes 1179648 | tf_op jit(solution)/shard_map/all_to_all | solution.py:29
  52.3 1.1 collective-permute-start.7
  53.3 2.3 %collective-permute-start.8 = (f16[384,512]{1,0:T(8,128)(2,1)S(1)}, f16[384,512]{1,0:T(8,128)(2,1)S(1)}, u32[]{:S(2)}, u32[]{:S(2)}) collective-permute-start(f16[384,512]{1,0:T(8,128)(2,1)S(1)} %get-tuple-element.33), channel_id=1, source_target_pairs={{0,96},{32,64},{64,32},{96,0},{1,97},{33,65},{65,33},{97,1},{2,98}... | collective-permute-start | bytes 1179656 | tf_op jit(solution)/shard_map/ppermute | solution.py:200
  55.6 15.6 %all-to-all-done.1.parts = bf16[8,48,768]{2,1,0:T(8,128)(2,1)S(1)} async-done(((bf16[8,48,768]{2,1,0:T(8,128)(2,1)}), bf16[8,48,768]{2,1,0:T(8,128)(2,1)S(1)}, u32[]{:S(2)}, u32[]{:S(2)}) %all-to-all-start.1) | async-done | bytes 589856 | tf_op jit(solution)/shard_map/all_to_all | solution.py:29
  72.0 2.0 %add_copies.1 = bf16[8,48,768]{2,1,0:T(8,128)(2,1)} custom-call(bf16[8,48,768]{2,1,0:T(8,128)(2,1)} %copy-done.1), custom_call_target="tpu_custom_call" | custom-call | flops 10485760 | bytes 1048576 | tf_op jit(solution)/shard_map/add_copies/pallas_call | solution.py:225
  74.0 3.5 %all-to-all-start.2 = ((bf16[8,48,768]{2,1,0:T(8,128)(2,1)}), bf16[8,48,768]{2,1,0:T(8,128)(2,1)S(1)}, u32[]{:S(2)}, u32[]{:S(2)}) async-start(bf16[8,48,768]{2,1,0:T(8,128)(2,1)} %add_copies.1), calls=%async_computation.2 | async-start | bytes 1179648 | tf_op jit(solution)/shard_map/all_to_all | solution.py:29
  77.5 1.4 %fusion.3 = f16[384,512]{1,0:T(8,128)(2,1)S(1)} fusion(f32[4,384,512]{2,1,0:T(8,128)} %correlate.1, f16[384,512]{1,0:T(8,128)(2,1)S(1)} %collective-permute-done.8, f16[384,512]{1,0:T(8,128)(2,1)S(1)} %collective-permute-done.7, f16[384,512]{1,0:T(8,128)(2,1)S(1)} %collective-permute-done.6), kind=kLoop, calls=%fused_computation.4 | loop fusion | flops 1376256 | bytes 2359296 | tf_op jit(solution)/shard_map/convert_element_type | solution.py:221
  79.5 17.3 %all-to-all-done.2.y0 = bf16[8,48,768]{2,1,0:T(8,128)(2,1)S(1)} async-done(((bf16[8,48,768]{2,1,0:T(8,128)(2,1)}), bf16[8,48,768]{2,1,0:T(8,128)(2,1)S(1)}, u32[]{:S(2)}, u32[]{:S(2)}) %all-to-all-start.2) | async-done | bytes 589856 | tf_op jit(solution)/shard_map/all_to_all | solution.py:29
  96.8 1.1 fusion.4
  99.4 2.3 %collective-permute-start.12 = (f16[384,512]{1,0:T(8,128)(2,1)S(1)}, f16[384,512]{1,0:T(8,128)(2,1)S(1)}, u32[]{:S(2)}, u32[]{:S(2)}) collective-permute-start(f16[384,512]{1,0:T(8,128)(2,1)S(1)} %get-tuple-element.35), channel_id=1, source_target_pairs={{0,96},{32,64},{64,32},{96,0},{1,97},{33,65},{65,33},{97,1},{2,98}... | collective-permute-start | bytes 1179656 | tf_op jit(solution)/shard_map/ppermute | solution.py:200
  101.8 6.1 %collective-permute-done.10 = f16[384,512]{1,0:T(8,128)(2,1)S(1)} collective-permute-done((f16[384,512]{1,0:T(8,128)(2,1)S(1)}, f16[384,512]{1,0:T(8,128)(2,1)S(1)}, u32[]{:S(2)}, u32[]{:S(2)}) %collective-permute-start.10) | collective-permute-done | bytes 393248 | tf_op jit(solution)/shard_map/ppermute | solution.py:200
  108.9 7.6 %collective-permute-done.11 = f16[384,512]{1,0:T(8,128)(2,1)S(1)} collective-permute-done((f16[384,512]{1,0:T(8,128)(2,1)S(1)}, f16[384,512]{1,0:T(8,128)(2,1)S(1)}, u32[]{:S(2)}, u32[]{:S(2)}) %collective-permute-start.11) | collective-permute-done | bytes 393248 | tf_op jit(solution)/shard_map/ppermute | solution.py:200
  119.5 2.2 %collective-permute-start.3 = (bf16[8,48,768]{2,1,0:T(8,128)(2,1)S(1)}, bf16[8,48,768]{2,1,0:T(8,128)(2,1)S(1)}, u32[]{:S(2)}, u32[]{:S(2)}) collective-permute-start(bf16[8,48,768]{2,1,0:T(8,128)(2,1)S(1)} %all-to-all-done.2.y0), channel_id=1, source_target_pairs={{0,1},{1,0},{2,3},{3,2},{4,5},{5,4},{6,7},{7,6},{8,9},{9,8},{10,11... | collective-permute-start | bytes 1769480 | tf_op jit(solution)/shard_map/ppermute | solution.py:244
  121.7 4.2 %split.1.u = bf16[3072,512]{1,0:T(8,128)(2,1)} custom-call(s32[2]{0:T(128)} %pad_add_fusion.place, f32[384,512]{1,0:T(8,128)} %get-tuple-element.34.u0, f32[384,512]{1,0:T(8,128)} %convert_element_type.56.u1, f32[384,512]{1,0:T(8,128)} %convert_element_type.57.u2, f32[384,512]{1,0:T(8,128)} %convert_element_type.58.u3), custom_call_target="tpu_custom_call" | custom-call | flops 99999997952 | bytes 100000000 | tf_op jit(solution)/shard_map/split/pallas_call | solution.py:232
  127.6 5.3 %combine.1 = (f32[384,256]{1,0:T(8,128)}, f32[384,256]{1,0:T(8,128)}) custom-call(s32[2]{0:T(128)} %pad_add_fusion.place, f32[32,8,256]{2,1,0:T(8,128)} %copy-done, f32[384,256]{1,0:T(8,128)} %get-tuple-element.24.pa, f32[384,256]{1,0:T(8,128)} %get-tuple-element.25.pb, bf16[8,48,768]{2,1,0:T(8,128)(2,1)} %copy-done.2, bf16[8,48,768]{2,1,0:T(8,128)(2,1)} %copy-done.7, ...), custom_call_target="tpu_custom_call" | custom-call | flops 1207959552 | bytes 8388608 | tf_op jit(solution)/shard_map/combine/pallas_call | solution.py:247
  (41 shorter events, 12.0 us)
Async XLA Ops:
  0.6 27.6 %collective-permute-start = (bf16[1536,256]{1,0:T(8,128)(2,1)}, bf16[1536,256]{1,0:T(8,128)(2,1)S(1)}, u32[]{:S(2)}, u32[]{:S(2)}) collective-permute-start(bf16[1536,256]{1,0:T(8,128)(2,1)} %w0.1), channel_id=1, source_target_pairs={{0,2},{2,0},{1,3},{3,1},{4,6},{6,4},{5,7},{7,5},{8,10},{10,8},{9,1... | collective-permute-start | bytes 2359304 | tf_op jit(solution)/shard_map/ppermute | solution.py:170
  2.8 25.5 %collective-permute-start.1 = (bf16[1536,256]{1,0:T(8,128)(2,1)}, bf16[1536,256]{1,0:T(8,128)(2,1)S(1)}, u32[]{:S(2)}, u32[]{:S(2)}) collective-permute-start(bf16[1536,256]{1,0:T(8,128)(2,1)} %w0.1), channel_id=1, source_target_pairs={{0,1},{1,0},{2,3},{3,2},{4,5},{5,4},{6,7},{7,6},{8,9},{9,8},{10,11... | collective-permute-start | bytes 2359304 | tf_op jit(solution)/shard_map/ppermute | solution.py:171
  7.6 20.6 %all-to-all-start = ((f32[32,8,256]{2,1,0:T(8,128)}), f32[32,8,256]{2,1,0:T(8,128)S(1)}, u32[]{:S(2)}, u32[]{:S(2)}) async-start(f32[32,8,256]{2,1,0:T(8,128)} %get-tuple-element.18), calls=%async_computation | async-start | bytes 524288 | tf_op jit(solution)/shard_map/all_to_all | solution.py:29
  28.2 1.6 %copy-start = (f32[32,8,256]{2,1,0:T(8,128)}, f32[32,8,256]{2,1,0:T(8,128)S(1)}, u32[]{:S(2)}) copy-start(f32[32,8,256]{2,1,0:T(8,128)S(1)} %all-to-all-done.sums) | copy-start | bytes 786436
  28.3 6.6 %copy-start.3 = (bf16[1536,256]{1,0:T(8,128)(2,1)}, bf16[1536,256]{1,0:T(8,128)(2,1)S(1)}, u32[]{:S(2)}) copy-start(bf16[1536,256]{1,0:T(8,128)(2,1)S(1)} %collective-permute-done.w2) | copy-start | bytes 2359300
  28.3 6.6 %copy-start.4 = (bf16[1536,256]{1,0:T(8,128)(2,1)}, bf16[1536,256]{1,0:T(8,128)(2,1)S(1)}, u32[]{:S(2)}) copy-start(bf16[1536,256]{1,0:T(8,128)(2,1)S(1)} %collective-permute-done.1.w1) | copy-start | bytes 2359300
  28.3 9.2 %collective-permute-start.2 = (bf16[1536,256]{1,0:T(8,128)(2,1)S(1)}, bf16[1536,256]{1,0:T(8,128)(2,1)S(1)}, u32[]{:S(2)}, u32[]{:S(2)}) collective-permute-start(bf16[1536,256]{1,0:T(8,128)(2,1)S(1)} %collective-permute-done.w2), channel_id=1, source_target_pairs={{0,1},{1,0},{2,3},{3,2},{4,5},{5,4},{6,7},{7,6},{8,9},{9,8},{10,11... | collective-permute-start | bytes 2359304 | tf_op jit(solution)/shard_map/ppermute | solution.py:187
  37.4 0.9 copy-start.5
  43.6 27.6 %all-to-all-start.1 = ((bf16[8,48,768]{2,1,0:T(8,128)(2,1)}), bf16[8,48,768]{2,1,0:T(8,128)(2,1)S(1)}, u32[]{:S(2)}, u32[]{:S(2)}) async-start(bf16[8,48,768]{2,1,0:T(8,128)(2,1)} %embed.1), calls=%async_computation.1 | async-start | bytes 1179648 | tf_op jit(solution)/shard_map/all_to_all | solution.py:29
  51.8 25.7 %collective-permute-start.6 = (f16[384,512]{1,0:T(8,128)(2,1)S(1)}, f16[384,512]{1,0:T(8,128)(2,1)S(1)}, u32[]{:S(2)}, u32[]{:S(2)}) collective-permute-start(f16[384,512]{1,0:T(8,128)(2,1)S(1)} %get-tuple-element.31), channel_id=1, source_target_pairs={{0,32},{32,0},{64,96},{96,64},{1,33},{33,1},{65,97},{97,65},{2,34}... | collective-permute-start | bytes 1179656 | tf_op jit(solution)/shard_map/ppermute | solution.py:200
  52.3 25.3 %collective-permute-start.7 = (f16[384,512]{1,0:T(8,128)(2,1)S(1)}, f16[384,512]{1,0:T(8,128)(2,1)S(1)}, u32[]{:S(2)}, u32[]{:S(2)}) collective-permute-start(f16[384,512]{1,0:T(8,128)(2,1)S(1)} %get-tuple-element.32), channel_id=1, source_target_pairs={{0,64},{32,96},{64,0},{96,32},{1,65},{33,97},{65,1},{97,33},{2,66}... | collective-permute-start | bytes 1179656 | tf_op jit(solution)/shard_map/ppermute | solution.py:200
  53.3 24.2 %collective-permute-start.8 = (f16[384,512]{1,0:T(8,128)(2,1)S(1)}, f16[384,512]{1,0:T(8,128)(2,1)S(1)}, u32[]{:S(2)}, u32[]{:S(2)}) collective-permute-start(f16[384,512]{1,0:T(8,128)(2,1)S(1)} %get-tuple-element.33), channel_id=1, source_target_pairs={{0,96},{32,64},{64,32},{96,0},{1,97},{33,65},{65,33},{97,1},{2,98}... | collective-permute-start | bytes 1179656 | tf_op jit(solution)/shard_map/ppermute | solution.py:200
  71.2 0.8 copy-start.1
  74.0 22.9 %all-to-all-start.2 = ((bf16[8,48,768]{2,1,0:T(8,128)(2,1)}), bf16[8,48,768]{2,1,0:T(8,128)(2,1)S(1)}, u32[]{:S(2)}, u32[]{:S(2)}) async-start(bf16[8,48,768]{2,1,0:T(8,128)(2,1)} %add_copies.1), calls=%async_computation.2 | async-start | bytes 1179648 | tf_op jit(solution)/shard_map/all_to_all | solution.py:29
  78.9 17.9 %collective-permute-start.9 = (f16[384,512]{1,0:T(8,128)(2,1)S(1)}, f16[384,512]{1,0:T(8,128)(2,1)S(1)}, u32[]{:S(2)}, u32[]{:S(2)}) collective-permute-start(f16[384,512]{1,0:T(8,128)(2,1)S(1)} %fusion.3), channel_id=1, source_target_pairs={{0,128},{128,0},{1,129},{129,1},{2,130},{130,2},{3,131},{131,3},{4... | collective-permute-start | bytes 1179656 | tf_op jit(solution)/shard_map/ppermute | solution.py:222
  96.8 22.6 %copy-start.2 = (bf16[8,48,768]{2,1,0:T(8,128)(2,1)}, bf16[8,48,768]{2,1,0:T(8,128)(2,1)S(1)}, u32[]{:S(2)}) copy-start(bf16[8,48,768]{2,1,0:T(8,128)(2,1)S(1)} %all-to-all-done.2.y0) | copy-start | bytes 1769476
  96.8 24.8 %collective-permute-start.4 = (bf16[8,48,768]{2,1,0:T(8,128)(2,1)S(1)}, bf16[8,48,768]{2,1,0:T(8,128)(2,1)S(1)}, u32[]{:S(2)}, u32[]{:S(2)}) collective-permute-start(bf16[8,48,768]{2,1,0:T(8,128)(2,1)S(1)} %all-to-all-done.2.y0), channel_id=1, source_target_pairs={{0,2},{2,0},{1,3},{3,1},{4,6},{6,4},{5,7},{7,5},{8,10},{10,8},{9,1... | collective-permute-start | bytes 1769480 | tf_op jit(solution)/shard_map/ppermute | solution.py:243
  97.9 10.0 %collective-permute-start.10 = (f16[384,512]{1,0:T(8,128)(2,1)S(1)}, f16[384,512]{1,0:T(8,128)(2,1)S(1)}, u32[]{:S(2)}, u32[]{:S(2)}) collective-permute-start(f16[384,512]{1,0:T(8,128)(2,1)S(1)} %get-tuple-element.35), channel_id=1, source_target_pairs={{0,32},{32,0},{64,96},{96,64},{1,33},{33,1},{65,97},{97,65},{2,34}... | collective-permute-start | bytes 1179656 | tf_op jit(solution)/shard_map/ppermute | solution.py:200
  98.4 18.1 %collective-permute-start.11 = (f16[384,512]{1,0:T(8,128)(2,1)S(1)}, f16[384,512]{1,0:T(8,128)(2,1)S(1)}, u32[]{:S(2)}, u32[]{:S(2)}) collective-permute-start(f16[384,512]{1,0:T(8,128)(2,1)S(1)} %get-tuple-element.35), channel_id=1, source_target_pairs={{0,64},{32,96},{64,0},{96,32},{1,65},{33,97},{65,1},{97,33},{2,66}... | collective-permute-start | bytes 1179656 | tf_op jit(solution)/shard_map/ppermute | solution.py:200
  99.4 19.0 %collective-permute-start.12 = (f16[384,512]{1,0:T(8,128)(2,1)S(1)}, f16[384,512]{1,0:T(8,128)(2,1)S(1)}, u32[]{:S(2)}, u32[]{:S(2)}) collective-permute-start(f16[384,512]{1,0:T(8,128)(2,1)S(1)} %get-tuple-element.35), channel_id=1, source_target_pairs={{0,96},{32,64},{64,32},{96,0},{1,97},{33,65},{65,33},{97,1},{2,98}... | collective-permute-start | bytes 1179656 | tf_op jit(solution)/shard_map/ppermute | solution.py:200
  119.5 6.5 %collective-permute-start.3 = (bf16[8,48,768]{2,1,0:T(8,128)(2,1)S(1)}, bf16[8,48,768]{2,1,0:T(8,128)(2,1)S(1)}, u32[]{:S(2)}, u32[]{:S(2)}) collective-permute-start(bf16[8,48,768]{2,1,0:T(8,128)(2,1)S(1)} %all-to-all-done.2.y0), channel_id=1, source_target_pairs={{0,1},{1,0},{2,3},{3,2},{4,5},{5,4},{6,7},{7,6},{8,9},{9,8},{10,11... | collective-permute-start | bytes 1769480 | tf_op jit(solution)/shard_map/ppermute | solution.py:244
  121.6 4.3 %copy-start.6 = (bf16[8,48,768]{2,1,0:T(8,128)(2,1)}, bf16[8,48,768]{2,1,0:T(8,128)(2,1)S(1)}, u32[]{:S(2)}) copy-start(bf16[8,48,768]{2,1,0:T(8,128)(2,1)S(1)} %collective-permute-done.4.y2) | copy-start | bytes 1769476
  121.6 4.3 %collective-permute-start.5 = (bf16[8,48,768]{2,1,0:T(8,128)(2,1)S(1)}, bf16[8,48,768]{2,1,0:T(8,128)(2,1)S(1)}, u32[]{:S(2)}, u32[]{:S(2)}) collective-permute-start(bf16[8,48,768]{2,1,0:T(8,128)(2,1)S(1)} %collective-permute-done.4.y2), channel_id=1, source_target_pairs={{0,1},{1,0},{2,3},{3,2},{4,5},{5,4},{6,7},{7,6},{8,9},{9,8},{10,11... | collective-permute-start | bytes 1769480 | tf_op jit(solution)/shard_map/ppermute | solution.py:245
  126.7 0.8 copy-start.8
  (1 other events, 0.8 us)

commit v2 on v1

v2 whole, which is shorter than its diff:
```python
import jax
import jax.numpy as jnp
import numpy as np
from jax import lax
from jax.experimental import pallas as pl
from jax.experimental.pallas import tpu as pltpu
from jax.sharding import Mesh, PartitionSpec as P

DP = ("xh", "y")
FEAT = ("z", "xl", "c")
PARTS = {"xh": 2, "y": 4, "z": 8, "xl": 2, "c": 2}
SWAP = [(0, 1), (1, 0)]
U_SCALE = 1024.0
EPS = 1e-05
f32, bf16, f16 = jnp.float32, jnp.bfloat16, jnp.float16

ROWS = 384
TOTAL = 3072
DEPTH = 1536
BLOCK = 256
QUARTER = ROWS // 4
PIECE = (48, 768)
SHARE = DEPTH // 4
EARLY = 1024
VMEM = pl.BlockSpec(memory_space=pltpu.VMEM)
SMEM = pl.BlockSpec(memory_space=pltpu.SMEM)
ANY = pl.BlockSpec(memory_space=pl.ANY)


def exchange(blocks, axes):
    return lax.all_to_all(blocks, axes, split_axis=0, concat_axis=0, tiled=True)


def dot(a, b, ca, cb):
    return lax.dot_general(a, b, (((ca,), (cb,)), ((), ())), preferred_element_type=f32)


def call(body, out, ins, flops, nbytes, scratch=(), name=None, out_specs=None, vmem=60):
    return pl.pallas_call(
        body,
        out_shape=out,
        in_specs=ins,
        out_specs=out_specs or jax.tree.map(lambda _: VMEM, out),
        scratch_shapes=scratch,
        compiler_params=pltpu.CompilerParams(vmem_limit_bytes=vmem * 2**20),
        cost_estimate=pl.CostEstimate(flops=flops, bytes_accessed=nbytes, transcendentals=0),
        name=name,
    )


def project(va, vb, w, pa, pb, sums, xa, xb, xw, sem):
    third = DEPTH // 3
    copies = []
    for k in range(3):
        at = pl.ds(k * third, third)
        copies.append(
            [
                pltpu.make_async_copy(va.at[:, at], xa.at[k], sem.at[3 * k]),
                pltpu.make_async_copy(vb.at[:, at], xb.at[k], sem.at[3 * k + 1]),
                pltpu.make_async_copy(w.at[at, :], xw.at[k], sem.at[3 * k + 2]),
            ]
        )
    for c in copies:
        for t in c:
            t.start()
    a = b = 0.0
    for k in range(3):
        for t in copies[k]:
            t.wait()
        a = a + dot(xa[k], xw[k], 1, 0)
        b = b + dot(xb[k], xw[k], 1, 0)
    pa[...] = a
    pb[...] = b
    col = [jnp.sum(t, axis=0, keepdims=True) for t in (a, a * a, b, b * b, a * b)]
    own = jnp.concatenate(col + [jnp.zeros((3, BLOCK), f32)], axis=0)
    sums[...] = jnp.broadcast_to(own[None], sums.shape)


def moments(sums, q):
    t = sums[q]
    for d in range(1, 8):
        t = t + sums[4 * d + q]
    t = t * (1.0 / TOTAL)
    ma, mb = t[0:1], t[2:3]
    ra = lax.rsqrt(t[1:2] - ma * ma + EPS)
    rb = lax.rsqrt(t[3:4] - mb * mb + EPS)
    return ma, ra, mb, rb, (t[4:5] - ma * mb) * ra * rb


def embed(place, sums, v, w0, w1, w2, w2b, w3, w3b, y, na, nb):
    q = place[0]
    half = EARLY
    ws = ((w0,), (w1,), (w2, w2b), (w3, w3b))
    for j, wj in enumerate(ws):
        ma, ra, mb, rb, _ = moments(sums, q ^ j)
        if len(wj) == 1:
            p = dot(v[...], wj[0][...], 1, 0)
        else:
            p = dot(v[:, :half], wj[0][...], 1, 0) + dot(v[:, half:], wj[1][...], 1, 0)
        cols = slice(j * BLOCK, (j + 1) * BLOCK)
        na[:, cols] = ((p[:QUARTER] - ma) * (ra * ra)).astype(bf16)
        nb[:, cols] = ((p[QUARTER:] - mb) * (rb * rb)).astype(bf16)
    n = jnp.concatenate([na[...], nb[...]], axis=0)
    for k in range(6):
        acc = 0.0
        for j, wj in enumerate(ws):
            late = len(wj) == 2 and k * 256 >= EARLY
            part = wj[1] if late else wj[0]
            first = k * 256 - (EARLY if late else 0)
            nj = n[:, j * BLOCK : (j + 1) * BLOCK]
            acc = acc + dot(nj, part[first : first + 256, :], 1, 1)
        acc = acc.astype(bf16)
        for i in range(4):
            y[2 * i + k // 3, :, (k % 3) * 256 : (k % 3 + 1) * 256] = acc[48 * i : 48 * i + 48]


def add_copies(parts, ready, out, x, t, sem, out_sem):
    copy = pltpu.make_async_copy(parts, x, sem)
    copy.start()
    copy.wait()
    total = x[0].astype(f32)
    for d in range(1, 8):
        total = total + x[d].astype(f32)
    t[...] = total.astype(bf16)
    done = [pltpu.make_async_copy(t, out.at[d], out_sem.at[d]) for d in range(8)]
    for c in done:
        c.start()
    for c in done:
        c.wait()


def turn(place, va, vb, ta, tb, quarter):
    at = pl.ds(pl.multiple_of(place[0] * QUARTER, 32), QUARTER)
    quarter[:QUARTER] = va[at, :]
    quarter[QUARTER:] = vb[at, :]
    for view, out in ((va, ta), (vb, tb)):
        v = view[...]
        centre = jnp.sum(v.astype(f32), axis=0, keepdims=True) * (1.0 / ROWS)
        centre = jnp.concatenate([centre, jnp.zeros((15, DEPTH), f32)], axis=0).astype(bf16)
        out[...] = jnp.concatenate([v, centre, jnp.zeros((112, DEPTH), bf16)], axis=0).T


def correlate(place, sums, pa, pb, ta, tb, u, xa, xb, un, sem, out_sem):
    q, yy = place[0], place[1]
    copies = []
    for b in range(4):
        at = pl.ds(b * SHARE, SHARE)
        copies.append(
            (
                pltpu.make_async_copy(ta.at[at, :], xa.at[b], sem.at[2 * b]),
                pltpu.make_async_copy(tb.at[at, :], xb.at[b], sem.at[2 * b + 1]),
            )
        )
    for c in copies:
        for t in c:
            t.start()
    ma, ra, mb, rb, _ = moments(sums, q)
    ns = []
    for p, m, s in ((pa, ma, ra), (pb, mb, rb)):
        n = (p[...] - m) * s
        rounded = n.astype(bf16)
        excess = jnp.sum(n - rounded.astype(f32), axis=0, keepdims=True)
        excess = jnp.concatenate([excess, jnp.zeros((15, BLOCK), f32)], axis=0).astype(bf16)
        ns.append(jnp.concatenate([rounded, excess, jnp.zeros((112, BLOCK), bf16)], axis=0))
    scale = U_SCALE / TOTAL
    done = []
    for b in range(4):
        for t in copies[b]:
            t.wait()
        un[b, :, :BLOCK] = dot(xb[b], ns[0], 1, 0) * scale
        un[b, :, BLOCK:] = dot(xa[b], ns[1], 1, 0) * scale
        out = pltpu.make_async_copy(un.at[b], u.at[b ^ yy], out_sem.at[b])
        out.start()
        done.append(out)
    for t in done:
        t.wait()


def combine(place, sums, pa, pb, *refs):
    ys, us, (out_a, out_b, ya, yb) = refs[:8], refs[8:16], refs[16:]
    q, yy = place[0], place[1]
    for j in range(4):
        for i in range(4):
            at = pl.multiple_of((q ^ j) * QUARTER + (i & 1) * 48, 16)
            for h in range(2):
                to = ya if i < 2 else yb
                to[pl.ds(at, 48), h * 768 : (h + 1) * 768] = ys[2 * j + i // 2][2 * (i & 1) + h]
    ma, ra, mb, rb, corr = moments(sums, q)
    for first, y, p, m, r, out in (
        (0, yb, pb, mb, rb, out_a),
        (BLOCK, ya, pa, ma, ra, out_b),
    ):
        acc = (p[...] - m) * (r * (corr - 2.0))
        cols = slice(first, first + BLOCK)
        for s in range(4):
            at = pl.ds(pl.multiple_of((yy ^ s) * SHARE, 128), SHARE)
            part = y[:, at]
            acc = acc + (dot(part, us[2 * s][:, cols], 1, 0) + dot(part, us[2 * s + 1][:, cols], 1, 0))
        out[...] = acc


def mark(arrived, out):
    out[...] = jnp.zeros(out.shape, f32)


def arrival(t, us):
    return pl.pallas_call(
        mark,
        out_shape=jax.ShapeDtypeStruct((8, 128), f32),
        in_specs=[ANY],
        out_specs=VMEM,
        cost_estimate=pl.CostEstimate(flops=us * 10**9, bytes_accessed=0, transcendentals=0),
        name="mark",
    )(t)


def hand_on(whole, ready, out):
    pass


def local(va, vb, w):
    q = lax.axis_index("xl") * 2 + lax.axis_index("c")
    place = jnp.stack([q, lax.axis_index("y")]).astype(jnp.int32)
    shape = jax.ShapeDtypeStruct
    sems = pltpu.SemaphoreType.DMA
    half = EARLY

    def swap(t, axis):
        return lax.ppermute(t, axis, SWAP)

    def along_y(t, s):
        return lax.ppermute(t, "y", [(i, i ^ s) for i in range(4)])

    w_c = swap(w, "c")
    w_x = swap(w[:half], "xl")

    pa, pb, own = call(
        project,
        (shape((ROWS, BLOCK), f32), shape((ROWS, BLOCK), f32), shape((32, 8, BLOCK), f32)),
        [ANY] * 3,
        4 * ROWS * DEPTH * BLOCK,
        4 * 2**20,
        [
            pltpu.VMEM((3, ROWS, DEPTH // 3), bf16),
            pltpu.VMEM((3, ROWS, DEPTH // 3), bf16),
            pltpu.VMEM((3, DEPTH // 3, BLOCK), bf16),
            sems((9,)),
        ],
        name="project",
    )(va, vb, w)
    sums = exchange(own, ("xh", "y", "xl", "c"))
    va, vb, pa = lax.optimization_barrier((va, vb, pa))
    ta, tb, v_quarter = call(
        turn,
        (shape((DEPTH, 512), bf16),) * 2 + (shape((2 * QUARTER, DEPTH), bf16),),
        [SMEM] + [VMEM] * 2,
        10 * 2**20,
        6 * 2**20,
        name="turn",
    )(place, va, vb)
    sums, ta, tb, v_quarter, w_late, w_x = lax.optimization_barrier(
        (sums, ta, tb, v_quarter, w[half:], w_x)
    )
    w_xb = swap(w_late, "xl")
    w_xcb = swap(w_xb, "c")

    u_parts = call(
        correlate,
        shape((4, SHARE, 2 * BLOCK), f32),
        [SMEM] + [VMEM] * 3 + [ANY] * 2,
        4 * ROWS * DEPTH * BLOCK,
        6 * 2**20,
        [
            pltpu.VMEM((4, SHARE, 512), bf16),
            pltpu.VMEM((4, SHARE, 512), bf16),
            pltpu.VMEM((4, SHARE, 2 * BLOCK), f32),
            sems((8,)),
            sems((4,)),
        ],
        out_specs=ANY,
        name="correlate",
    )(place, sums, pa, pb, ta, tb)
    u_parts, w_x = lax.optimization_barrier((u_parts, w_x))
    w_xc = swap(w_x, "c")
    u = u_parts[0]
    for s in (1, 2, 3):
        u = u + along_y(u_parts[s].astype(f16), s).astype(f32)
    u_near = arrival(u[:8, :128], 7)
    u = u.astype(f16)
    u = u.astype(f32) + swap(u, "xh").astype(f32)
    u_far = arrival(u[:8, :128], 6)
    u = lax.optimization_barrier(u.astype(f16))
    split = []
    for t in [u] + [along_y(u, s) for s in (1, 2, 3)]:
        t = t.astype(f32) * (1.0 / U_SCALE)
        high = lax.reduce_precision(t, 8, 7)
        split += [high.astype(bf16), (t - high).astype(bf16)]

    y_part = call(
        embed,
        shape((8,) + PIECE, bf16),
        [SMEM] + [VMEM] * 8,
        16 * ROWS * DEPTH * BLOCK // 2,
        7 * 2**20,
        [pltpu.VMEM((QUARTER, 4 * BLOCK), bf16)] * 2,
        name="embed",
        vmem=20,
    )(place, sums, v_quarter, w, w_c, w_x, w_xb, w_xc, w_xcb)
    y_copies = call(
        add_copies,
        shape((8,) + PIECE, bf16),
        [ANY] * 2,
        10 * 2**20,
        2**20,
        [pltpu.VMEM((8,) + PIECE, bf16), pltpu.VMEM(PIECE, bf16), sems, sems((8,))],
        out_specs=ANY,
        name="add_copies",
        vmem=63,
    )(exchange(y_part, "z"), u_near)
    y0 = pl.pallas_call(
        hand_on,
        out_shape=shape((8,) + PIECE, bf16),
        in_specs=[ANY, ANY],
        out_specs=ANY,
        input_output_aliases={0: 0},
        compiler_params=pltpu.CompilerParams(vmem_limit_bytes=63 * 2**20),
        name="hand_on",
    )(exchange(y_copies, "z"), u_far)
    y0 = [y0[:4], y0[4:]]
    y2 = [swap(t, "xl") for t in y0]
    y1 = [swap(t, "c") for t in y0]
    y3 = [swap(t, "c") for t in y2]

    return call(
        combine,
        (shape((ROWS, BLOCK), f32),) * 2,
        [SMEM] + [VMEM] * 19,
        8 * ROWS * DEPTH * BLOCK,
        8 * 2**20,
        [pltpu.VMEM((ROWS, DEPTH), bf16)] * 2,
        name="combine",
        vmem=20,
    )(place, sums, pa, pb, *y0, *y1, *y2, *y3, *split)


def solution(mesh):
    fine = Mesh(np.asarray(mesh.devices).reshape(tuple(PARTS.values())), tuple(PARTS))
    return jax.shard_map(
        local,
        mesh=fine,
        in_specs=(P(DP, None), P(DP, None), P(None, FEAT)),
        out_specs=(P(DP, FEAT), P(DP, FEAT)),
        check_vma=False,
    )
```

time: 133 us -> 115 us (0.86)
  waiting for transfers between devices: 57.8 us -> 27.9 us
  starting transfers between devices: 33.2 us -> 44.8 us
  Pallas kernels: 29.1 us -> 21.9 us
  other arithmetic: 8.34 us -> 11.9 us
  local copies, waits for them, and re-layouts: 3.61 us -> 6.59 us
    all_to_all x3, waiting for transfers between devices: 43.1 us -> 21.4 us  [exchange(): return lax.all_to_all(blocks, axes, split_axis=0, concat_axis=0, tiled=True)]
    ppermute x7 -> x12, starting transfers between devices: 7.22 us -> 19.3 us  [swap(): return lax.ppermute(t, axis, SWAP)]
    ppermute x6, waiting for transfers between devices: 14.7 us -> 6.44 us  [along_y(): return lax.ppermute(t, 'y', [(i, i ^ s) for i in range(4)])]
    pallas_call x6 -> x8, Pallas kernels: 25.6 us -> 18.5 us  [the longest x1 4.78 us: local(): call(correlate, shape((4, SHARE, 2 * BLOCK), f32), [SMEM] + [VMEM] * 3 +...]
    slice x0 -> x5, local copies, waits for them, and re-layouts: none -> 3.37 us  [the longest x1 1.09 us: local(): y0 = [y0[:4], y0[4:]]]
    convert_element_type x4 -> x5, other arithmetic: 4.08 us -> 6.59 us  [the longest x4 4.58 us: local(): split += [high.astype(bf16), (t - high).astype(bf16)]]
  transfers between devices with their start and end apart: 16 -> 21, of which waited for: 6 -> 5; matrix products, arithmetic and copies ran while one was open for 6% -> 13% of each run, Pallas kernels for 14% -> 16%
where the time goes in v2:
time: 115 us; the launch traced here: 114 us
  starting transfers between devices  44.8 us (39%)
  waiting for transfers between devices  27.9 us (24%)
  Pallas kernels  21.9 us (19%)
  other arithmetic  11.9 us (10%)
  local copies, waits for them, and re-layouts  6.59 us (6%)
    all_to_all x3, waiting for transfers between devices, exchange(): return lax.all_to_all(blocks, axes, split_axis=0, concat_axis=0, tiled=True)  21.4 us
    ppermute x12, starting transfers between devices, swap(): return lax.ppermute(t, axis, SWAP)  19.3 us
    all_to_all x3, starting transfers between devices, exchange(): return lax.all_to_all(blocks, axes, split_axis=0, concat_axis=0, tiled=True)  18.3 us
    ppermute x6, starting transfers between devices, along_y(): return lax.ppermute(t, 'y', [(i, i ^ s) for i in range(4)])  7.11 us
    ppermute x6, waiting for transfers between devices, along_y(): return lax.ppermute(t, 'y', [(i, i ^ s) for i in range(4)])  6.44 us
    pallas_call x1, Pallas kernels, local(): call(correlate, shape((4, SHARE, 2 * BLOCK), f32), [SMEM] + [VMEM] * 3 +...  4.78 us
    convert_element_type x4, other arithmetic, local(): split += [high.astype(bf16), (t - high).astype(bf16)]  4.58 us
    pallas_call x1, Pallas kernels, local(): call(turn, (shape((DEPTH, 512), bf16),) * 2 + (shape((2 * QUARTER, DEPTH)...  3.97 us
  transfers between devices with their start and end apart: 21, of which 5 were waited for; matrix products, arithmetic and copies ran while one was open for 13% of the time, Pallas kernels for 16%

profile of v2, /device:TPU:1, one launch (start us, length us, event | category | flops | bytes accessed | tf_op | source)
XLA Modules:
  0.0 113.9 jit_solution(6401031963404451174)
XLA Ops:
  1.7 2.1 %collective-permute-start = (bf16[1024,256]{1,0:T(8,128)(2,1)S(1)}, bf16[1024,256]{1,0:T(8,128)(2,1)S(1)}, u32[]{:S(2)}, u32[]{:S(2)}) collective-permute-start(bf16[1024,256]{1,0:T(8,128)(2,1)S(1)} %slice.34), channel_id=1, source_target_pairs={{0,2},{2,0},{1,3},{3,1},{4,6},{6,4},{5,7},{7,5},{8,10},{10,8},{9,1... | collective-permute-start | bytes 1572872 | tf_op jit(solution)/shard_map/ppermute | solution.py:229
  5.2 3.4 %project.1 = (f32[384,256]{1,0:T(8,128)}, f32[384,256]{1,0:T(8,128)}, f32[32,8,256]{2,1,0:T(8,128)}) custom-call(bf16[384,1536]{1,0:T(8,128)(2,1)} %va.2, bf16[384,1536]{1,0:T(8,128)(2,1)} %vb.2, bf16[1536,256]{1,0:T(8,128)(2,1)} %w0.1), custom_call_target="tpu_custom_call" | custom-call | flops 603979776 | bytes 4194304 | tf_op jit(solution)/shard_map/project/pallas_call | solution.py:237
  8.5 6.6 %all-to-all-start = ((f32[32,8,256]{2,1,0:T(8,128)}), f32[32,8,256]{2,1,0:T(8,128)S(1)}, u32[]{:S(2)}, u32[]{:S(2)}) async-start(f32[32,8,256]{2,1,0:T(8,128)} %get-tuple-element.19), calls=%async_computation | async-start | bytes 524288 | tf_op jit(solution)/shard_map/all_to_all | solution.py:31
  15.8 4.0 %turn.1 = (bf16[1536,512]{1,0:T(8,128)(2,1)}, bf16[1536,512]{1,0:T(8,128)(2,1)}, bf16[192,1536]{1,0:T(8,128)(2,1)}) custom-call(s32[2]{0:T(128)} %pad_add_fusion.place, bf16[384,1536]{1,0:T(8,128)(2,1)} %va.2, bf16[384,1536]{1,0:T(8,128)(2,1)} %vb.2), custom_call_target="tpu_custom_call" | custom-call | flops 10485760 | bytes 6291456 | tf_op jit(solution)/shard_map/turn/pallas_call | solution.py:253
  19.7 3.9 %all-to-all-done.sums = f32[32,8,256]{2,1,0:T(8,128)S(1)} async-done(((f32[32,8,256]{2,1,0:T(8,128)}), f32[32,8,256]{2,1,0:T(8,128)S(1)}, u32[]{:S(2)}, u32[]{:S(2)}) %all-to-all-start) | async-done | bytes 262176 | tf_op jit(solution)/shard_map/all_to_all | solution.py:31
  24.4 4.8 %correlate.1 = f32[4,384,512]{2,1,0:T(8,128)} custom-call(s32[2]{0:T(128)} %pad_add_fusion.place, f32[32,8,256]{2,1,0:T(8,128)} %copy-done.1, f32[384,256]{1,0:T(8,128)} %get-tuple-element.27.pa, f32[384,256]{1,0:T(8,128)} %get-tuple-element.28.pb, bf16[1536,512]{1,0:T(8,128)(2,1)} %get-tuple-element.30.ta, bf16[1536,512]{1,0:T(8,128)(2,1)} %get-tuple-element.31.tb), custom_call_target="tpu_custom_call" | custom-call | flops 603979776 | bytes 6291456 | tf_op jit(solution)/shard_map/correlate/pallas_call | solution.py:267
  30.3 2.3 %convert.5 = f16[4,384,512]{2,1,0:T(8,128)(2,1)S(1)} convert(f32[4,384,512]{2,1,0:T(8,128)} %correlate.1) | non-fusion elementwise | flops 786432 | bytes 4718592 | tf_op jit(solution)/shard_map/convert.2
  35.6 2.0 %collective-permute-start.7 = (f16[384,512]{1,0:T(8,128)(2,1)}, f16[384,512]{1,0:T(8,128)(2,1)}, u32[]{:S(2)}, u32[]{:S(2)}) collective-permute-start(f16[384,512]{1,0:T(8,128)(2,1)} %get-tuple-element.39), channel_id=1, source_target_pairs={{0,96},{32,64},{64,32},{96,0},{1,97},{33,65},{65,33},{97,1},{2,98}... | collective-permute-start | bytes 1179656 | tf_op jit(solution)/shard_map/ppermute | solution.py:232
  37.7 3.2 %embed.1 = bf16[8,48,768]{2,1,0:T(8,128)(2,1)} custom-call(s32[2]{0:T(128)S(1)} %copy-done.6, f32[32,8,256]{2,1,0:T(8,128)S(1)} %copy-done.2, bf16[192,1536]{1,0:T(8,128)(2,1)S(1)} %copy-done.5, bf16[1536,256]{1,0:T(8,128)(2,1)S(1)} %copy-done, bf16[1536,256]{1,0:T(8,128)(2,1)S(1)} %collective-permute-done.1.w1, ...), custom_call_target="tpu_custom_call" | custom-call | flops 1207959552 | bytes 7340032 | tf_op jit(solution)/shard_map/embed/pallas_call | solution.py:299
  40.9 8.2 %all-to-all-start.1 = ((bf16[8,48,768]{2,1,0:T(8,128)(2,1)}), bf16[8,48,768]{2,1,0:T(8,128)(2,1)S(1)}, u32[]{:S(2)}, u32[]{:S(2)}) async-start(bf16[8,48,768]{2,1,0:T(8,128)(2,1)} %embed.1), calls=%async_computation.1 | async-start | bytes 1179648 | tf_op jit(solution)/shard_map/all_to_all | solution.py:31
  49.1 4.4 %collective-permute-done.6 = f16[384,512]{1,0:T(8,128)(2,1)} collective-permute-done((f16[384,512]{1,0:T(8,128)(2,1)}, f16[384,512]{1,0:T(8,128)(2,1)}, u32[]{:S(2)}, u32[]{:S(2)}) %collective-permute-start.6) | collective-permute-done | bytes 393248 | tf_op jit(solution)/shard_map/ppermute | solution.py:232
  53.5 2.0 %collective-permute-done.7 = f16[384,512]{1,0:T(8,128)(2,1)} collective-permute-done((f16[384,512]{1,0:T(8,128)(2,1)}, f16[384,512]{1,0:T(8,128)(2,1)}, u32[]{:S(2)}, u32[]{:S(2)}) %collective-permute-start.7) | collective-permute-done | bytes 393248 | tf_op jit(solution)/shard_map/ppermute | solution.py:232
  55.5 2.4 %fusion.7 = (f16[384,512]{1,0:T(8,128)(2,1)}, f32[384,512]{1,0:T(8,128)S(1)}) fusion(f16[384,512]{1,0:T(8,128)(2,1)} %collective-permute-done.7, f16[384,512]{1,0:T(8,128)(2,1)} %collective-permute-done.6, f16[384,512]{1,0:T(8,128)(2,1)S(1)} %collective-permute-done.5, f32[4,384,512]{2,1,0:T(8,128)} %correlate.1), kind=kLoop, calls=%fused_computation.25 | loop fusion | flops 1376256 | bytes 3145728 | tf_op jit(solution)/shard_map/convert_element_type | solution.py:289
  60.0 6.9 %all-to-all-done.1.parts = bf16[8,48,768]{2,1,0:T(8,128)(2,1)S(1)} async-done(((bf16[8,48,768]{2,1,0:T(8,128)(2,1)}), bf16[8,48,768]{2,1,0:T(8,128)(2,1)S(1)}, u32[]{:S(2)}, u32[]{:S(2)}) %all-to-all-start.1) | async-done | bytes 589856 | tf_op jit(solution)/shard_map/all_to_all | solution.py:31
  67.7 2.1 %add_copies.1 = bf16[8,48,768]{2,1,0:T(8,128)(2,1)} custom-call(bf16[8,48,768]{2,1,0:T(8,128)(2,1)} %copy-done.8, f32[8,128]{1,0:T(8,128)} %mark.2.ready), custom_call_target="tpu_custom_call" | custom-call | flops 10485760 | bytes 1048576 | tf_op jit(solution)/shard_map/add_copies/pallas_call | solution.py:309
  69.8 3.5 %all-to-all-start.2 = ((bf16[8,48,768]{2,1,0:T(8,128)(2,1)}), bf16[8,48,768]{2,1,0:T(8,128)(2,1)S(1)}, u32[]{:S(2)}, u32[]{:S(2)}) async-start(bf16[8,48,768]{2,1,0:T(8,128)(2,1)} %add_copies.1), calls=%async_computation.2 | async-start | bytes 1179648 | tf_op jit(solution)/shard_map/all_to_all | solution.py:31
  73.4 2.0 %fusion.6 = (f16[384,512]{1,0:T(8,128)(2,1)}, f32[384,512]{1,0:T(8,128)S(1)}) fusion(f16[384,512]{1,0:T(8,128)(2,1)} %collective-permute-done.8, f16[384,512]{1,0:T(8,128)(2,1)} %get-tuple-element.36), kind=kLoop, calls=%fused_computation.24 | loop fusion | flops 786432 | bytes 1966080 | tf_op jit(solution)/shard_map/convert_element_type | solution.py:292
  75.4 1.7 %collective-permute-start.17 = (f16[384,512]{1,0:T(8,128)(2,1)}, f16[384,512]{1,0:T(8,128)(2,1)}, u32[]{:S(2)}, u32[]{:S(2)}) collective-permute-start(f16[384,512]{1,0:T(8,128)(2,1)} %get-tuple-element.41), channel_id=1, source_target_pairs={{0,96},{32,64},{64,32},{96,0},{1,97},{33,65},{65,33},{97,1},{2,98}... | collective-permute-start | bytes 1179656 | tf_op jit(solution)/shard_map/ppermute | solution.py:232
  77.1 1.5 %collective-permute-start.15 = (f16[384,512]{1,0:T(8,128)(2,1)}, f16[384,512]{1,0:T(8,128)(2,1)}, u32[]{:S(2)}, u32[]{:S(2)}) collective-permute-start(f16[384,512]{1,0:T(8,128)(2,1)} %get-tuple-element.41), channel_id=1, source_target_pairs={{0,32},{32,0},{64,96},{96,64},{1,33},{33,1},{65,97},{97,65},{2,34}... | collective-permute-start | bytes 1179656 | tf_op jit(solution)/shard_map/ppermute | solution.py:232
  79.8 10.7 %all-to-all-done.2.whole = bf16[8,48,768]{2,1,0:T(8,128)(2,1)S(1)} async-done(((bf16[8,48,768]{2,1,0:T(8,128)(2,1)}), bf16[8,48,768]{2,1,0:T(8,128)(2,1)S(1)}, u32[]{:S(2)}, u32[]{:S(2)}) %all-to-all-start.2) | async-done | bytes 589856 | tf_op jit(solution)/shard_map/all_to_all | solution.py:31
  96.3 3.3 %collective-permute-start.10 = (bf16[4,48,768]{2,1,0:T(8,128)(2,1)S(1)}, bf16[4,48,768]{2,1,0:T(8,128)(2,1)S(1)}, u32[]{:S(2)}, u32[]{:S(2)}) collective-permute-start(bf16[4,48,768]{2,1,0:T(8,128)(2,1)S(1)} %get-tuple-element.43.refs_1_), channel_id=1, source_target_pairs={{0,1},{1,0},{2,3},{3,2},{4,5},{5,4},{6,7},{7,6},{8,9},{9,8},{10,11... | collective-permute-start | bytes 884744 | tf_op jit(solution)/shard_map/ppermute | solution.py:229
  99.7 5.3 %collective-permute-start.13 = (bf16[4,48,768]{2,1,0:T(8,128)(2,1)S(1)}, bf16[4,48,768]{2,1,0:T(8,128)(2,1)S(1)}, u32[]{:S(2)}, u32[]{:S(2)}) collective-permute-start(bf16[4,48,768]{2,1,0:T(8,128)(2,1)S(1)} %collective-permute-done.11.refs_4_), channel_id=1, source_target_pairs={{0,1},{1,0},{2,3},{3,2},{4,5},{5,4},{6,7},{7,6},{8,9},{9,8},{10,11... | collective-permute-start | bytes 884744 | tf_op jit(solution)/shard_map/ppermute | solution.py:229
  105.1 3.2 %collective-permute-start.14 = (bf16[4,48,768]{2,1,0:T(8,128)(2,1)S(1)}, bf16[4,48,768]{2,1,0:T(8,128)(2,1)S(1)}, u32[]{:S(2)}, u32[]{:S(2)}) collective-permute-start(bf16[4,48,768]{2,1,0:T(8,128)(2,1)S(1)} %collective-permute-done.12.refs_5_), channel_id=1, source_target_pairs={{0,1},{1,0},{2,3},{3,2},{4,5},{5,4},{6,7},{7,6},{8,9},{9,8},{10,11... | collective-permute-start | bytes 884744 | tf_op jit(solution)/shard_map/ppermute | solution.py:229
  110.6 3.3 %combine.1 = (f32[384,256]{1,0:T(8,128)}, f32[384,256]{1,0:T(8,128)}) custom-call(s32[2]{0:T(128)S(1)} %copy-done.6, f32[32,8,256]{2,1,0:T(8,128)S(1)} %copy-done.2, f32[384,256]{1,0:T(8,128)S(1)} %copy-done.3, f32[384,256]{1,0:T(8,128)S(1)} %copy-done.4, bf16[4,48,768]{2,1,0:T(8,128)(2,1)S(1)} %get-tuple-element.44.refs_0_, ...), custom_call_target="tpu_custom_call" | custom-call | flops 1207959552 | bytes 8388608 | tf_op jit(solution)/shard_map/combine/pallas_call | solution.py:334
  (59 shorter events, 20.2 us)
Async XLA Ops:
  1.7 13.4 %copy-start = (bf16[1536,256]{1,0:T(8,128)(2,1)S(1)}, bf16[1536,256]{1,0:T(8,128)(2,1)}, u32[]{:S(2)}) copy-start(bf16[1536,256]{1,0:T(8,128)(2,1)} %w0.1) | copy-start | bytes 2359300
  1.7 22.0 %collective-permute-start = (bf16[1024,256]{1,0:T(8,128)(2,1)S(1)}, bf16[1024,256]{1,0:T(8,128)(2,1)S(1)}, u32[]{:S(2)}, u32[]{:S(2)}) collective-permute-start(bf16[1024,256]{1,0:T(8,128)(2,1)S(1)} %slice.34), channel_id=1, source_target_pairs={{0,2},{2,0},{1,3},{3,1},{4,6},{6,4},{5,7},{7,5},{8,10},{10,8},{9,1... | collective-permute-start | bytes 1572872 | tf_op jit(solution)/shard_map/ppermute | solution.py:229
  3.9 31.8 %collective-permute-start.1 = (bf16[1536,256]{1,0:T(8,128)(2,1)}, bf16[1536,256]{1,0:T(8,128)(2,1)S(1)}, u32[]{:S(2)}, u32[]{:S(2)}) collective-permute-start(bf16[1536,256]{1,0:T(8,128)(2,1)} %w0.1), channel_id=1, source_target_pairs={{0,1},{1,0},{2,3},{3,2},{4,5},{5,4},{6,7},{7,6},{8,9},{9,8},{10,11... | collective-permute-start | bytes 2359304 | tf_op jit(solution)/shard_map/ppermute | solution.py:229
  8.5 15.1 %all-to-all-start = ((f32[32,8,256]{2,1,0:T(8,128)}), f32[32,8,256]{2,1,0:T(8,128)S(1)}, u32[]{:S(2)}, u32[]{:S(2)}) async-start(f32[32,8,256]{2,1,0:T(8,128)} %get-tuple-element.19), calls=%async_computation | async-start | bytes 524288 | tf_op jit(solution)/shard_map/all_to_all | solution.py:31
  23.7 8.9 %collective-permute-start.2 = (bf16[512,256]{1,0:T(8,128)(2,1)S(1)}, bf16[512,256]{1,0:T(8,128)(2,1)S(1)}, u32[]{:S(2)}, u32[]{:S(2)}) collective-permute-start(bf16[512,256]{1,0:T(8,128)(2,1)S(1)} %slice.33), channel_id=1, source_target_pairs={{0,2},{2,0},{1,3},{3,1},{4,6},{6,4},{5,7},{7,5},{8,10},{10,8},{9,1... | collective-permute-start | bytes 786440 | tf_op jit(solution)/shard_map/ppermute | solution.py:229
  29.2 8.5 %collective-permute-start.3 = (bf16[1024,256]{1,0:T(8,128)(2,1)S(1)}, bf16[1024,256]{1,0:T(8,128)(2,1)S(1)}, u32[]{:S(2)}, u32[]{:S(2)}) collective-permute-start(bf16[1024,256]{1,0:T(8,128)(2,1)S(1)} %collective-permute-done.w2), channel_id=1, source_target_pairs={{0,1},{1,0},{2,3},{3,2},{4,5},{5,4},{6,7},{7,6},{8,9},{9,8},{10,11... | collective-permute-start | bytes 1572872 | tf_op jit(solution)/shard_map/ppermute | solution.py:229
  32.6 5.1 %collective-permute-start.4 = (bf16[512,256]{1,0:T(8,128)(2,1)S(1)}, bf16[512,256]{1,0:T(8,128)(2,1)S(1)}, u32[]{:S(2)}, u32[]{:S(2)}) collective-permute-start(bf16[512,256]{1,0:T(8,128)(2,1)S(1)} %collective-permute-done.2.w2b), channel_id=1, source_target_pairs={{0,1},{1,0},{2,3},{3,2},{4,5},{5,4},{6,7},{7,6},{8,9},{9,8},{10,11... | collective-permute-start | bytes 786440 | tf_op jit(solution)/shard_map/ppermute | solution.py:229
  33.8 15.2 %collective-permute-start.5 = (f16[384,512]{1,0:T(8,128)(2,1)}, f16[384,512]{1,0:T(8,128)(2,1)S(1)}, u32[]{:S(2)}, u32[]{:S(2)}) collective-permute-start(f16[384,512]{1,0:T(8,128)(2,1)} %get-tuple-element.38), channel_id=1, source_target_pairs={{0,32},{32,0},{64,96},{96,64},{1,33},{33,1},{65,97},{97,65},{2,34}... | collective-permute-start | bytes 1179656 | tf_op jit(solution)/shard_map/ppermute | solution.py:232
  34.2 19.3 %collective-permute-start.6 = (f16[384,512]{1,0:T(8,128)(2,1)}, f16[384,512]{1,0:T(8,128)(2,1)}, u32[]{:S(2)}, u32[]{:S(2)}) collective-permute-start(f16[384,512]{1,0:T(8,128)(2,1)} %get-tuple-element.40), channel_id=1, source_target_pairs={{0,64},{32,96},{64,0},{96,32},{1,65},{33,97},{65,1},{97,33},{2,66}... | collective-permute-start | bytes 1179656 | tf_op jit(solution)/shard_map/ppermute | solution.py:232
  35.6 19.9 %collective-permute-start.7 = (f16[384,512]{1,0:T(8,128)(2,1)}, f16[384,512]{1,0:T(8,128)(2,1)}, u32[]{:S(2)}, u32[]{:S(2)}) collective-permute-start(f16[384,512]{1,0:T(8,128)(2,1)} %get-tuple-element.39), channel_id=1, source_target_pairs={{0,96},{32,64},{64,32},{96,0},{1,97},{33,65},{65,33},{97,1},{2,98}... | collective-permute-start | bytes 1179656 | tf_op jit(solution)/shard_map/ppermute | solution.py:232
  40.9 26.0 %all-to-all-start.1 = ((bf16[8,48,768]{2,1,0:T(8,128)(2,1)}), bf16[8,48,768]{2,1,0:T(8,128)(2,1)S(1)}, u32[]{:S(2)}, u32[]{:S(2)}) async-start(bf16[8,48,768]{2,1,0:T(8,128)(2,1)} %embed.1), calls=%async_computation.1 | async-start | bytes 1179648 | tf_op jit(solution)/shard_map/all_to_all | solution.py:31
  57.9 15.4 %collective-permute-start.8 = (f16[384,512]{1,0:T(8,128)(2,1)}, f16[384,512]{1,0:T(8,128)(2,1)}, u32[]{:S(2)}, u32[]{:S(2)}) collective-permute-start(f16[384,512]{1,0:T(8,128)(2,1)} %get-tuple-element.36), channel_id=1, source_target_pairs={{0,128},{128,0},{1,129},{129,1},{2,130},{130,2},{3,131},{131,3},{4... | collective-permute-start | bytes 1179656 | tf_op jit(solution)/shard_map/ppermute | solution.py:229
  69.8 20.7 %all-to-all-start.2 = ((bf16[8,48,768]{2,1,0:T(8,128)(2,1)}), bf16[8,48,768]{2,1,0:T(8,128)(2,1)S(1)}, u32[]{:S(2)}, u32[]{:S(2)}) async-start(bf16[8,48,768]{2,1,0:T(8,128)(2,1)} %add_copies.1), calls=%async_computation.2 | async-start | bytes 1179648 | tf_op jit(solution)/shard_map/all_to_all | solution.py:31
  75.4 19.7 %collective-permute-start.17 = (f16[384,512]{1,0:T(8,128)(2,1)}, f16[384,512]{1,0:T(8,128)(2,1)}, u32[]{:S(2)}, u32[]{:S(2)}) collective-permute-start(f16[384,512]{1,0:T(8,128)(2,1)} %get-tuple-element.41), channel_id=1, source_target_pairs={{0,96},{32,64},{64,32},{96,0},{1,97},{33,65},{65,33},{97,1},{2,98}... | collective-permute-start | bytes 1179656 | tf_op jit(solution)/shard_map/ppermute | solution.py:232
  77.1 22.5 %collective-permute-start.16 = (f16[384,512]{1,0:T(8,128)(2,1)}, f16[384,512]{1,0:T(8,128)(2,1)}, u32[]{:S(2)}, u32[]{:S(2)}) collective-permute-start(f16[384,512]{1,0:T(8,128)(2,1)} %get-tuple-element.41), channel_id=1, source_target_pairs={{0,64},{32,96},{64,0},{96,32},{1,65},{33,97},{65,1},{97,33},{2,66}... | collective-permute-start | bytes 1179656 | tf_op jit(solution)/shard_map/ppermute | solution.py:232
  77.1 32.3 %collective-permute-start.15 = (f16[384,512]{1,0:T(8,128)(2,1)}, f16[384,512]{1,0:T(8,128)(2,1)}, u32[]{:S(2)}, u32[]{:S(2)}) collective-permute-start(f16[384,512]{1,0:T(8,128)(2,1)} %get-tuple-element.41), channel_id=1, source_target_pairs={{0,32},{32,0},{64,96},{96,64},{1,33},{33,1},{65,97},{97,65},{2,34}... | collective-permute-start | bytes 1179656 | tf_op jit(solution)/shard_map/ppermute | solution.py:232
  92.4 7.3 %collective-permute-start.11 = (bf16[4,48,768]{2,1,0:T(8,128)(2,1)S(1)}, bf16[4,48,768]{2,1,0:T(8,128)(2,1)S(1)}, u32[]{:S(2)}, u32[]{:S(2)}) collective-permute-start(bf16[4,48,768]{2,1,0:T(8,128)(2,1)S(1)} %get-tuple-element.44.refs_0_), channel_id=1, source_target_pairs={{0,2},{2,0},{1,3},{3,1},{4,6},{6,4},{5,7},{7,5},{8,10},{10,8},{9,1... | collective-permute-start | bytes 884744 | tf_op jit(solution)/shard_map/ppermute | solution.py:229
  93.5 11.5 %collective-permute-start.12 = (bf16[4,48,768]{2,1,0:T(8,128)(2,1)S(1)}, bf16[4,48,768]{2,1,0:T(8,128)(2,1)S(1)}, u32[]{:S(2)}, u32[]{:S(2)}) collective-permute-start(bf16[4,48,768]{2,1,0:T(8,128)(2,1)S(1)} %get-tuple-element.43.refs_1_), channel_id=1, source_target_pairs={{0,2},{2,0},{1,3},{3,1},{4,6},{6,4},{5,7},{7,5},{8,10},{10,8},{9,1... | collective-permute-start | bytes 884744 | tf_op jit(solution)/shard_map/ppermute | solution.py:229
  95.1 15.5 %copy-start.3 = (f32[384,256]{1,0:T(8,128)S(1)}, f32[384,256]{1,0:T(8,128)}, u32[]{:S(2)}) copy-start(f32[384,256]{1,0:T(8,128)} %get-tuple-element.27.pa) | copy-start | bytes 1179652
  95.1 15.5 %copy-start.4 = (f32[384,256]{1,0:T(8,128)S(1)}, f32[384,256]{1,0:T(8,128)}, u32[]{:S(2)}) copy-start(f32[384,256]{1,0:T(8,128)} %get-tuple-element.28.pb) | copy-start | bytes 1179652
  96.3 14.2 %collective-permute-start.10 = (bf16[4,48,768]{2,1,0:T(8,128)(2,1)S(1)}, bf16[4,48,768]{2,1,0:T(8,128)(2,1)S(1)}, u32[]{:S(2)}, u32[]{:S(2)}) collective-permute-start(bf16[4,48,768]{2,1,0:T(8,128)(2,1)S(1)} %get-tuple-element.43.refs_1_), channel_id=1, source_target_pairs={{0,1},{1,0},{2,3},{3,2},{4,5},{5,4},{6,7},{7,6},{8,9},{9,8},{10,11... | collective-permute-start | bytes 884744 | tf_op jit(solution)/shard_map/ppermute | solution.py:229
  99.6 10.9 %collective-permute-start.9 = (bf16[4,48,768]{2,1,0:T(8,128)(2,1)S(1)}, bf16[4,48,768]{2,1,0:T(8,128)(2,1)S(1)}, u32[]{:S(2)}, u32[]{:S(2)}) collective-permute-start(bf16[4,48,768]{2,1,0:T(8,128)(2,1)S(1)} %get-tuple-element.44.refs_0_), channel_id=1, source_target_pairs={{0,1},{1,0},{2,3},{3,2},{4,5},{5,4},{6,7},{7,6},{8,9},{9,8},{10,11... | collective-permute-start | bytes 884744 | tf_op jit(solution)/shard_map/ppermute | solution.py:229
  99.7 10.8 %collective-permute-start.13 = (bf16[4,48,768]{2,1,0:T(8,128)(2,1)S(1)}, bf16[4,48,768]{2,1,0:T(8,128)(2,1)S(1)}, u32[]{:S(2)}, u32[]{:S(2)}) collective-permute-start(bf16[4,48,768]{2,1,0:T(8,128)(2,1)S(1)} %collective-permute-done.11.refs_4_), channel_id=1, source_target_pairs={{0,1},{1,0},{2,3},{3,2},{4,5},{5,4},{6,7},{7,6},{8,9},{9,8},{10,11... | collective-permute-start | bytes 884744 | tf_op jit(solution)/shard_map/ppermute | solution.py:229
  105.1 5.5 %collective-permute-start.14 = (bf16[4,48,768]{2,1,0:T(8,128)(2,1)S(1)}, bf16[4,48,768]{2,1,0:T(8,128)(2,1)S(1)}, u32[]{:S(2)}, u32[]{:S(2)}) collective-permute-start(bf16[4,48,768]{2,1,0:T(8,128)(2,1)S(1)} %collective-permute-done.12.refs_5_), channel_id=1, source_target_pairs={{0,1},{1,0},{2,3},{3,2},{4,5},{5,4},{6,7},{7,6},{8,9},{9,8},{10,11... | collective-permute-start | bytes 884744 | tf_op jit(solution)/shard_map/ppermute | solution.py:229
  (6 other events, 17.7 us)

commit v3 on v2

--- a/solution.py
+++ b/solution.py
@@ -114,19 +114,11 @@
             y[2 * i + k // 3, :, (k % 3) * 256 : (k % 3 + 1) * 256] = acc[48 * i : 48 * i + 48]
 
 
-def add_copies(parts, ready, out, x, t, sem, out_sem):
-    copy = pltpu.make_async_copy(parts, x, sem)
-    copy.start()
-    copy.wait()
-    total = x[0].astype(f32)
+def add_copies(parts, ready, out):
+    total = parts[0].astype(f32)
     for d in range(1, 8):
-        total = total + x[d].astype(f32)
-    t[...] = total.astype(bf16)
-    done = [pltpu.make_async_copy(t, out.at[d], out_sem.at[d]) for d in range(8)]
-    for c in done:
-        c.start()
-    for c in done:
-        c.wait()
+        total = total + parts[d].astype(f32)
+    out[...] = jnp.broadcast_to(total.astype(bf16)[None], out.shape)
 
 
 def turn(place, va, vb, ta, tb, quarter):
@@ -140,23 +132,29 @@
         out[...] = jnp.concatenate([v, centre, jnp.zeros((112, DEPTH), bf16)], axis=0).T
 
 
-def correlate(place, sums, pa, pb, ta, tb, u, xa, xb, un, sem, out_sem):
+def correlate(place, sums, pa, pb, ta, tb, u0, u1, u2, u3, xs, xpa, xpb, xa, xb, un, sem, out_sem):
     q, yy = place[0], place[1]
-    copies = []
-    for b in range(4):
-        at = pl.ds(b * SHARE, SHARE)
-        copies.append(
-            (
-                pltpu.make_async_copy(ta.at[at, :], xa.at[b], sem.at[2 * b]),
-                pltpu.make_async_copy(tb.at[at, :], xb.at[b], sem.at[2 * b + 1]),
-            )
+    stats = [
+        pltpu.make_async_copy(src, dst, sem.at[8 + i])
+        for i, (src, dst) in enumerate(((sums, xs), (pa, xpa), (pb, xpb)))
+    ]
+    copies = {}
+    for s in (1, 2, 3, 0):
+        at = pl.ds(pl.multiple_of((s ^ yy) * SHARE, SHARE), SHARE)
+        copies[s] = (
+            pltpu.make_async_copy(ta.at[at, :], xa.at[s], sem.at[2 * s]),
+            pltpu.make_async_copy(tb.at[at, :], xb.at[s], sem.at[2 * s + 1]),
         )
-    for c in copies:
+    for t in stats:
+        t.start()
+    for c in copies.values():
         for t in c:
             t.start()
-    ma, ra, mb, rb, _ = moments(sums, q)
+    for t in stats:
+        t.wait()
+    ma, ra, mb, rb, _ = moments(xs, q)
     ns = []
-    for p, m, s in ((pa, ma, ra), (pb, mb, rb)):
+    for p, m, s in ((xpa, ma, ra), (xpb, mb, rb)):
         n = (p[...] - m) * s
         rounded = n.astype(bf16)
         excess = jnp.sum(n - rounded.astype(f32), axis=0, keepdims=True)
@@ -164,12 +162,12 @@
         ns.append(jnp.concatenate([rounded, excess, jnp.zeros((112, BLOCK), bf16)], axis=0))
     scale = U_SCALE / TOTAL
     done = []
-    for b in range(4):
-        for t in copies[b]:
+    for s, u in ((1, u1), (2, u2), (3, u3), (0, u0)):
+        for t in copies[s]:
             t.wait()
-        un[b, :, :BLOCK] = dot(xb[b], ns[0], 1, 0) * scale
-        un[b, :, BLOCK:] = dot(xa[b], ns[1], 1, 0) * scale
-        out = pltpu.make_async_copy(un.at[b], u.at[b ^ yy], out_sem.at[b])
+        un[s, :, :BLOCK] = dot(xb[s], ns[0], 1, 0) * scale
+        un[s, :, BLOCK:] = dot(xa[s], ns[1], 1, 0) * scale
+        out = pltpu.make_async_copy(un.at[s], u, out_sem.at[s])
         out.start()
         done.append(out)
     for t in done:
@@ -214,8 +212,9 @@
     )(t)
 
 
-def hand_on(whole, ready, out):
-    pass
+def halve(whole, ready, first, second):
+    first[...] = whole[:4]
+    second[...] = whole[4:]
 
 
 def local(va, vb, w):
@@ -266,29 +265,32 @@
 
     u_parts = call(
         correlate,
-        shape((4, SHARE, 2 * BLOCK), f32),
-        [SMEM] + [VMEM] * 3 + [ANY] * 2,
+        (shape((SHARE, 2 * BLOCK), f32),) * 4,
+        [SMEM] + [ANY] * 5,
         4 * ROWS * DEPTH * BLOCK,
         6 * 2**20,
         [
+            pltpu.VMEM((32, 8, BLOCK), f32),
+            pltpu.VMEM((ROWS, BLOCK), f32),
+            pltpu.VMEM((ROWS, BLOCK), f32),
             pltpu.VMEM((4, SHARE, 512), bf16),
             pltpu.VMEM((4, SHARE, 512), bf16),
             pltpu.VMEM((4, SHARE, 2 * BLOCK), f32),
-            sems((8,)),
+            sems((11,)),
             sems((4,)),
         ],
-        out_specs=ANY,
+        out_specs=(ANY,) * 4,
         name="correlate",
     )(place, sums, pa, pb, ta, tb)
-    u_parts, w_x = lax.optimization_barrier((u_parts, w_x))
+    *u_parts, w_x = lax.optimization_barrier((*u_parts, w_x))
     w_xc = swap(w_x, "c")
     u = u_parts[0]
     for s in (1, 2, 3):
         u = u + along_y(u_parts[s].astype(f16), s).astype(f32)
-    u_near = arrival(u[:8, :128], 7)
+    u_near = arrival(u[:8, :128], 8)
     u = u.astype(f16)
     u = u.astype(f32) + swap(u, "xh").astype(f32)
-    u_far = arrival(u[:8, :128], 6)
+    u_far = arrival(u[:8, :128], 4)
     u = lax.optimization_barrier(u.astype(f16))
     split = []
     for t in [u] + [along_y(u, s) for s in (1, 2, 3)]:
@@ -309,26 +311,24 @@
     y_copies = call(
         add_copies,
         shape((8,) + PIECE, bf16),
-        [ANY] * 2,
+        [VMEM] * 2,
         10 * 2**20,
         2**20,
-        [pltpu.VMEM((8,) + PIECE, bf16), pltpu.VMEM(PIECE, bf16), sems, sems((8,))],
-        out_specs=ANY,
         name="add_copies",
-        vmem=63,
+        vmem=4,
     )(exchange(y_part, "z"), u_near)
-    y0 = pl.pallas_call(
-        hand_on,
-        out_shape=shape((8,) + PIECE, bf16),
-        in_specs=[ANY, ANY],
-        out_specs=ANY,
-        input_output_aliases={0: 0},
-        compiler_params=pltpu.CompilerParams(vmem_limit_bytes=63 * 2**20),
-        name="hand_on",
+    y0 = call(
+        halve,
+        (shape((4,) + PIECE, bf16),) * 2,
+        [VMEM] * 2,
+        0,
+        2**20,
+        name="halve",
+        vmem=4,
     )(exchange(y_copies, "z"), u_far)
-    y0 = [y0[:4], y0[4:]]
     y2 = [swap(t, "xl") for t in y0]
     y1 = [swap(t, "c") for t in y0]
+    y2[1], *split = lax.optimization_barrier((y2[1], *split))
     y3 = [swap(t, "c") for t in y2]
 
     return call(

time: 115 us -> 119 us (1.035)
  waiting for transfers between devices: 27.9 us -> 41.2 us
  local copies, waits for them, and re-layouts: 6.59 us -> 3.36 us
  starting transfers between devices: 44.8 us -> 42.7 us
  other arithmetic: 11.9 us -> 9.96 us
  Pallas kernels: 21.9 us -> 20.5 us
    ppermute x6, waiting for transfers between devices: 6.44 us -> 18.3 us  [along_y(): return lax.ppermute(t, 'y', [(i, i ^ s) for i in range(4)])]
    ppermute x12, waiting for transfers between devices: 0.03 us -> 6.46 us  [swap(): return lax.ppermute(t, axis, SWAP)]
    all_to_all x3, waiting for transfers between devices: 21.4 us -> 16.4 us  [exchange(): return lax.all_to_all(blocks, axes, split_axis=0, concat_axis=0, tiled=True)]
    convert_element_type x0 -> x3, other arithmetic: none -> 4.7 us  [local(): u = u + along_y(u_parts[s].astype(f16), s).astype(f32)]
    another operation x1 -> x0, other arithmetic: 2.27 us -> none
    ppermute x12, starting transfers between devices: 19.3 us -> 17.1 us  [swap(): return lax.ppermute(t, axis, SWAP)]
    convert_element_type x1, other arithmetic: 2.41 us -> 0.22 us  [local(): u = u.astype(f16)]
    pallas_call x3, Pallas kernels: 6.83 us -> 5.51 us  [the longest x1 4.57 us: local(): call(correlate, (shape((SHARE, 2 * BLOCK), f32),) * 4, [SMEM] + [ANY] * 5...]
  transfers between devices with their start and end apart: 21 -> 21, of which waited for: 5 -> 8; matrix products, arithmetic and copies ran while one was open for 13% -> 9% of each run, Pallas kernels for 16% -> 14%
where the time goes in v3:
time: 119 us
  starting transfers between devices  42.7 us (36%)
  waiting for transfers between devices  41.2 us (35%)
  Pallas kernels  20.5 us (17%)
  other arithmetic  9.96 us (8%)
  local copies, waits for them, and re-layouts  3.36 us (3%)
    all_to_all x3, starting transfers between devices, exchange(): return lax.all_to_all(blocks, axes, split_axis=0, concat_axis=0, tiled=True)  18.4 us
    ppermute x6, waiting for transfers between devices, along_y(): return lax.ppermute(t, 'y', [(i, i ^ s) for i in range(4)])  18.3 us
    ppermute x12, starting transfers between devices, swap(): return lax.ppermute(t, axis, SWAP)  17.1 us
    all_to_all x3, waiting for transfers between devices, exchange(): return lax.all_to_all(blocks, axes, split_axis=0, concat_axis=0, tiled=True)  16.4 us
    ppermute x6, starting transfers between devices, along_y(): return lax.ppermute(t, 'y', [(i, i ^ s) for i in range(4)])  7.14 us
    ppermute x12, waiting for transfers between devices, swap(): return lax.ppermute(t, axis, SWAP)  6.46 us
    convert_element_type x3, other arithmetic, local(): u = u + along_y(u_parts[s].astype(f16), s).astype(f32)  4.7 us
    pallas_call x1, Pallas kernels, local(): call(correlate, (shape((SHARE, 2 * BLOCK), f32),) * 4, [SMEM] + [ANY] * 5...  4.57 us
  transfers between devices with their start and end apart: 21, of which 8 were waited for; matrix products, arithmetic and copies ran while one was open for 9% of the time, Pallas kernels for 14%

profile of v3, /device:TPU:1, one launch (start us, length us, event | category | flops | bytes accessed | tf_op | source)
XLA Modules:
  0.0 118.5 jit_solution(8784322777869395741)
XLA Ops:
  1.7 2.1 %collective-permute-start = (bf16[1024,256]{1,0:T(8,128)(2,1)S(1)}, bf16[1024,256]{1,0:T(8,128)(2,1)S(1)}, u32[]{:S(2)}, u32[]{:S(2)}) collective-permute-start(bf16[1024,256]{1,0:T(8,128)(2,1)S(1)} %slice.13), channel_id=1, source_target_pairs={{0,2},{2,0},{1,3},{3,1},{4,6},{6,4},{5,7},{7,5},{8,10},{10,8},{9,1... | collective-permute-start | bytes 1572872 | tf_op jit(solution)/shard_map/ppermute | solution.py:228
  3.9 1.3 %collective-permute-start.1 = (bf16[1536,256]{1,0:T(8,128)(2,1)}, bf16[1536,256]{1,0:T(8,128)(2,1)S(1)}, u32[]{:S(2)}, u32[]{:S(2)}) collective-permute-start(bf16[1536,256]{1,0:T(8,128)(2,1)} %w0.1), channel_id=1, source_target_pairs={{0,1},{1,0},{2,3},{3,2},{4,5},{5,4},{6,7},{7,6},{8,9},{9,8},{10,11... | collective-permute-start | bytes 2359304 | tf_op jit(solution)/shard_map/ppermute | solution.py:228
  5.2 3.4 %project.1 = (f32[384,256]{1,0:T(8,128)}, f32[384,256]{1,0:T(8,128)}, f32[32,8,256]{2,1,0:T(8,128)}) custom-call(bf16[384,1536]{1,0:T(8,128)(2,1)} %va.2, bf16[384,1536]{1,0:T(8,128)(2,1)} %vb.2, bf16[1536,256]{1,0:T(8,128)(2,1)} %w0.1), custom_call_target="tpu_custom_call" | custom-call | flops 603979776 | bytes 4194304 | tf_op jit(solution)/shard_map/project/pallas_call | solution.py:236
  8.6 6.6 %all-to-all-start = ((f32[32,8,256]{2,1,0:T(8,128)}), f32[32,8,256]{2,1,0:T(8,128)S(1)}, u32[]{:S(2)}, u32[]{:S(2)}) async-start(f32[32,8,256]{2,1,0:T(8,128)} %get-tuple-element.37), calls=%async_computation | async-start | bytes 524288 | tf_op jit(solution)/shard_map/all_to_all | solution.py:31
  15.8 3.9 %turn.1 = (bf16[1536,512]{1,0:T(8,128)(2,1)}, bf16[1536,512]{1,0:T(8,128)(2,1)}, bf16[192,1536]{1,0:T(8,128)(2,1)}) custom-call(s32[2]{0:T(128)} %pad_add_fusion.place, bf16[384,1536]{1,0:T(8,128)(2,1)} %va.2, bf16[384,1536]{1,0:T(8,128)(2,1)} %vb.2), custom_call_target="tpu_custom_call" | custom-call | flops 10485760 | bytes 6291456 | tf_op jit(solution)/shard_map/turn/pallas_call | solution.py:252
  19.7 4.0 %all-to-all-done.sums = f32[32,8,256]{2,1,0:T(8,128)S(1)} async-done(((f32[32,8,256]{2,1,0:T(8,128)}), f32[32,8,256]{2,1,0:T(8,128)S(1)}, u32[]{:S(2)}, u32[]{:S(2)}) %all-to-all-start) | async-done | bytes 262176 | tf_op jit(solution)/shard_map/all_to_all | solution.py:31
  24.4 4.6 %correlate.1 = (f32[384,512]{1,0:T(8,128)}, f32[384,512]{1,0:T(8,128)}, f32[384,512]{1,0:T(8,128)}, f32[384,512]{1,0:T(8,128)}) custom-call(s32[2]{0:T(128)} %pad_add_fusion.place, f32[32,8,256]{2,1,0:T(8,128)} %copy-done.1, f32[384,256]{1,0:T(8,128)} %get-tuple-element.45.pa, f32[384,256]{1,0:T(8,128)} %get-tuple-element.46.pb, ...), custom_call_target="tpu_custom_call" | custom-call | flops 603979776 | bytes 6291456 | tf_op jit(solution)/shard_map/correlate/pallas_call | solution.py:266
  30.1 1.9 %convert_element_type.66 = f16[384,512]{1,0:T(8,128)(2,1)} convert(f32[384,512]{1,0:T(8,128)} %get-tuple-element.58) | non-fusion elementwise | flops 196608 | bytes 1179648 | tf_op jit(solution)/shard_map/convert_element_type | solution.py:289
  32.5 1.9 %convert_element_type.68 = f16[384,512]{1,0:T(8,128)(2,1)} convert(f32[384,512]{1,0:T(8,128)} %get-tuple-element.59) | non-fusion elementwise | flops 196608 | bytes 1179648 | tf_op jit(solution)/shard_map/convert_element_type | solution.py:289
  36.3 2.4 %collective-permute-start.7 = (f16[384,512]{1,0:T(8,128)(2,1)}, f16[384,512]{1,0:T(8,128)(2,1)S(1)}, u32[]{:S(2)}, u32[]{:S(2)}) collective-permute-start(f16[384,512]{1,0:T(8,128)(2,1)} %convert_element_type.70), channel_id=1, source_target_pairs={{0,96},{32,64},{64,32},{96,0},{1,97},{33,65},{65,33},{97,1},{2,98}... | collective-permute-start | bytes 1179656 | tf_op jit(solution)/shard_map/ppermute | solution.py:231
  40.8 3.2 %embed.1 = bf16[8,48,768]{2,1,0:T(8,128)(2,1)} custom-call(s32[2]{0:T(128)S(1)} %copy-done.6, f32[32,8,256]{2,1,0:T(8,128)S(1)} %copy-done.2, bf16[192,1536]{1,0:T(8,128)(2,1)S(1)} %copy-done.5, bf16[1536,256]{1,0:T(8,128)(2,1)S(1)} %copy-done, bf16[1536,256]{1,0:T(8,128)(2,1)S(1)} %collective-permute-done.1.w1, ...), custom_call_target="tpu_custom_call" | custom-call | flops 1207959552 | bytes 7340032 | tf_op jit(solution)/shard_map/embed/pallas_call | solution.py:301
  44.0 8.3 %all-to-all-start.1 = ((bf16[8,48,768]{2,1,0:T(8,128)(2,1)}), bf16[8,48,768]{2,1,0:T(8,128)(2,1)S(1)}, u32[]{:S(2)}, u32[]{:S(2)}) async-start(bf16[8,48,768]{2,1,0:T(8,128)(2,1)} %embed.1), calls=%async_computation.1 | async-start | bytes 1179648 | tf_op jit(solution)/shard_map/all_to_all | solution.py:31
  52.3 3.7 %collective-permute-done.7 = f16[384,512]{1,0:T(8,128)(2,1)S(1)} collective-permute-done((f16[384,512]{1,0:T(8,128)(2,1)}, f16[384,512]{1,0:T(8,128)(2,1)S(1)}, u32[]{:S(2)}, u32[]{:S(2)}) %collective-permute-start.7) | collective-permute-done | bytes 393248 | tf_op jit(solution)/shard_map/ppermute | solution.py:231
  56.3 1.9 %collective-permute-start.8 = (f16[384,512]{1,0:T(8,128)(2,1)S(1)}, f16[384,512]{1,0:T(8,128)(2,1)S(1)}, u32[]{:S(2)}, u32[]{:S(2)}) collective-permute-start(f16[384,512]{1,0:T(8,128)(2,1)S(1)} %get-tuple-element.72), channel_id=1, source_target_pairs={{0,128},{128,0},{1,129},{129,1},{2,130},{130,2},{3,131},{131,3},{4... | collective-permute-start | bytes 1179656 | tf_op jit(solution)/shard_map/ppermute | solution.py:228
  59.3 12.4 %all-to-all-done.1.parts = bf16[8,48,768]{2,1,0:T(8,128)(2,1)S(1)} async-done(((bf16[8,48,768]{2,1,0:T(8,128)(2,1)}), bf16[8,48,768]{2,1,0:T(8,128)(2,1)S(1)}, u32[]{:S(2)}, u32[]{:S(2)}) %all-to-all-start.1) | async-done | bytes 589856 | tf_op jit(solution)/shard_map/all_to_all | solution.py:31
  73.3 3.5 %all-to-all-start.2 = ((bf16[8,48,768]{2,1,0:T(8,128)(2,1)}), bf16[8,48,768]{2,1,0:T(8,128)(2,1)S(1)}, u32[]{:S(2)}, u32[]{:S(2)}) async-start(bf16[8,48,768]{2,1,0:T(8,128)(2,1)} %add_copies.1), calls=%async_computation.2 | async-start | bytes 1179648 | tf_op jit(solution)/shard_map/all_to_all | solution.py:31
  78.7 2.3 %collective-permute-start.13 = (f16[384,512]{1,0:T(8,128)(2,1)}, f16[384,512]{1,0:T(8,128)(2,1)}, u32[]{:S(2)}, u32[]{:S(2)}) collective-permute-start(f16[384,512]{1,0:T(8,128)(2,1)} %get-tuple-element.74), channel_id=1, source_target_pairs={{0,32},{32,0},{64,96},{96,64},{1,33},{33,1},{65,97},{97,65},{2,34}... | collective-permute-start | bytes 1179656 | tf_op jit(solution)/shard_map/ppermute | solution.py:231
  83.3 14.6 %collective-permute-done.15 = f16[384,512]{1,0:T(8,128)(2,1)S(1)} collective-permute-done((f16[384,512]{1,0:T(8,128)(2,1)}, f16[384,512]{1,0:T(8,128)(2,1)S(1)}, u32[]{:S(2)}, u32[]{:S(2)}) %collective-permute-start.15) | collective-permute-done | bytes 393248 | tf_op jit(solution)/shard_map/ppermute | solution.py:231
  102.0 1.8 %collective-permute-start.10 = (bf16[4,48,768]{2,1,0:T(8,128)(2,1)S(1)}, bf16[4,48,768]{2,1,0:T(8,128)(2,1)S(1)}, u32[]{:S(2)}, u32[]{:S(2)}) collective-permute-start(bf16[4,48,768]{2,1,0:T(8,128)(2,1)S(1)} %get-tuple-element.62.refs_1_), channel_id=1, source_target_pairs={{0,1},{1,0},{2,3},{3,2},{4,5},{5,4},{6,7},{7,6},{8,9},{9,8},{10,11... | collective-permute-start | bytes 884744 | tf_op jit(solution)/shard_map/ppermute | solution.py:228
  103.9 1.6 %collective-permute-done.12.refs_5_ = bf16[4,48,768]{2,1,0:T(8,128)(2,1)S(1)} collective-permute-done((bf16[4,48,768]{2,1,0:T(8,128)(2,1)S(1)}, bf16[4,48,768]{2,1,0:T(8,128)(2,1)S(1)}, u32[]{:S(2)}, u32[]{:S(2)}) %collective-permute-start.12) | collective-permute-done | bytes 294944 | tf_op jit(solution)/shard_map/ppermute | solution.py:228
  105.5 3.8 %collective-permute-start.17 = (bf16[4,48,768]{2,1,0:T(8,128)(2,1)S(1)}, bf16[4,48,768]{2,1,0:T(8,128)(2,1)S(1)}, u32[]{:S(2)}, u32[]{:S(2)}) collective-permute-start(bf16[4,48,768]{2,1,0:T(8,128)(2,1)S(1)} %collective-permute-done.12.refs_5_), channel_id=1, source_target_pairs={{0,1},{1,0},{2,3},{3,2},{4,5},{5,4},{6,7},{7,6},{8,9},{9,8},{10,11... | collective-permute-start | bytes 884744 | tf_op jit(solution)/shard_map/ppermute | solution.py:228
  109.4 2.5 %collective-permute-done.11.refs_4_ = bf16[4,48,768]{2,1,0:T(8,128)(2,1)S(1)} collective-permute-done((bf16[4,48,768]{2,1,0:T(8,128)(2,1)S(1)}, bf16[4,48,768]{2,1,0:T(8,128)(2,1)S(1)}, u32[]{:S(2)}, u32[]{:S(2)}) %collective-permute-start.11) | collective-permute-done | bytes 294944 | tf_op jit(solution)/shard_map/ppermute | solution.py:228
  111.8 2.1 %collective-permute-start.16 = (bf16[4,48,768]{2,1,0:T(8,128)(2,1)S(1)}, bf16[4,48,768]{2,1,0:T(8,128)(2,1)S(1)}, u32[]{:S(2)}, u32[]{:S(2)}) collective-permute-start(bf16[4,48,768]{2,1,0:T(8,128)(2,1)S(1)} %collective-permute-done.11.refs_4_), channel_id=1, source_target_pairs={{0,1},{1,0},{2,3},{3,2},{4,5},{5,4},{6,7},{7,6},{8,9},{9,8},{10,11... | collective-permute-start | bytes 884744 | tf_op jit(solution)/shard_map/ppermute | solution.py:228
  115.2 3.3 %combine.1 = (f32[384,256]{1,0:T(8,128)}, f32[384,256]{1,0:T(8,128)}) custom-call(s32[2]{0:T(128)S(1)} %copy-done.6, f32[32,8,256]{2,1,0:T(8,128)S(1)} %copy-done.2, f32[384,256]{1,0:T(8,128)S(1)} %copy-done.3, f32[384,256]{1,0:T(8,128)S(1)} %copy-done.4, bf16[4,48,768]{2,1,0:T(8,128)(2,1)S(1)} %get-tuple-element.61.refs_0_, ...), custom_call_target="tpu_custom_call" | custom-call | flops 1207959552 | bytes 8388608 | tf_op jit(solution)/shard_map/combine/pallas_call | solution.py:334
  (63 shorter events, 20.4 us)
Async XLA Ops:
  1.7 22.0 %collective-permute-start = (bf16[1024,256]{1,0:T(8,128)(2,1)S(1)}, bf16[1024,256]{1,0:T(8,128)(2,1)S(1)}, u32[]{:S(2)}, u32[]{:S(2)}) collective-permute-start(bf16[1024,256]{1,0:T(8,128)(2,1)S(1)} %slice.13), channel_id=1, source_target_pairs={{0,2},{2,0},{1,3},{3,1},{4,6},{6,4},{5,7},{7,5},{8,10},{10,8},{9,1... | collective-permute-start | bytes 1572872 | tf_op jit(solution)/shard_map/ppermute | solution.py:228
  3.9 34.9 %collective-permute-start.1 = (bf16[1536,256]{1,0:T(8,128)(2,1)}, bf16[1536,256]{1,0:T(8,128)(2,1)S(1)}, u32[]{:S(2)}, u32[]{:S(2)}) collective-permute-start(bf16[1536,256]{1,0:T(8,128)(2,1)} %w0.1), channel_id=1, source_target_pairs={{0,1},{1,0},{2,3},{3,2},{4,5},{5,4},{6,7},{7,6},{8,9},{9,8},{10,11... | collective-permute-start | bytes 2359304 | tf_op jit(solution)/shard_map/ppermute | solution.py:228
  8.6 15.1 %all-to-all-start = ((f32[32,8,256]{2,1,0:T(8,128)}), f32[32,8,256]{2,1,0:T(8,128)S(1)}, u32[]{:S(2)}, u32[]{:S(2)}) async-start(f32[32,8,256]{2,1,0:T(8,128)} %get-tuple-element.37), calls=%async_computation | async-start | bytes 524288 | tf_op jit(solution)/shard_map/all_to_all | solution.py:31
  23.7 12.6 %collective-permute-start.2 = (bf16[512,256]{1,0:T(8,128)(2,1)S(1)}, bf16[512,256]{1,0:T(8,128)(2,1)S(1)}, u32[]{:S(2)}, u32[]{:S(2)}) collective-permute-start(bf16[512,256]{1,0:T(8,128)(2,1)S(1)} %slice.12), channel_id=1, source_target_pairs={{0,2},{2,0},{1,3},{3,1},{4,6},{6,4},{5,7},{7,5},{8,10},{10,8},{9,1... | collective-permute-start | bytes 786440 | tf_op jit(solution)/shard_map/ppermute | solution.py:228
  29.0 10.7 %collective-permute-start.3 = (bf16[1024,256]{1,0:T(8,128)(2,1)S(1)}, bf16[1024,256]{1,0:T(8,128)(2,1)S(1)}, u32[]{:S(2)}, u32[]{:S(2)}) collective-permute-start(bf16[1024,256]{1,0:T(8,128)(2,1)S(1)} %collective-permute-done.w2), channel_id=1, source_target_pairs={{0,1},{1,0},{2,3},{3,2},{4,5},{5,4},{6,7},{7,6},{8,9},{9,8},{10,11... | collective-permute-start | bytes 1572872 | tf_op jit(solution)/shard_map/ppermute | solution.py:228
  32.1 20.2 %collective-permute-start.5 = (f16[384,512]{1,0:T(8,128)(2,1)}, f16[384,512]{1,0:T(8,128)(2,1)S(1)}, u32[]{:S(2)}, u32[]{:S(2)}) collective-permute-start(f16[384,512]{1,0:T(8,128)(2,1)} %convert_element_type.66), channel_id=1, source_target_pairs={{0,32},{32,0},{64,96},{96,64},{1,33},{33,1},{65,97},{97,65},{2,34}... | collective-permute-start | bytes 1179656 | tf_op jit(solution)/shard_map/ppermute | solution.py:231
  34.5 17.9 %collective-permute-start.6 = (f16[384,512]{1,0:T(8,128)(2,1)}, f16[384,512]{1,0:T(8,128)(2,1)S(1)}, u32[]{:S(2)}, u32[]{:S(2)}) collective-permute-start(f16[384,512]{1,0:T(8,128)(2,1)} %convert_element_type.68), channel_id=1, source_target_pairs={{0,64},{32,96},{64,0},{96,32},{1,65},{33,97},{65,1},{97,33},{2,66}... | collective-permute-start | bytes 1179656 | tf_op jit(solution)/shard_map/ppermute | solution.py:231
  36.3 19.7 %collective-permute-start.7 = (f16[384,512]{1,0:T(8,128)(2,1)}, f16[384,512]{1,0:T(8,128)(2,1)S(1)}, u32[]{:S(2)}, u32[]{:S(2)}) collective-permute-start(f16[384,512]{1,0:T(8,128)(2,1)} %convert_element_type.70), channel_id=1, source_target_pairs={{0,96},{32,64},{64,32},{96,0},{1,97},{33,65},{65,33},{97,1},{2,98}... | collective-permute-start | bytes 1179656 | tf_op jit(solution)/shard_map/ppermute | solution.py:231
  38.7 2.1 %collective-permute-start.4 = (bf16[512,256]{1,0:T(8,128)(2,1)S(1)}, bf16[512,256]{1,0:T(8,128)(2,1)S(1)}, u32[]{:S(2)}, u32[]{:S(2)}) collective-permute-start(bf16[512,256]{1,0:T(8,128)(2,1)S(1)} %collective-permute-done.2.w2b), channel_id=1, source_target_pairs={{0,1},{1,0},{2,3},{3,2},{4,5},{5,4},{6,7},{7,6},{8,9},{9,8},{10,11... | collective-permute-start | bytes 786440 | tf_op jit(solution)/shard_map/ppermute | solution.py:228
  44.0 27.7 %all-to-all-start.1 = ((bf16[8,48,768]{2,1,0:T(8,128)(2,1)}), bf16[8,48,768]{2,1,0:T(8,128)(2,1)S(1)}, u32[]{:S(2)}, u32[]{:S(2)}) async-start(bf16[8,48,768]{2,1,0:T(8,128)(2,1)} %embed.1), calls=%async_computation.1 | async-start | bytes 1179648 | tf_op jit(solution)/shard_map/all_to_all | solution.py:31
  56.3 20.5 %collective-permute-start.8 = (f16[384,512]{1,0:T(8,128)(2,1)S(1)}, f16[384,512]{1,0:T(8,128)(2,1)S(1)}, u32[]{:S(2)}, u32[]{:S(2)}) collective-permute-start(f16[384,512]{1,0:T(8,128)(2,1)S(1)} %get-tuple-element.72), channel_id=1, source_target_pairs={{0,128},{128,0},{1,129},{129,1},{2,130},{130,2},{3,131},{131,3},{4... | collective-permute-start | bytes 1179656 | tf_op jit(solution)/shard_map/ppermute | solution.py:228
  73.3 24.8 %all-to-all-start.2 = ((bf16[8,48,768]{2,1,0:T(8,128)(2,1)}), bf16[8,48,768]{2,1,0:T(8,128)(2,1)S(1)}, u32[]{:S(2)}, u32[]{:S(2)}) async-start(bf16[8,48,768]{2,1,0:T(8,128)(2,1)} %add_copies.1), calls=%async_computation.2 | async-start | bytes 1179648 | tf_op jit(solution)/shard_map/all_to_all | solution.py:31
  77.7 20.2 %collective-permute-start.15 = (f16[384,512]{1,0:T(8,128)(2,1)}, f16[384,512]{1,0:T(8,128)(2,1)S(1)}, u32[]{:S(2)}, u32[]{:S(2)}) collective-permute-start(f16[384,512]{1,0:T(8,128)(2,1)} %get-tuple-element.74), channel_id=1, source_target_pairs={{0,96},{32,64},{64,32},{96,0},{1,97},{33,65},{65,33},{97,1},{2,98}... | collective-permute-start | bytes 1179656 | tf_op jit(solution)/shard_map/ppermute | solution.py:231
  78.1 21.5 %collective-permute-start.14 = (f16[384,512]{1,0:T(8,128)(2,1)}, f16[384,512]{1,0:T(8,128)(2,1)}, u32[]{:S(2)}, u32[]{:S(2)}) collective-permute-start(f16[384,512]{1,0:T(8,128)(2,1)} %get-tuple-element.74), channel_id=1, source_target_pairs={{0,64},{32,96},{64,0},{96,32},{1,65},{33,97},{65,1},{97,33},{2,66}... | collective-permute-start | bytes 1179656 | tf_op jit(solution)/shard_map/ppermute | solution.py:231
  78.7 22.1 %collective-permute-start.13 = (f16[384,512]{1,0:T(8,128)(2,1)}, f16[384,512]{1,0:T(8,128)(2,1)}, u32[]{:S(2)}, u32[]{:S(2)}) collective-permute-start(f16[384,512]{1,0:T(8,128)(2,1)} %get-tuple-element.74), channel_id=1, source_target_pairs={{0,32},{32,0},{64,96},{96,64},{1,33},{33,1},{65,97},{97,65},{2,34}... | collective-permute-start | bytes 1179656 | tf_op jit(solution)/shard_map/ppermute | solution.py:231
  82.1 15.9 %copy-start.7 = (f32[8,128]{1,0:T(8,128)S(1)}, f32[8,128]{1,0:T(8,128)}, u32[]{:S(2)}) copy-start(f32[8,128]{1,0:T(8,128)} %mark.3.ready) | copy-start | bytes 12292
  98.0 17.1 %copy-start.3 = (f32[384,256]{1,0:T(8,128)S(1)}, f32[384,256]{1,0:T(8,128)}, u32[]{:S(2)}) copy-start(f32[384,256]{1,0:T(8,128)} %get-tuple-element.45.pa) | copy-start | bytes 1179652
  98.1 17.1 %copy-start.4 = (f32[384,256]{1,0:T(8,128)S(1)}, f32[384,256]{1,0:T(8,128)}, u32[]{:S(2)}) copy-start(f32[384,256]{1,0:T(8,128)} %get-tuple-element.46.pb) | copy-start | bytes 1179652
  98.1 7.4 %collective-permute-start.12 = (bf16[4,48,768]{2,1,0:T(8,128)(2,1)S(1)}, bf16[4,48,768]{2,1,0:T(8,128)(2,1)S(1)}, u32[]{:S(2)}, u32[]{:S(2)}) collective-permute-start(bf16[4,48,768]{2,1,0:T(8,128)(2,1)S(1)} %get-tuple-element.62.refs_1_), channel_id=1, source_target_pairs={{0,2},{2,0},{1,3},{3,1},{4,6},{6,4},{5,7},{7,5},{8,10},{10,8},{9,1... | collective-permute-start | bytes 884744 | tf_op jit(solution)/shard_map/ppermute | solution.py:228
  99.4 12.4 %collective-permute-start.11 = (bf16[4,48,768]{2,1,0:T(8,128)(2,1)S(1)}, bf16[4,48,768]{2,1,0:T(8,128)(2,1)S(1)}, u32[]{:S(2)}, u32[]{:S(2)}) collective-permute-start(bf16[4,48,768]{2,1,0:T(8,128)(2,1)S(1)} %get-tuple-element.61.refs_0_), channel_id=1, source_target_pairs={{0,2},{2,0},{1,3},{3,1},{4,6},{6,4},{5,7},{7,5},{8,10},{10,8},{9,1... | collective-permute-start | bytes 884744 | tf_op jit(solution)/shard_map/ppermute | solution.py:228
  102.0 12.0 %collective-permute-start.10 = (bf16[4,48,768]{2,1,0:T(8,128)(2,1)S(1)}, bf16[4,48,768]{2,1,0:T(8,128)(2,1)S(1)}, u32[]{:S(2)}, u32[]{:S(2)}) collective-permute-start(bf16[4,48,768]{2,1,0:T(8,128)(2,1)S(1)} %get-tuple-element.62.refs_1_), channel_id=1, source_target_pairs={{0,1},{1,0},{2,3},{3,2},{4,5},{5,4},{6,7},{7,6},{8,9},{9,8},{10,11... | collective-permute-start | bytes 884744 | tf_op jit(solution)/shard_map/ppermute | solution.py:228
  103.8 10.2 %collective-permute-start.9 = (bf16[4,48,768]{2,1,0:T(8,128)(2,1)S(1)}, bf16[4,48,768]{2,1,0:T(8,128)(2,1)S(1)}, u32[]{:S(2)}, u32[]{:S(2)}) collective-permute-start(bf16[4,48,768]{2,1,0:T(8,128)(2,1)S(1)} %get-tuple-element.61.refs_0_), channel_id=1, source_target_pairs={{0,1},{1,0},{2,3},{3,2},{4,5},{5,4},{6,7},{7,6},{8,9},{9,8},{10,11... | collective-permute-start | bytes 884744 | tf_op jit(solution)/shard_map/ppermute | solution.py:228
  105.5 8.5 %collective-permute-start.17 = (bf16[4,48,768]{2,1,0:T(8,128)(2,1)S(1)}, bf16[4,48,768]{2,1,0:T(8,128)(2,1)S(1)}, u32[]{:S(2)}, u32[]{:S(2)}) collective-permute-start(bf16[4,48,768]{2,1,0:T(8,128)(2,1)S(1)} %collective-permute-done.12.refs_5_), channel_id=1, source_target_pairs={{0,1},{1,0},{2,3},{3,2},{4,5},{5,4},{6,7},{7,6},{8,9},{9,8},{10,11... | collective-permute-start | bytes 884744 | tf_op jit(solution)/shard_map/ppermute | solution.py:228
  111.8 3.3 %collective-permute-start.16 = (bf16[4,48,768]{2,1,0:T(8,128)(2,1)S(1)}, bf16[4,48,768]{2,1,0:T(8,128)(2,1)S(1)}, u32[]{:S(2)}, u32[]{:S(2)}) collective-permute-start(bf16[4,48,768]{2,1,0:T(8,128)(2,1)S(1)} %collective-permute-done.11.refs_4_), channel_id=1, source_target_pairs={{0,1},{1,0},{2,3},{3,2},{4,5},{5,4},{6,7},{7,6},{8,9},{9,8},{10,11... | collective-permute-start | bytes 884744 | tf_op jit(solution)/shard_map/ppermute | solution.py:228
  (8 other events, 69.0 us)

commit v4 on v3

--- a/solution.py
+++ b/solution.py
@@ -132,7 +132,7 @@
         out[...] = jnp.concatenate([v, centre, jnp.zeros((112, DEPTH), bf16)], axis=0).T
 
 
-def correlate(place, sums, pa, pb, ta, tb, u0, u1, u2, u3, xs, xpa, xpb, xa, xb, un, sem, out_sem):
+def correlate(place, sums, pa, pb, ta, tb, u0, u1, u2, u3, xs, xpa, xpb, xa, xb, sem):
     q, yy = place[0], place[1]
     stats = [
         pltpu.make_async_copy(src, dst, sem.at[8 + i])
@@ -140,7 +140,7 @@
     ]
     copies = {}
     for s in (1, 2, 3, 0):
-        at = pl.ds(pl.multiple_of((s ^ yy) * SHARE, SHARE), SHARE)
+        at = pl.ds(pl.multiple_of(((yy + s) & 3) * SHARE, SHARE), SHARE)
         copies[s] = (
             pltpu.make_async_copy(ta.at[at, :], xa.at[s], sem.at[2 * s]),
             pltpu.make_async_copy(tb.at[at, :], xb.at[s], sem.at[2 * s + 1]),
@@ -161,17 +161,11 @@
         excess = jnp.concatenate([excess, jnp.zeros((15, BLOCK), f32)], axis=0).astype(bf16)
         ns.append(jnp.concatenate([rounded, excess, jnp.zeros((112, BLOCK), bf16)], axis=0))
     scale = U_SCALE / TOTAL
-    done = []
     for s, u in ((1, u1), (2, u2), (3, u3), (0, u0)):
         for t in copies[s]:
             t.wait()
-        un[s, :, :BLOCK] = dot(xb[s], ns[0], 1, 0) * scale
-        un[s, :, BLOCK:] = dot(xa[s], ns[1], 1, 0) * scale
-        out = pltpu.make_async_copy(un.at[s], u, out_sem.at[s])
-        out.start()
-        done.append(out)
-    for t in done:
-        t.wait()
+        u[:, :BLOCK] = dot(xb[s], ns[0], 1, 0) * scale
+        u[:, BLOCK:] = dot(xa[s], ns[1], 1, 0) * scale
 
 
 def combine(place, sums, pa, pb, *refs):
@@ -191,7 +185,7 @@
         acc = (p[...] - m) * (r * (corr - 2.0))
         cols = slice(first, first + BLOCK)
         for s in range(4):
-            at = pl.ds(pl.multiple_of((yy ^ s) * SHARE, 128), SHARE)
+            at = pl.ds(pl.multiple_of(((yy + 4 - s) & 3) * SHARE, 128), SHARE)
             part = y[:, at]
             acc = acc + (dot(part, us[2 * s][:, cols], 1, 0) + dot(part, us[2 * s + 1][:, cols], 1, 0))
         out[...] = acc
@@ -228,7 +222,7 @@
         return lax.ppermute(t, axis, SWAP)
 
     def along_y(t, s):
-        return lax.ppermute(t, "y", [(i, i ^ s) for i in range(4)])
+        return lax.ppermute(t, "y", [(i, (i + s) % 4) for i in range(4)])
 
     w_c = swap(w, "c")
     w_x = swap(w[:half], "xl")
@@ -275,12 +269,10 @@
             pltpu.VMEM((ROWS, BLOCK), f32),
             pltpu.VMEM((4, SHARE, 512), bf16),
             pltpu.VMEM((4, SHARE, 512), bf16),
-            pltpu.VMEM((4, SHARE, 2 * BLOCK), f32),
             sems((11,)),
-            sems((4,)),
         ],
-        out_specs=(ANY,) * 4,
         name="correlate",
+        vmem=20,
     )(place, sums, pa, pb, ta, tb)
     *u_parts, w_x = lax.optimization_barrier((*u_parts, w_x))
     w_xc = swap(w_x, "c")
@@ -292,11 +284,7 @@
     u = u.astype(f32) + swap(u, "xh").astype(f32)
     u_far = arrival(u[:8, :128], 4)
     u = lax.optimization_barrier(u.astype(f16))
-    split = []
-    for t in [u] + [along_y(u, s) for s in (1, 2, 3)]:
-        t = t.astype(f32) * (1.0 / U_SCALE)
-        high = lax.reduce_precision(t, 8, 7)
-        split += [high.astype(bf16), (t - high).astype(bf16)]
+    us = [u] + [along_y(u, s) for s in (1, 2, 3)]
 
     y_part = call(
         embed,
@@ -327,8 +315,13 @@
         vmem=4,
     )(exchange(y_copies, "z"), u_far)
     y2 = [swap(t, "xl") for t in y0]
+    *y0, us[1], us[2], us[3] = lax.optimization_barrier((*y0, *us[1:]))
+    split = []
+    for t in us:
+        t = t.astype(f32) * (1.0 / U_SCALE)
+        high = lax.reduce_precision(t, 8, 7)
+        split += [high.astype(bf16), (t - high).astype(bf16)]
     y1 = [swap(t, "c") for t in y0]
-    y2[1], *split = lax.optimization_barrier((y2[1], *split))
     y3 = [swap(t, "c") for t in y2]
 
     return call(

time: 119 us -> 119 us (level)
  local copies, waits for them, and re-layouts: 3.36 us -> 8.51 us
  starting transfers between devices: 42.7 us -> 38 us
  other arithmetic: 9.96 us -> 8.18 us
  waiting for transfers between devices: 41.2 us -> 42.4 us
    ppermute x6, waiting for transfers between devices: 18.3 us -> 4.7 us  [along_y(): return lax.ppermute(t, 'y', [(i, (i + s) % 4) for i in range(4)])]
    all_to_all x3, waiting for transfers between devices: 16.4 us -> 27.3 us  [exchange(): return lax.all_to_all(blocks, axes, split_axis=0, concat_axis=0, tiled=True)]
    ppermute x12, starting transfers between devices: 17.1 us -> 12.9 us  [swap(): return lax.ppermute(t, axis, SWAP)]
    ppermute x12, waiting for transfers between devices: 6.46 us -> 10.5 us  [swap(): return lax.ppermute(t, axis, SWAP)]
    unnamed x22, local copies, waits for them, and re-layouts: 1.1 us -> 4.71 us
    convert_element_type x3, other arithmetic: 4.7 us -> 2.41 us  [local(): u = u + along_y(u_parts[s].astype(f16), s).astype(f32)]
    convert_element_type x1, other arithmetic: 0.22 us -> 1.5 us  [local(): u = u.astype(f16)]
    convert_element_type x4 -> x3, other arithmetic: 3.52 us -> 2.56 us  [local(): split += [high.astype(bf16), (t - high).astype(bf16)]]
  transfers between devices with their start and end apart: 21 -> 21, of which waited for: 8 -> 9; matrix products, arithmetic and copies ran while one was open for 9% -> 9% of each run, Pallas kernels for 14% -> 14%
where the time goes in v4:
time: 119 us; the launch traced here: 118 us
  waiting for transfers between devices  42.4 us (36%)
  starting transfers between devices  38 us (32%)
  Pallas kernels  20.1 us (17%)
  local copies, waits for them, and re-layouts  8.51 us (7%)
  other arithmetic  8.18 us (7%)
    all_to_all x3, waiting for transfers between devices, exchange(): return lax.all_to_all(blocks, axes, split_axis=0, concat_axis=0, tiled=True)  27.3 us
    all_to_all x3, starting transfers between devices, exchange(): return lax.all_to_all(blocks, axes, split_axis=0, concat_axis=0, tiled=True)  18.4 us
    ppermute x12, starting transfers between devices, swap(): return lax.ppermute(t, axis, SWAP)  12.9 us
    ppermute x12, waiting for transfers between devices, swap(): return lax.ppermute(t, axis, SWAP)  10.5 us
    ppermute x6, starting transfers between devices, along_y(): return lax.ppermute(t, 'y', [(i, (i + s) % 4) for i in range(4)])  6.7 us
    unnamed x22, local copies, waits for them, and re-layouts  4.71 us
    ppermute x6, waiting for transfers between devices, along_y(): return lax.ppermute(t, 'y', [(i, (i + s) % 4) for i in range(4)])  4.7 us
    pallas_call x1, Pallas kernels, local(): call(correlate, (shape((SHARE, 2 * BLOCK), f32),) * 4, [SMEM] + [ANY] * 5...  4.2 us
  transfers between devices with their start and end apart: 21, of which 9 were waited for; matrix products, arithmetic and copies ran while one was open for 9% of the time, Pallas kernels for 14%

profile of v4, /device:TPU:1, one launch (start us, length us, event | category | flops | bytes accessed | tf_op | source)
XLA Modules:
  0.0 118.1 jit_solution(4704440823284932431)
XLA Ops:
  0.6 1.9 %slice.13 = bf16[1024,256]{1,0:T(8,128)(2,1)} slice(bf16[1536,256]{1,0:T(8,128)(2,1)} %w0.1), slice={[0:1024], [0:256]} | slice | bytes 1048576 | tf_op jit(solution)/shard_map/slice | solution.py:228
  2.5 2.0 %collective-permute-start = (bf16[1024,256]{1,0:T(8,128)(2,1)}, bf16[1024,256]{1,0:T(8,128)(2,1)S(1)}, u32[]{:S(2)}, u32[]{:S(2)}) collective-permute-start(bf16[1024,256]{1,0:T(8,128)(2,1)} %slice.13), channel_id=1, source_target_pairs={{0,2},{2,0},{1,3},{3,1},{4,6},{6,4},{5,7},{7,5},{8,10},{10,8},{9,1... | collective-permute-start | bytes 1572872 | tf_op jit(solution)/shard_map/ppermute | solution.py:222
  5.7 3.4 %project.1 = (f32[384,256]{1,0:T(8,128)}, f32[384,256]{1,0:T(8,128)}, f32[32,8,256]{2,1,0:T(8,128)}) custom-call(bf16[384,1536]{1,0:T(8,128)(2,1)} %va.2, bf16[384,1536]{1,0:T(8,128)(2,1)} %vb.2, bf16[1536,256]{1,0:T(8,128)(2,1)} %w0.1), custom_call_target="tpu_custom_call" | custom-call | flops 603979776 | bytes 4194304 | tf_op jit(solution)/shard_map/project/pallas_call | solution.py:230
  9.1 6.7 %all-to-all-start = ((f32[32,8,256]{2,1,0:T(8,128)}), f32[32,8,256]{2,1,0:T(8,128)S(1)}, u32[]{:S(2)}, u32[]{:S(2)}) async-start(f32[32,8,256]{2,1,0:T(8,128)} %get-tuple-element.33), calls=%async_computation | async-start | bytes 524288 | tf_op jit(solution)/shard_map/all_to_all | solution.py:31
  17.2 3.9 %turn.1 = (bf16[1536,512]{1,0:T(8,128)(2,1)}, bf16[1536,512]{1,0:T(8,128)(2,1)}, bf16[192,1536]{1,0:T(8,128)(2,1)}) custom-call(s32[2]{0:T(128)} %pad_add_fusion.place, bf16[384,1536]{1,0:T(8,128)(2,1)} %va.2, bf16[384,1536]{1,0:T(8,128)(2,1)} %vb.2), custom_call_target="tpu_custom_call" | custom-call | flops 10485760 | bytes 6291456 | tf_op jit(solution)/shard_map/turn/pallas_call | solution.py:246
  21.1 3.3 %all-to-all-done.sums = f32[32,8,256]{2,1,0:T(8,128)S(1)} async-done(((f32[32,8,256]{2,1,0:T(8,128)}), f32[32,8,256]{2,1,0:T(8,128)S(1)}, u32[]{:S(2)}, u32[]{:S(2)}) %all-to-all-start) | async-done | bytes 262176 | tf_op jit(solution)/shard_map/all_to_all | solution.py:31
  25.2 1.4 %copy-done.1 = bf16[1536,512]{1,0:T(8,128)(2,1)S(1)} copy-done((bf16[1536,512]{1,0:T(8,128)(2,1)S(1)}, bf16[1536,512]{1,0:T(8,128)(2,1)}, u32[]{:S(2)}) %copy-start.1) | copy-done | bytes 1572888
  26.6 1.4 %copy-done.2 = bf16[1536,512]{1,0:T(8,128)(2,1)S(1)} copy-done((bf16[1536,512]{1,0:T(8,128)(2,1)S(1)}, bf16[1536,512]{1,0:T(8,128)(2,1)}, u32[]{:S(2)}) %copy-start.2) | copy-done | bytes 1572888
  28.0 4.2 %correlate.1 = (f32[384,512]{1,0:T(8,128)S(1)}, f32[384,512]{1,0:T(8,128)S(1)}, f32[384,512]{1,0:T(8,128)S(1)}, f32[384,512]{1,0:T(8,128)S(1)}) custom-call(s32[2]{0:T(128)S(1)} %copy-done.8, f32[32,8,256]{2,1,0:T(8,128)S(1)} %all-to-all-done.sums, f32[384,256]{1,0:T(8,128)S(1)} %copy-done.3, f32[384,256]{1,0:T(8,128)S(1)} %copy-done.4, ...), custom_call_target="tpu_custom_call" | custom-call | flops 603979776 | bytes 6291456 | tf_op jit(solution)/shard_map/correlate/pallas_call | solution.py:260
  37.3 1.3 %collective-permute-start.7 = (f16[384,512]{1,0:T(8,128)(2,1)}, f16[384,512]{1,0:T(8,128)(2,1)}, u32[]{:S(2)}, u32[]{:S(2)}) collective-permute-start(f16[384,512]{1,0:T(8,128)(2,1)} %convert_element_type.70), channel_id=1, source_target_pairs={{0,96},{32,0},{64,32},{96,64},{1,97},{33,1},{65,33},{97,65},{2,98}... | collective-permute-start | bytes 1179656 | tf_op jit(solution)/shard_map/ppermute | solution.py:225
  40.6 3.1 %embed.1 = bf16[8,48,768]{2,1,0:T(8,128)(2,1)} custom-call(s32[2]{0:T(128)S(1)} %copy-done.8, f32[32,8,256]{2,1,0:T(8,128)S(1)} %all-to-all-done.sums, bf16[192,1536]{1,0:T(8,128)(2,1)S(1)} %copy-done.5, bf16[1536,256]{1,0:T(8,128)(2,1)S(1)} %copy-done, bf16[1536,256]{1,0:T(8,128)(2,1)S(1)} %collective-permute-done.1.w1, bf16[1024,256]{1,0:T(8,128)(2,1)S(1)} %copy-done.7, ...), custom_call_target="tpu_custom_call" | custom-call | flops 1207959552 | bytes 7340032 | tf_op jit(solution)/shard_map/embed/pallas_call | solution.py:289
  43.7 8.1 %all-to-all-start.1 = ((bf16[8,48,768]{2,1,0:T(8,128)(2,1)}), bf16[8,48,768]{2,1,0:T(8,128)(2,1)S(1)}, u32[]{:S(2)}, u32[]{:S(2)}) async-start(bf16[8,48,768]{2,1,0:T(8,128)(2,1)} %embed.1), calls=%async_computation.1 | async-start | bytes 1179648 | tf_op jit(solution)/shard_map/all_to_all | solution.py:31
  51.9 3.0 %collective-permute-done.5 = f16[384,512]{1,0:T(8,128)(2,1)} collective-permute-done((f16[384,512]{1,0:T(8,128)(2,1)}, f16[384,512]{1,0:T(8,128)(2,1)}, u32[]{:S(2)}, u32[]{:S(2)}) %collective-permute-start.5) | collective-permute-done | bytes 393248 | tf_op jit(solution)/shard_map/ppermute | solution.py:225
  56.0 1.5 %fusion.5 = (f16[384,512]{1,0:T(8,128)(2,1)S(1)}, f32[384,512]{1,0:T(8,128)S(1)}) fusion(f16[384,512]{1,0:T(8,128)(2,1)} %collective-permute-done.7, f16[384,512]{1,0:T(8,128)(2,1)} %collective-permute-done.6, f32[384,512]{1,0:T(8,128)S(1)} %get-tuple-element.53, f16[384,512]{1,0:T(8,128)(2,1)} %collective-permute-done.5), kind=kLoop, calls=%fused_computation.20 | loop fusion | flops 1376256 | bytes 3145728 | tf_op jit(solution)/shard_map/convert_element_type | solution.py:283
  57.5 1.6 %collective-permute-start.8 = (f16[384,512]{1,0:T(8,128)(2,1)S(1)}, f16[384,512]{1,0:T(8,128)(2,1)}, u32[]{:S(2)}, u32[]{:S(2)}) collective-permute-start(f16[384,512]{1,0:T(8,128)(2,1)S(1)} %get-tuple-element.64), channel_id=1, source_target_pairs={{0,128},{128,0},{1,129},{129,1},{2,130},{130,2},{3,131},{131,3},{4... | collective-permute-start | bytes 1179656 | tf_op jit(solution)/shard_map/ppermute | solution.py:222
  60.3 10.9 %all-to-all-done.1.parts = bf16[8,48,768]{2,1,0:T(8,128)(2,1)S(1)} async-done(((bf16[8,48,768]{2,1,0:T(8,128)(2,1)}), bf16[8,48,768]{2,1,0:T(8,128)(2,1)S(1)}, u32[]{:S(2)}, u32[]{:S(2)}) %all-to-all-start.1) | async-done | bytes 589856 | tf_op jit(solution)/shard_map/all_to_all | solution.py:31
  72.8 3.5 %all-to-all-start.2 = ((bf16[8,48,768]{2,1,0:T(8,128)(2,1)}), bf16[8,48,768]{2,1,0:T(8,128)(2,1)S(1)}, u32[]{:S(2)}, u32[]{:S(2)}) async-start(bf16[8,48,768]{2,1,0:T(8,128)(2,1)} %add_copies.1), calls=%async_computation.2 | async-start | bytes 1179648 | tf_op jit(solution)/shard_map/all_to_all | solution.py:31
  77.5 2.4 %collective-permute-start.10 = (f16[384,512]{1,0:T(8,128)(2,1)S(1)}, f16[384,512]{1,0:T(8,128)(2,1)S(1)}, u32[]{:S(2)}, u32[]{:S(2)}) collective-permute-start(f16[384,512]{1,0:T(8,128)(2,1)S(1)} %get-tuple-element.66), channel_id=1, source_target_pairs={{0,64},{32,96},{64,0},{96,32},{1,65},{33,97},{65,1},{97,33},{2,66}... | collective-permute-start | bytes 1179656 | tf_op jit(solution)/shard_map/ppermute | solution.py:225
  82.6 13.1 %all-to-all-done.2.whole = bf16[8,48,768]{2,1,0:T(8,128)(2,1)S(1)} async-done(((bf16[8,48,768]{2,1,0:T(8,128)(2,1)}), bf16[8,48,768]{2,1,0:T(8,128)(2,1)S(1)}, u32[]{:S(2)}, u32[]{:S(2)}) %all-to-all-start.2) | async-done | bytes 589856 | tf_op jit(solution)/shard_map/all_to_all | solution.py:31
  99.4 5.2 %collective-permute-done.14.refs_4_ = bf16[4,48,768]{2,1,0:T(8,128)(2,1)S(1)} collective-permute-done((bf16[4,48,768]{2,1,0:T(8,128)(2,1)S(1)}, bf16[4,48,768]{2,1,0:T(8,128)(2,1)S(1)}, u32[]{:S(2)}, u32[]{:S(2)}) %collective-permute-start.14) | collective-permute-done | bytes 294944 | tf_op jit(solution)/shard_map/ppermute | solution.py:222
  104.6 2.3 %collective-permute-start.16 = (bf16[4,48,768]{2,1,0:T(8,128)(2,1)S(1)}, bf16[4,48,768]{2,1,0:T(8,128)(2,1)S(1)}, u32[]{:S(2)}, u32[]{:S(2)}) collective-permute-start(bf16[4,48,768]{2,1,0:T(8,128)(2,1)S(1)} %collective-permute-done.14.refs_4_), channel_id=1, source_target_pairs={{0,1},{1,0},{2,3},{3,2},{4,5},{5,4},{6,7},{7,6},{8,9},{9,8},{10,11... | collective-permute-start | bytes 884744 | tf_op jit(solution)/shard_map/ppermute | solution.py:222
  106.8 4.1 %collective-permute-done.15.refs_5_ = bf16[4,48,768]{2,1,0:T(8,128)(2,1)S(1)} collective-permute-done((bf16[4,48,768]{2,1,0:T(8,128)(2,1)S(1)}, bf16[4,48,768]{2,1,0:T(8,128)(2,1)S(1)}, u32[]{:S(2)}, u32[]{:S(2)}) %collective-permute-start.15) | collective-permute-done | bytes 294944 | tf_op jit(solution)/shard_map/ppermute | solution.py:222
  110.9 1.3 %collective-permute-start.17 = (bf16[4,48,768]{2,1,0:T(8,128)(2,1)S(1)}, bf16[4,48,768]{2,1,0:T(8,128)(2,1)S(1)}, u32[]{:S(2)}, u32[]{:S(2)}) collective-permute-start(bf16[4,48,768]{2,1,0:T(8,128)(2,1)S(1)} %collective-permute-done.15.refs_5_), channel_id=1, source_target_pairs={{0,1},{1,0},{2,3},{3,2},{4,5},{5,4},{6,7},{7,6},{8,9},{9,8},{10,11... | collective-permute-start | bytes 884744 | tf_op jit(solution)/shard_map/ppermute | solution.py:222
  114.7 3.3 %combine.1 = (f32[384,256]{1,0:T(8,128)}, f32[384,256]{1,0:T(8,128)}) custom-call(s32[2]{0:T(128)S(1)} %copy-done.8, f32[32,8,256]{2,1,0:T(8,128)S(1)} %all-to-all-done.sums, f32[384,256]{1,0:T(8,128)S(1)} %copy-done.3, f32[384,256]{1,0:T(8,128)S(1)} %copy-done.4, bf16[4,48,768]{2,1,0:T(8,128)(2,1)S(1)} %get-tuple-element.59.refs_0_, ...), custom_call_target="tpu_custom_call" | custom-call | flops 1207959552 | bytes 8388608 | tf_op jit(solution)/shard_map/combine/pallas_call | solution.py:327
  (62 shorter events, 24.1 us)
Async XLA Ops:
  2.5 13.3 %copy-start = (bf16[1536,256]{1,0:T(8,128)(2,1)S(1)}, bf16[1536,256]{1,0:T(8,128)(2,1)}, u32[]{:S(2)}) copy-start(bf16[1536,256]{1,0:T(8,128)(2,1)} %w0.1) | copy-start | bytes 2359300
  2.5 21.9 %collective-permute-start = (bf16[1024,256]{1,0:T(8,128)(2,1)}, bf16[1024,256]{1,0:T(8,128)(2,1)S(1)}, u32[]{:S(2)}, u32[]{:S(2)}) collective-permute-start(bf16[1024,256]{1,0:T(8,128)(2,1)} %slice.13), channel_id=1, source_target_pairs={{0,2},{2,0},{1,3},{3,1},{4,6},{6,4},{5,7},{7,5},{8,10},{10,8},{9,1... | collective-permute-start | bytes 1572872 | tf_op jit(solution)/shard_map/ppermute | solution.py:222
  4.5 34.1 %collective-permute-start.1 = (bf16[1536,256]{1,0:T(8,128)(2,1)}, bf16[1536,256]{1,0:T(8,128)(2,1)S(1)}, u32[]{:S(2)}, u32[]{:S(2)}) collective-permute-start(bf16[1536,256]{1,0:T(8,128)(2,1)} %w0.1), channel_id=1, source_target_pairs={{0,1},{1,0},{2,3},{3,2},{4,5},{5,4},{6,7},{7,6},{8,9},{9,8},{10,11... | collective-permute-start | bytes 2359304 | tf_op jit(solution)/shard_map/ppermute | solution.py:222
  9.1 15.2 %all-to-all-start = ((f32[32,8,256]{2,1,0:T(8,128)}), f32[32,8,256]{2,1,0:T(8,128)S(1)}, u32[]{:S(2)}, u32[]{:S(2)}) async-start(f32[32,8,256]{2,1,0:T(8,128)} %get-tuple-element.33), calls=%async_computation | async-start | bytes 524288 | tf_op jit(solution)/shard_map/all_to_all | solution.py:31
  15.8 9.4 %copy-start.3 = (f32[384,256]{1,0:T(8,128)S(1)}, f32[384,256]{1,0:T(8,128)}, u32[]{:S(2)}) copy-start(f32[384,256]{1,0:T(8,128)} %get-tuple-element.41.pa) | copy-start | bytes 1179652
  15.8 9.4 %copy-start.4 = (f32[384,256]{1,0:T(8,128)S(1)}, f32[384,256]{1,0:T(8,128)}, u32[]{:S(2)}) copy-start(f32[384,256]{1,0:T(8,128)} %get-tuple-element.42.pb) | copy-start | bytes 1179652
  24.4 12.9 %collective-permute-start.2 = (bf16[512,256]{1,0:T(8,128)(2,1)}, bf16[512,256]{1,0:T(8,128)(2,1)S(1)}, u32[]{:S(2)}, u32[]{:S(2)}) collective-permute-start(bf16[512,256]{1,0:T(8,128)(2,1)} %slice.12), channel_id=1, source_target_pairs={{0,2},{2,0},{1,3},{3,1},{4,6},{6,4},{5,7},{7,5},{8,10},{10,8},{9,1... | collective-permute-start | bytes 786440 | tf_op jit(solution)/shard_map/ppermute | solution.py:222
  32.2 7.2 %collective-permute-start.3 = (bf16[1024,256]{1,0:T(8,128)(2,1)S(1)}, bf16[1024,256]{1,0:T(8,128)(2,1)S(1)}, u32[]{:S(2)}, u32[]{:S(2)}) collective-permute-start(bf16[1024,256]{1,0:T(8,128)(2,1)S(1)} %copy-done.7), channel_id=1, source_target_pairs={{0,1},{1,0},{2,3},{3,2},{4,5},{5,4},{6,7},{7,6},{8,9},{9,8},{10,11... | collective-permute-start | bytes 1572872 | tf_op jit(solution)/shard_map/ppermute | solution.py:222
  34.2 20.7 %collective-permute-start.5 = (f16[384,512]{1,0:T(8,128)(2,1)}, f16[384,512]{1,0:T(8,128)(2,1)}, u32[]{:S(2)}, u32[]{:S(2)}) collective-permute-start(f16[384,512]{1,0:T(8,128)(2,1)} %convert_element_type.66), channel_id=1, source_target_pairs={{0,32},{32,64},{64,96},{96,0},{1,33},{33,65},{65,97},{97,1},{2,34}... | collective-permute-start | bytes 1179656 | tf_op jit(solution)/shard_map/ppermute | solution.py:225
  35.4 19.5 %collective-permute-start.6 = (f16[384,512]{1,0:T(8,128)(2,1)}, f16[384,512]{1,0:T(8,128)(2,1)}, u32[]{:S(2)}, u32[]{:S(2)}) collective-permute-start(f16[384,512]{1,0:T(8,128)(2,1)} %convert_element_type.68), channel_id=1, source_target_pairs={{0,64},{32,96},{64,0},{96,32},{1,65},{33,97},{65,1},{97,33},{2,66}... | collective-permute-start | bytes 1179656 | tf_op jit(solution)/shard_map/ppermute | solution.py:225
  37.3 18.7 %collective-permute-start.7 = (f16[384,512]{1,0:T(8,128)(2,1)}, f16[384,512]{1,0:T(8,128)(2,1)}, u32[]{:S(2)}, u32[]{:S(2)}) collective-permute-start(f16[384,512]{1,0:T(8,128)(2,1)} %convert_element_type.70), channel_id=1, source_target_pairs={{0,96},{32,0},{64,32},{96,64},{1,97},{33,1},{65,33},{97,65},{2,98}... | collective-permute-start | bytes 1179656 | tf_op jit(solution)/shard_map/ppermute | solution.py:225
  38.6 2.0 %collective-permute-start.4 = (bf16[512,256]{1,0:T(8,128)(2,1)S(1)}, bf16[512,256]{1,0:T(8,128)(2,1)S(1)}, u32[]{:S(2)}, u32[]{:S(2)}) collective-permute-start(bf16[512,256]{1,0:T(8,128)(2,1)S(1)} %collective-permute-done.2.w2b), channel_id=1, source_target_pairs={{0,1},{1,0},{2,3},{3,2},{4,5},{5,4},{6,7},{7,6},{8,9},{9,8},{10,11... | collective-permute-start | bytes 786440 | tf_op jit(solution)/shard_map/ppermute | solution.py:222
  43.7 27.5 %all-to-all-start.1 = ((bf16[8,48,768]{2,1,0:T(8,128)(2,1)}), bf16[8,48,768]{2,1,0:T(8,128)(2,1)S(1)}, u32[]{:S(2)}, u32[]{:S(2)}) async-start(bf16[8,48,768]{2,1,0:T(8,128)(2,1)} %embed.1), calls=%async_computation.1 | async-start | bytes 1179648 | tf_op jit(solution)/shard_map/all_to_all | solution.py:31
  57.5 18.9 %collective-permute-start.8 = (f16[384,512]{1,0:T(8,128)(2,1)S(1)}, f16[384,512]{1,0:T(8,128)(2,1)}, u32[]{:S(2)}, u32[]{:S(2)}) collective-permute-start(f16[384,512]{1,0:T(8,128)(2,1)S(1)} %get-tuple-element.64), channel_id=1, source_target_pairs={{0,128},{128,0},{1,129},{129,1},{2,130},{130,2},{3,131},{131,3},{4... | collective-permute-start | bytes 1179656 | tf_op jit(solution)/shard_map/ppermute | solution.py:222
  72.8 22.9 %all-to-all-start.2 = ((bf16[8,48,768]{2,1,0:T(8,128)(2,1)}), bf16[8,48,768]{2,1,0:T(8,128)(2,1)S(1)}, u32[]{:S(2)}, u32[]{:S(2)}) async-start(bf16[8,48,768]{2,1,0:T(8,128)(2,1)} %add_copies.1), calls=%async_computation.2 | async-start | bytes 1179648 | tf_op jit(solution)/shard_map/all_to_all | solution.py:31
  77.5 20.6 %collective-permute-start.10 = (f16[384,512]{1,0:T(8,128)(2,1)S(1)}, f16[384,512]{1,0:T(8,128)(2,1)S(1)}, u32[]{:S(2)}, u32[]{:S(2)}) collective-permute-start(f16[384,512]{1,0:T(8,128)(2,1)S(1)} %get-tuple-element.66), channel_id=1, source_target_pairs={{0,64},{32,96},{64,0},{96,32},{1,65},{33,97},{65,1},{97,33},{2,66}... | collective-permute-start | bytes 1179656 | tf_op jit(solution)/shard_map/ppermute | solution.py:225
  80.0 18.1 %collective-permute-start.11 = (f16[384,512]{1,0:T(8,128)(2,1)S(1)}, f16[384,512]{1,0:T(8,128)(2,1)}, u32[]{:S(2)}, u32[]{:S(2)}) collective-permute-start(f16[384,512]{1,0:T(8,128)(2,1)S(1)} %get-tuple-element.66), channel_id=1, source_target_pairs={{0,96},{32,0},{64,32},{96,64},{1,97},{33,1},{65,33},{97,65},{2,98}... | collective-permute-start | bytes 1179656 | tf_op jit(solution)/shard_map/ppermute | solution.py:225
  80.4 18.3 %collective-permute-start.9 = (f16[384,512]{1,0:T(8,128)(2,1)S(1)}, f16[384,512]{1,0:T(8,128)(2,1)}, u32[]{:S(2)}, u32[]{:S(2)}) collective-permute-start(f16[384,512]{1,0:T(8,128)(2,1)S(1)} %get-tuple-element.66), channel_id=1, source_target_pairs={{0,32},{32,64},{64,96},{96,0},{1,33},{33,65},{65,97},{97,1},{2,34}... | collective-permute-start | bytes 1179656 | tf_op jit(solution)/shard_map/ppermute | solution.py:225
  96.4 8.2 %collective-permute-start.14 = (bf16[4,48,768]{2,1,0:T(8,128)(2,1)S(1)}, bf16[4,48,768]{2,1,0:T(8,128)(2,1)S(1)}, u32[]{:S(2)}, u32[]{:S(2)}) collective-permute-start(bf16[4,48,768]{2,1,0:T(8,128)(2,1)S(1)} %get-tuple-element.59.refs_0_), channel_id=1, source_target_pairs={{0,2},{2,0},{1,3},{3,1},{4,6},{6,4},{5,7},{7,5},{8,10},{10,8},{9,1... | collective-permute-start | bytes 884744 | tf_op jit(solution)/shard_map/ppermute | solution.py:222
  97.4 13.5 %collective-permute-start.15 = (bf16[4,48,768]{2,1,0:T(8,128)(2,1)S(1)}, bf16[4,48,768]{2,1,0:T(8,128)(2,1)S(1)}, u32[]{:S(2)}, u32[]{:S(2)}) collective-permute-start(bf16[4,48,768]{2,1,0:T(8,128)(2,1)S(1)} %get-tuple-element.60.refs_1_), channel_id=1, source_target_pairs={{0,2},{2,0},{1,3},{3,1},{4,6},{6,4},{5,7},{7,5},{8,10},{10,8},{9,1... | collective-permute-start | bytes 884744 | tf_op jit(solution)/shard_map/ppermute | solution.py:222
  98.7 16.0 %collective-permute-start.12 = (bf16[4,48,768]{2,1,0:T(8,128)(2,1)S(1)}, bf16[4,48,768]{2,1,0:T(8,128)(2,1)S(1)}, u32[]{:S(2)}, u32[]{:S(2)}) collective-permute-start(bf16[4,48,768]{2,1,0:T(8,128)(2,1)S(1)} %get-tuple-element.59.refs_0_), channel_id=1, source_target_pairs={{0,1},{1,0},{2,3},{3,2},{4,5},{5,4},{6,7},{7,6},{8,9},{9,8},{10,11... | collective-permute-start | bytes 884744 | tf_op jit(solution)/shard_map/ppermute | solution.py:222
  99.3 15.4 %collective-permute-start.13 = (bf16[4,48,768]{2,1,0:T(8,128)(2,1)S(1)}, bf16[4,48,768]{2,1,0:T(8,128)(2,1)S(1)}, u32[]{:S(2)}, u32[]{:S(2)}) collective-permute-start(bf16[4,48,768]{2,1,0:T(8,128)(2,1)S(1)} %get-tuple-element.60.refs_1_), channel_id=1, source_target_pairs={{0,1},{1,0},{2,3},{3,2},{4,5},{5,4},{6,7},{7,6},{8,9},{9,8},{10,11... | collective-permute-start | bytes 884744 | tf_op jit(solution)/shard_map/ppermute | solution.py:222
  104.6 10.1 %collective-permute-start.16 = (bf16[4,48,768]{2,1,0:T(8,128)(2,1)S(1)}, bf16[4,48,768]{2,1,0:T(8,128)(2,1)S(1)}, u32[]{:S(2)}, u32[]{:S(2)}) collective-permute-start(bf16[4,48,768]{2,1,0:T(8,128)(2,1)S(1)} %collective-permute-done.14.refs_4_), channel_id=1, source_target_pairs={{0,1},{1,0},{2,3},{3,2},{4,5},{5,4},{6,7},{7,6},{8,9},{9,8},{10,11... | collective-permute-start | bytes 884744 | tf_op jit(solution)/shard_map/ppermute | solution.py:222
  110.9 3.8 %collective-permute-start.17 = (bf16[4,48,768]{2,1,0:T(8,128)(2,1)S(1)}, bf16[4,48,768]{2,1,0:T(8,128)(2,1)S(1)}, u32[]{:S(2)}, u32[]{:S(2)}) collective-permute-start(bf16[4,48,768]{2,1,0:T(8,128)(2,1)S(1)} %collective-permute-done.15.refs_5_), channel_id=1, source_target_pairs={{0,1},{1,0},{2,3},{3,2},{4,5},{5,4},{6,7},{7,6},{8,9},{9,8},{10,11... | collective-permute-start | bytes 884744 | tf_op jit(solution)/shard_map/ppermute | solution.py:222
  (8 other events, 25.6 us)

commit v5 on v4

--- a/solution.py
+++ b/solution.py
@@ -132,7 +132,7 @@
         out[...] = jnp.concatenate([v, centre, jnp.zeros((112, DEPTH), bf16)], axis=0).T
 
 
-def correlate(place, sums, pa, pb, ta, tb, u0, u1, u2, u3, xs, xpa, xpb, xa, xb, sem):
+def correlate(place, sums, pa, pb, ta, tb, u0, u1, u2, u3, xs, xpa, xpb, xa, xb, x0, x1, x2, x3, sem, out_sem):
     q, yy = place[0], place[1]
     stats = [
         pltpu.make_async_copy(src, dst, sem.at[8 + i])
@@ -161,11 +161,17 @@
         excess = jnp.concatenate([excess, jnp.zeros((15, BLOCK), f32)], axis=0).astype(bf16)
         ns.append(jnp.concatenate([rounded, excess, jnp.zeros((112, BLOCK), bf16)], axis=0))
     scale = U_SCALE / TOTAL
-    for s, u in ((1, u1), (2, u2), (3, u3), (0, u0)):
+    done = []
+    for s, x, u in ((1, x1, u1), (2, x2, u2), (3, x3, u3), (0, x0, u0)):
         for t in copies[s]:
             t.wait()
-        u[:, :BLOCK] = dot(xb[s], ns[0], 1, 0) * scale
-        u[:, BLOCK:] = dot(xa[s], ns[1], 1, 0) * scale
+        x[:, :BLOCK] = (dot(xb[s], ns[0], 1, 0) * scale).astype(x.dtype)
+        x[:, BLOCK:] = (dot(xa[s], ns[1], 1, 0) * scale).astype(x.dtype)
+        out = pltpu.make_async_copy(x, u, out_sem.at[s])
+        out.start()
+        done.append(out)
+    for t in done:
+        t.wait()
 
 
 def combine(place, sums, pa, pb, *refs):
@@ -259,7 +265,7 @@
 
     u_parts = call(
         correlate,
-        (shape((SHARE, 2 * BLOCK), f32),) * 4,
+        (shape((SHARE, 2 * BLOCK), f32),) + (shape((SHARE, 2 * BLOCK), bf16),) * 3,
         [SMEM] + [ANY] * 5,
         4 * ROWS * DEPTH * BLOCK,
         6 * 2**20,
@@ -269,16 +275,21 @@
             pltpu.VMEM((ROWS, BLOCK), f32),
             pltpu.VMEM((4, SHARE, 512), bf16),
             pltpu.VMEM((4, SHARE, 512), bf16),
+            pltpu.VMEM((SHARE, 2 * BLOCK), f32),
+            pltpu.VMEM((SHARE, 2 * BLOCK), bf16),
+            pltpu.VMEM((SHARE, 2 * BLOCK), bf16),
+            pltpu.VMEM((SHARE, 2 * BLOCK), bf16),
             sems((11,)),
+            sems((4,)),
         ],
+        out_specs=(ANY,) * 4,
         name="correlate",
-        vmem=20,
     )(place, sums, pa, pb, ta, tb)
     *u_parts, w_x = lax.optimization_barrier((*u_parts, w_x))
     w_xc = swap(w_x, "c")
     u = u_parts[0]
     for s in (1, 2, 3):
-        u = u + along_y(u_parts[s].astype(f16), s).astype(f32)
+        u = u + along_y(u_parts[s], s).astype(f32)
     u_near = arrival(u[:8, :128], 8)
     u = u.astype(f16)
     u = u.astype(f32) + swap(u, "xh").astype(f32)
@@ -322,6 +333,7 @@
         high = lax.reduce_precision(t, 8, 7)
         split += [high.astype(bf16), (t - high).astype(bf16)]
     y1 = [swap(t, "c") for t in y0]
+    y2[1], *split = lax.optimization_barrier((y2[1], *split))
     y3 = [swap(t, "c") for t in y2]
 
     return call(

time: 119 us -> 113 us (0.950)
  other arithmetic: 8.18 us -> 4.67 us
  local copies, waits for them, and re-layouts: 8.51 us -> 5.71 us
    convert_element_type x3 -> x0, other arithmetic: 2.41 us -> none  [local(): u = u + along_y(u_parts[s].astype(f16), s).astype(f32)]
    unnamed x22, local copies, waits for them, and re-layouts: 4.71 us -> 2.73 us
    all_to_all x3, waiting for transfers between devices: 27.3 us -> 28.6 us  [exchange(): return lax.all_to_all(blocks, axes, split_axis=0, concat_axis=0, tiled=True)]
  transfers between devices with their start and end apart: 21 -> 21, of which waited for: 9 -> 9; matrix products, arithmetic and copies ran while one was open for 9% -> 6% of each run, Pallas kernels for 14% -> 15%
where the time goes in v5:
time: 113 us; the launch traced here: 112 us
  waiting for transfers between devices  41.6 us (37%)
  starting transfers between devices  38.9 us (34%)
  Pallas kernels  20.7 us (18%)
  local copies, waits for them, and re-layouts  5.71 us (5%)
  other arithmetic  4.67 us (4%)
    all_to_all x3, waiting for transfers between devices, exchange(): return lax.all_to_all(blocks, axes, split_axis=0, concat_axis=0, tiled=True)  28.6 us
    all_to_all x3, starting transfers between devices, exchange(): return lax.all_to_all(blocks, axes, split_axis=0, concat_axis=0, tiled=True)  18.4 us
    ppermute x12, starting transfers between devices, swap(): return lax.ppermute(t, axis, SWAP)  13.8 us
    ppermute x12, waiting for transfers between devices, swap(): return lax.ppermute(t, axis, SWAP)  9.37 us
    ppermute x6, starting transfers between devices, along_y(): return lax.ppermute(t, 'y', [(i, (i + s) % 4) for i in range(4)])  6.69 us
    pallas_call x1, Pallas kernels, local(): call(correlate, (shape((SHARE, 2 * BLOCK), f32),) + (shape((SHARE, 2 * BL...  4.71 us
    pallas_call x1, Pallas kernels, local(): call(turn, (shape((DEPTH, 512), bf16),) * 2 + (shape((2 * QUARTER, DEPTH)...  3.96 us
    ppermute x6, waiting for transfers between devices, along_y(): return lax.ppermute(t, 'y', [(i, (i + s) % 4) for i in range(4)])  3.71 us
  transfers between devices with their start and end apart: 21, of which 9 were waited for; matrix products, arithmetic and copies ran while one was open for 6% of the time, Pallas kernels for 15%

profile of v5, /device:TPU:1, one launch (start us, length us, event | category | flops | bytes accessed | tf_op | source)
XLA Modules:
  0.0 112.4 jit_solution(3755817398721556763)
XLA Ops:
  1.7 2.1 %collective-permute-start = (bf16[1024,256]{1,0:T(8,128)(2,1)S(1)}, bf16[1024,256]{1,0:T(8,128)(2,1)S(1)}, u32[]{:S(2)}, u32[]{:S(2)}) collective-permute-start(bf16[1024,256]{1,0:T(8,128)(2,1)S(1)} %slice.13), channel_id=1, source_target_pairs={{0,2},{2,0},{1,3},{3,1},{4,6},{6,4},{5,7},{7,5},{8,10},{10,8},{9,1... | collective-permute-start | bytes 1572872 | tf_op jit(solution)/shard_map/ppermute | solution.py:228
  3.9 1.3 %collective-permute-start.1 = (bf16[1536,256]{1,0:T(8,128)(2,1)}, bf16[1536,256]{1,0:T(8,128)(2,1)S(1)}, u32[]{:S(2)}, u32[]{:S(2)}) collective-permute-start(bf16[1536,256]{1,0:T(8,128)(2,1)} %w0.1), channel_id=1, source_target_pairs={{0,1},{1,0},{2,3},{3,2},{4,5},{5,4},{6,7},{7,6},{8,9},{9,8},{10,11... | collective-permute-start | bytes 2359304 | tf_op jit(solution)/shard_map/ppermute | solution.py:228
  5.2 3.4 %project.1 = (f32[384,256]{1,0:T(8,128)}, f32[384,256]{1,0:T(8,128)}, f32[32,8,256]{2,1,0:T(8,128)}) custom-call(bf16[384,1536]{1,0:T(8,128)(2,1)} %va.2, bf16[384,1536]{1,0:T(8,128)(2,1)} %vb.2, bf16[1536,256]{1,0:T(8,128)(2,1)} %w0.1), custom_call_target="tpu_custom_call" | custom-call | flops 603979776 | bytes 4194304 | tf_op jit(solution)/shard_map/project/pallas_call | solution.py:236
  8.5 6.6 %all-to-all-start = ((f32[32,8,256]{2,1,0:T(8,128)}), f32[32,8,256]{2,1,0:T(8,128)S(1)}, u32[]{:S(2)}, u32[]{:S(2)}) async-start(f32[32,8,256]{2,1,0:T(8,128)} %get-tuple-element.42), calls=%async_computation | async-start | bytes 524288 | tf_op jit(solution)/shard_map/all_to_all | solution.py:31
  16.5 4.0 %turn.1 = (bf16[1536,512]{1,0:T(8,128)(2,1)}, bf16[1536,512]{1,0:T(8,128)(2,1)}, bf16[192,1536]{1,0:T(8,128)(2,1)}) custom-call(s32[2]{0:T(128)} %pad_add_fusion.place, bf16[384,1536]{1,0:T(8,128)(2,1)} %va.2, bf16[384,1536]{1,0:T(8,128)(2,1)} %vb.2), custom_call_target="tpu_custom_call" | custom-call | flops 10485760 | bytes 6291456 | tf_op jit(solution)/shard_map/turn/pallas_call | solution.py:252
  20.4 3.3 %all-to-all-done.sums = f32[32,8,256]{2,1,0:T(8,128)S(1)} async-done(((f32[32,8,256]{2,1,0:T(8,128)}), f32[32,8,256]{2,1,0:T(8,128)S(1)}, u32[]{:S(2)}, u32[]{:S(2)}) %all-to-all-start) | async-done | bytes 262176 | tf_op jit(solution)/shard_map/all_to_all | solution.py:31
  24.4 4.7 %correlate.1 = (f32[384,512]{1,0:T(8,128)}, bf16[384,512]{1,0:T(8,128)(2,1)}, bf16[384,512]{1,0:T(8,128)(2,1)}, bf16[384,512]{1,0:T(8,128)(2,1)}) custom-call(s32[2]{0:T(128)} %pad_add_fusion.place, f32[32,8,256]{2,1,0:T(8,128)} %copy-done.1, f32[384,256]{1,0:T(8,128)} %get-tuple-element.50.pa, f32[384,256]{1,0:T(8,128)} %get-tuple-element.51.pb, ...), custom_call_target="tpu_custom_call" | custom-call | flops 603979776 | bytes 6291456 | tf_op jit(solution)/shard_map/correlate/pallas_call | solution.py:266
  31.7 1.3 %collective-permute-start.7 = (bf16[384,512]{1,0:T(8,128)(2,1)}, bf16[384,512]{1,0:T(8,128)(2,1)}, u32[]{:S(2)}, u32[]{:S(2)}) collective-permute-start(bf16[384,512]{1,0:T(8,128)(2,1)} %get-tuple-element.65), channel_id=1, source_target_pairs={{0,96},{32,0},{64,32},{96,64},{1,97},{33,1},{65,33},{97,65},{2,98}... | collective-permute-start | bytes 1179656 | tf_op jit(solution)/shard_map/ppermute | solution.py:231
  36.0 3.2 %embed.1 = bf16[8,48,768]{2,1,0:T(8,128)(2,1)} custom-call(s32[2]{0:T(128)S(1)} %copy-done.7, f32[32,8,256]{2,1,0:T(8,128)S(1)} %copy-done.2, bf16[192,1536]{1,0:T(8,128)(2,1)S(1)} %copy-done.6, bf16[1536,256]{1,0:T(8,128)(2,1)S(1)} %copy-done, bf16[1536,256]{1,0:T(8,128)(2,1)S(1)} %collective-permute-done.1.w1, ...), custom_call_target="tpu_custom_call" | custom-call | flops 1207959552 | bytes 7340032 | tf_op jit(solution)/shard_map/embed/pallas_call | solution.py:300
  39.1 8.3 %all-to-all-start.1 = ((bf16[8,48,768]{2,1,0:T(8,128)(2,1)}), bf16[8,48,768]{2,1,0:T(8,128)(2,1)S(1)}, u32[]{:S(2)}, u32[]{:S(2)}) async-start(bf16[8,48,768]{2,1,0:T(8,128)(2,1)} %embed.1), calls=%async_computation.1 | async-start | bytes 1179648 | tf_op jit(solution)/shard_map/all_to_all | solution.py:31
  47.5 3.3 %collective-permute-done.5 = bf16[384,512]{1,0:T(8,128)(2,1)S(1)} collective-permute-done((bf16[384,512]{1,0:T(8,128)(2,1)}, bf16[384,512]{1,0:T(8,128)(2,1)S(1)}, u32[]{:S(2)}, u32[]{:S(2)}) %collective-permute-start.5) | collective-permute-done | bytes 393248 | tf_op jit(solution)/shard_map/ppermute | solution.py:231
  51.2 1.4 %fusion.5 = (f16[384,512]{1,0:T(8,128)(2,1)S(1)}, f32[384,512]{1,0:T(8,128)S(1)}) fusion(bf16[384,512]{1,0:T(8,128)(2,1)} %collective-permute-done.7, bf16[384,512]{1,0:T(8,128)(2,1)} %collective-permute-done.6, f32[384,512]{1,0:T(8,128)S(1)} %copy-done.10, bf16[384,512]{1,0:T(8,128)(2,1)S(1)} %collective-permute-done.5), kind=kLoop, calls=%fused_computation.20 | loop fusion | flops 1376256 | bytes 3145728 | tf_op jit(solution)/shard_map/convert_element_type | solution.py:294
  52.6 1.7 %collective-permute-start.8 = (f16[384,512]{1,0:T(8,128)(2,1)S(1)}, f16[384,512]{1,0:T(8,128)(2,1)S(1)}, u32[]{:S(2)}, u32[]{:S(2)}) collective-permute-start(f16[384,512]{1,0:T(8,128)(2,1)S(1)} %get-tuple-element.82), channel_id=1, source_target_pairs={{0,128},{128,0},{1,129},{129,1},{2,130},{130,2},{3,131},{131,3},{4... | collective-permute-start | bytes 1179656 | tf_op jit(solution)/shard_map/ppermute | solution.py:228
  55.4 11.4 %all-to-all-done.1.parts = bf16[8,48,768]{2,1,0:T(8,128)(2,1)S(1)} async-done(((bf16[8,48,768]{2,1,0:T(8,128)(2,1)}), bf16[8,48,768]{2,1,0:T(8,128)(2,1)S(1)}, u32[]{:S(2)}, u32[]{:S(2)}) %all-to-all-start.1) | async-done | bytes 589856 | tf_op jit(solution)/shard_map/all_to_all | solution.py:31
  68.4 3.5 %all-to-all-start.2 = ((bf16[8,48,768]{2,1,0:T(8,128)(2,1)}), bf16[8,48,768]{2,1,0:T(8,128)(2,1)S(1)}, u32[]{:S(2)}, u32[]{:S(2)}) async-start(bf16[8,48,768]{2,1,0:T(8,128)(2,1)} %add_copies.1), calls=%async_computation.2 | async-start | bytes 1179648 | tf_op jit(solution)/shard_map/all_to_all | solution.py:31
  72.1 2.4 %collective-permute-start.10 = (f16[384,512]{1,0:T(8,128)(2,1)S(1)}, f16[384,512]{1,0:T(8,128)(2,1)S(1)}, u32[]{:S(2)}, u32[]{:S(2)}) collective-permute-start(f16[384,512]{1,0:T(8,128)(2,1)S(1)} %get-tuple-element.84), channel_id=1, source_target_pairs={{0,64},{32,96},{64,0},{96,32},{1,65},{33,97},{65,1},{97,33},{2,66}... | collective-permute-start | bytes 1179656 | tf_op jit(solution)/shard_map/ppermute | solution.py:231
  77.3 13.9 %all-to-all-done.2.whole = bf16[8,48,768]{2,1,0:T(8,128)(2,1)S(1)} async-done(((bf16[8,48,768]{2,1,0:T(8,128)(2,1)}), bf16[8,48,768]{2,1,0:T(8,128)(2,1)S(1)}, u32[]{:S(2)}, u32[]{:S(2)}) %all-to-all-start.2) | async-done | bytes 589856 | tf_op jit(solution)/shard_map/all_to_all | solution.py:31
  95.9 1.3 %fusion.1 = (bf16[384,512]{1,0:T(8,128)(2,1)S(1)}, bf16[384,512]{1,0:T(8,128)(2,1)S(1)}, bf16[384,512]{1,0:T(8,128)(2,1)S(1)}, bf16[384,512]{1,0:T(8,128)(2,1)S(1)}) fusion(f16[384,512]{1,0:T(8,128)(2,1)} %collective-permute-done.9, f16[384,512]{1,0:T(8,128)(2,1)S(1)} %collective-permute-done.10), kind=kLoop, calls=%fused_computation.9 | loop fusion | flops 2359296 | bytes 2359296 | tf_op jit(solution)/shard_map/convert_element_type | solution.py:334
  97.2 2.9 %collective-permute-done.15.refs_5_ = bf16[4,48,768]{2,1,0:T(8,128)(2,1)S(1)} collective-permute-done((bf16[4,48,768]{2,1,0:T(8,128)(2,1)S(1)}, bf16[4,48,768]{2,1,0:T(8,128)(2,1)S(1)}, u32[]{:S(2)}, u32[]{:S(2)}) %collective-permute-start.15) | collective-permute-done | bytes 294944 | tf_op jit(solution)/shard_map/ppermute | solution.py:228
  100.2 2.3 %collective-permute-start.17 = (bf16[4,48,768]{2,1,0:T(8,128)(2,1)S(1)}, bf16[4,48,768]{2,1,0:T(8,128)(2,1)S(1)}, u32[]{:S(2)}, u32[]{:S(2)}) collective-permute-start(bf16[4,48,768]{2,1,0:T(8,128)(2,1)S(1)} %collective-permute-done.15.refs_5_), channel_id=1, source_target_pairs={{0,1},{1,0},{2,3},{3,2},{4,5},{5,4},{6,7},{7,6},{8,9},{9,8},{10,11... | collective-permute-start | bytes 884744 | tf_op jit(solution)/shard_map/ppermute | solution.py:228
  102.4 4.1 %collective-permute-done.14.refs_4_ = bf16[4,48,768]{2,1,0:T(8,128)(2,1)S(1)} collective-permute-done((bf16[4,48,768]{2,1,0:T(8,128)(2,1)S(1)}, bf16[4,48,768]{2,1,0:T(8,128)(2,1)S(1)}, u32[]{:S(2)}, u32[]{:S(2)}) %collective-permute-start.14) | collective-permute-done | bytes 294944 | tf_op jit(solution)/shard_map/ppermute | solution.py:228
  106.5 1.3 %collective-permute-start.16 = (bf16[4,48,768]{2,1,0:T(8,128)(2,1)S(1)}, bf16[4,48,768]{2,1,0:T(8,128)(2,1)S(1)}, u32[]{:S(2)}, u32[]{:S(2)}) collective-permute-start(bf16[4,48,768]{2,1,0:T(8,128)(2,1)S(1)} %collective-permute-done.14.refs_4_), channel_id=1, source_target_pairs={{0,1},{1,0},{2,3},{3,2},{4,5},{5,4},{6,7},{7,6},{8,9},{9,8},{10,11... | collective-permute-start | bytes 884744 | tf_op jit(solution)/shard_map/ppermute | solution.py:228
  107.8 1.2 %collective-permute-done.16.refs_6_ = bf16[4,48,768]{2,1,0:T(8,128)(2,1)S(1)} collective-permute-done((bf16[4,48,768]{2,1,0:T(8,128)(2,1)S(1)}, bf16[4,48,768]{2,1,0:T(8,128)(2,1)S(1)}, u32[]{:S(2)}, u32[]{:S(2)}) %collective-permute-start.16) | collective-permute-done | bytes 294944 | tf_op jit(solution)/shard_map/ppermute | solution.py:228
  109.0 3.3 %combine.1 = (f32[384,256]{1,0:T(8,128)}, f32[384,256]{1,0:T(8,128)}) custom-call(s32[2]{0:T(128)S(1)} %copy-done.7, f32[32,8,256]{2,1,0:T(8,128)S(1)} %copy-done.3, f32[384,256]{1,0:T(8,128)S(1)} %copy-done.4, f32[384,256]{1,0:T(8,128)S(1)} %copy-done.5, bf16[4,48,768]{2,1,0:T(8,128)(2,1)S(1)} %get-tuple-element.68.refs_0_, ...), custom_call_target="tpu_custom_call" | custom-call | flops 1207959552 | bytes 8388608 | tf_op jit(solution)/shard_map/combine/pallas_call | solution.py:339
  (59 shorter events, 19.5 us)
Async XLA Ops:
  1.7 22.0 %collective-permute-start = (bf16[1024,256]{1,0:T(8,128)(2,1)S(1)}, bf16[1024,256]{1,0:T(8,128)(2,1)S(1)}, u32[]{:S(2)}, u32[]{:S(2)}) collective-permute-start(bf16[1024,256]{1,0:T(8,128)(2,1)S(1)} %slice.13), channel_id=1, source_target_pairs={{0,2},{2,0},{1,3},{3,1},{4,6},{6,4},{5,7},{7,5},{8,10},{10,8},{9,1... | collective-permute-start | bytes 1572872 | tf_op jit(solution)/shard_map/ppermute | solution.py:228
  3.9 29.2 %collective-permute-start.1 = (bf16[1536,256]{1,0:T(8,128)(2,1)}, bf16[1536,256]{1,0:T(8,128)(2,1)S(1)}, u32[]{:S(2)}, u32[]{:S(2)}) collective-permute-start(bf16[1536,256]{1,0:T(8,128)(2,1)} %w0.1), channel_id=1, source_target_pairs={{0,1},{1,0},{2,3},{3,2},{4,5},{5,4},{6,7},{7,6},{8,9},{9,8},{10,11... | collective-permute-start | bytes 2359304 | tf_op jit(solution)/shard_map/ppermute | solution.py:228
  8.5 15.1 %all-to-all-start = ((f32[32,8,256]{2,1,0:T(8,128)}), f32[32,8,256]{2,1,0:T(8,128)S(1)}, u32[]{:S(2)}, u32[]{:S(2)}) async-start(f32[32,8,256]{2,1,0:T(8,128)} %get-tuple-element.42), calls=%async_computation | async-start | bytes 524288 | tf_op jit(solution)/shard_map/all_to_all | solution.py:31
  23.7 8.1 %collective-permute-start.2 = (bf16[512,256]{1,0:T(8,128)(2,1)}, bf16[512,256]{1,0:T(8,128)(2,1)S(1)}, u32[]{:S(2)}, u32[]{:S(2)}) collective-permute-start(bf16[512,256]{1,0:T(8,128)(2,1)} %slice.12), channel_id=1, source_target_pairs={{0,2},{2,0},{1,3},{3,1},{4,6},{6,4},{5,7},{7,5},{8,10},{10,8},{9,1... | collective-permute-start | bytes 786440 | tf_op jit(solution)/shard_map/ppermute | solution.py:228
  29.1 4.8 %collective-permute-start.3 = (bf16[1024,256]{1,0:T(8,128)(2,1)S(1)}, bf16[1024,256]{1,0:T(8,128)(2,1)S(1)}, u32[]{:S(2)}, u32[]{:S(2)}) collective-permute-start(bf16[1024,256]{1,0:T(8,128)(2,1)S(1)} %collective-permute-done.w2), channel_id=1, source_target_pairs={{0,1},{1,0},{2,3},{3,2},{4,5},{5,4},{6,7},{7,6},{8,9},{9,8},{10,11... | collective-permute-start | bytes 1572872 | tf_op jit(solution)/shard_map/ppermute | solution.py:228
  30.2 20.5 %collective-permute-start.5 = (bf16[384,512]{1,0:T(8,128)(2,1)}, bf16[384,512]{1,0:T(8,128)(2,1)S(1)}, u32[]{:S(2)}, u32[]{:S(2)}) collective-permute-start(bf16[384,512]{1,0:T(8,128)(2,1)} %get-tuple-element.63), channel_id=1, source_target_pairs={{0,32},{32,64},{64,96},{96,0},{1,33},{33,65},{65,97},{97,1},{2,34}... | collective-permute-start | bytes 1179656 | tf_op jit(solution)/shard_map/ppermute | solution.py:231
  30.6 20.1 %collective-permute-start.6 = (bf16[384,512]{1,0:T(8,128)(2,1)}, bf16[384,512]{1,0:T(8,128)(2,1)}, u32[]{:S(2)}, u32[]{:S(2)}) collective-permute-start(bf16[384,512]{1,0:T(8,128)(2,1)} %get-tuple-element.64), channel_id=1, source_target_pairs={{0,64},{32,96},{64,0},{96,32},{1,65},{33,97},{65,1},{97,33},{2,66}... | collective-permute-start | bytes 1179656 | tf_op jit(solution)/shard_map/ppermute | solution.py:231
  31.7 19.4 %collective-permute-start.7 = (bf16[384,512]{1,0:T(8,128)(2,1)}, bf16[384,512]{1,0:T(8,128)(2,1)}, u32[]{:S(2)}, u32[]{:S(2)}) collective-permute-start(bf16[384,512]{1,0:T(8,128)(2,1)} %get-tuple-element.65), channel_id=1, source_target_pairs={{0,96},{32,0},{64,32},{96,64},{1,97},{33,1},{65,33},{97,65},{2,98}... | collective-permute-start | bytes 1179656 | tf_op jit(solution)/shard_map/ppermute | solution.py:231
  33.0 2.0 %collective-permute-start.4 = (bf16[512,256]{1,0:T(8,128)(2,1)S(1)}, bf16[512,256]{1,0:T(8,128)(2,1)S(1)}, u32[]{:S(2)}, u32[]{:S(2)}) collective-permute-start(bf16[512,256]{1,0:T(8,128)(2,1)S(1)} %collective-permute-done.2.w2b), channel_id=1, source_target_pairs={{0,1},{1,0},{2,3},{3,2},{4,5},{5,4},{6,7},{7,6},{8,9},{9,8},{10,11... | collective-permute-start | bytes 786440 | tf_op jit(solution)/shard_map/ppermute | solution.py:228
  39.1 27.7 %all-to-all-start.1 = ((bf16[8,48,768]{2,1,0:T(8,128)(2,1)}), bf16[8,48,768]{2,1,0:T(8,128)(2,1)S(1)}, u32[]{:S(2)}, u32[]{:S(2)}) async-start(bf16[8,48,768]{2,1,0:T(8,128)(2,1)} %embed.1), calls=%async_computation.1 | async-start | bytes 1179648 | tf_op jit(solution)/shard_map/all_to_all | solution.py:31
  52.6 19.4 %collective-permute-start.8 = (f16[384,512]{1,0:T(8,128)(2,1)S(1)}, f16[384,512]{1,0:T(8,128)(2,1)S(1)}, u32[]{:S(2)}, u32[]{:S(2)}) collective-permute-start(f16[384,512]{1,0:T(8,128)(2,1)S(1)} %get-tuple-element.82), channel_id=1, source_target_pairs={{0,128},{128,0},{1,129},{129,1},{2,130},{130,2},{3,131},{131,3},{4... | collective-permute-start | bytes 1179656 | tf_op jit(solution)/shard_map/ppermute | solution.py:228
  68.4 22.9 %all-to-all-start.2 = ((bf16[8,48,768]{2,1,0:T(8,128)(2,1)}), bf16[8,48,768]{2,1,0:T(8,128)(2,1)S(1)}, u32[]{:S(2)}, u32[]{:S(2)}) async-start(bf16[8,48,768]{2,1,0:T(8,128)(2,1)} %add_copies.1), calls=%async_computation.2 | async-start | bytes 1179648 | tf_op jit(solution)/shard_map/all_to_all | solution.py:31
  72.1 21.4 %collective-permute-start.10 = (f16[384,512]{1,0:T(8,128)(2,1)S(1)}, f16[384,512]{1,0:T(8,128)(2,1)S(1)}, u32[]{:S(2)}, u32[]{:S(2)}) collective-permute-start(f16[384,512]{1,0:T(8,128)(2,1)S(1)} %get-tuple-element.84), channel_id=1, source_target_pairs={{0,64},{32,96},{64,0},{96,32},{1,65},{33,97},{65,1},{97,33},{2,66}... | collective-permute-start | bytes 1179656 | tf_op jit(solution)/shard_map/ppermute | solution.py:231
  74.5 19.0 %collective-permute-start.11 = (f16[384,512]{1,0:T(8,128)(2,1)S(1)}, f16[384,512]{1,0:T(8,128)(2,1)}, u32[]{:S(2)}, u32[]{:S(2)}) collective-permute-start(f16[384,512]{1,0:T(8,128)(2,1)S(1)} %get-tuple-element.84), channel_id=1, source_target_pairs={{0,96},{32,0},{64,32},{96,64},{1,97},{33,1},{65,33},{97,65},{2,98}... | collective-permute-start | bytes 1179656 | tf_op jit(solution)/shard_map/ppermute | solution.py:231
  75.1 18.5 %collective-permute-start.9 = (f16[384,512]{1,0:T(8,128)(2,1)S(1)}, f16[384,512]{1,0:T(8,128)(2,1)}, u32[]{:S(2)}, u32[]{:S(2)}) collective-permute-start(f16[384,512]{1,0:T(8,128)(2,1)S(1)} %get-tuple-element.84), channel_id=1, source_target_pairs={{0,32},{32,64},{64,96},{96,0},{1,33},{33,65},{65,97},{97,1},{2,34}... | collective-permute-start | bytes 1179656 | tf_op jit(solution)/shard_map/ppermute | solution.py:231
  92.0 8.2 %collective-permute-start.15 = (bf16[4,48,768]{2,1,0:T(8,128)(2,1)S(1)}, bf16[4,48,768]{2,1,0:T(8,128)(2,1)S(1)}, u32[]{:S(2)}, u32[]{:S(2)}) collective-permute-start(bf16[4,48,768]{2,1,0:T(8,128)(2,1)S(1)} %get-tuple-element.69.refs_1_), channel_id=1, source_target_pairs={{0,2},{2,0},{1,3},{3,1},{4,6},{6,4},{5,7},{7,5},{8,10},{10,8},{9,1... | collective-permute-start | bytes 884744 | tf_op jit(solution)/shard_map/ppermute | solution.py:228
  93.1 16.0 %copy-start.3 = (f32[32,8,256]{2,1,0:T(8,128)S(1)}, f32[32,8,256]{2,1,0:T(8,128)}, u32[]{:S(2)}) copy-start(f32[32,8,256]{2,1,0:T(8,128)} %copy-done.1) | copy-start | bytes 786436
  93.1 16.0 %copy-start.4 = (f32[384,256]{1,0:T(8,128)S(1)}, f32[384,256]{1,0:T(8,128)}, u32[]{:S(2)}) copy-start(f32[384,256]{1,0:T(8,128)} %get-tuple-element.50.pa) | copy-start | bytes 1179652
  93.1 16.0 %copy-start.5 = (f32[384,256]{1,0:T(8,128)S(1)}, f32[384,256]{1,0:T(8,128)}, u32[]{:S(2)}) copy-start(f32[384,256]{1,0:T(8,128)} %get-tuple-element.51.pb) | copy-start | bytes 1179652
  93.1 13.4 %collective-permute-start.14 = (bf16[4,48,768]{2,1,0:T(8,128)(2,1)S(1)}, bf16[4,48,768]{2,1,0:T(8,128)(2,1)S(1)}, u32[]{:S(2)}, u32[]{:S(2)}) collective-permute-start(bf16[4,48,768]{2,1,0:T(8,128)(2,1)S(1)} %get-tuple-element.68.refs_0_), channel_id=1, source_target_pairs={{0,2},{2,0},{1,3},{3,1},{4,6},{6,4},{5,7},{7,5},{8,10},{10,8},{9,1... | collective-permute-start | bytes 884744 | tf_op jit(solution)/shard_map/ppermute | solution.py:228
  94.7 13.1 %collective-permute-start.12 = (bf16[4,48,768]{2,1,0:T(8,128)(2,1)S(1)}, bf16[4,48,768]{2,1,0:T(8,128)(2,1)S(1)}, u32[]{:S(2)}, u32[]{:S(2)}) collective-permute-start(bf16[4,48,768]{2,1,0:T(8,128)(2,1)S(1)} %get-tuple-element.68.refs_0_), channel_id=1, source_target_pairs={{0,1},{1,0},{2,3},{3,2},{4,5},{5,4},{6,7},{7,6},{8,9},{9,8},{10,11... | collective-permute-start | bytes 884744 | tf_op jit(solution)/shard_map/ppermute | solution.py:228
  95.8 12.0 %collective-permute-start.13 = (bf16[4,48,768]{2,1,0:T(8,128)(2,1)S(1)}, bf16[4,48,768]{2,1,0:T(8,128)(2,1)S(1)}, u32[]{:S(2)}, u32[]{:S(2)}) collective-permute-start(bf16[4,48,768]{2,1,0:T(8,128)(2,1)S(1)} %get-tuple-element.69.refs_1_), channel_id=1, source_target_pairs={{0,1},{1,0},{2,3},{3,2},{4,5},{5,4},{6,7},{7,6},{8,9},{9,8},{10,11... | collective-permute-start | bytes 884744 | tf_op jit(solution)/shard_map/ppermute | solution.py:228
  100.2 7.7 %collective-permute-start.17 = (bf16[4,48,768]{2,1,0:T(8,128)(2,1)S(1)}, bf16[4,48,768]{2,1,0:T(8,128)(2,1)S(1)}, u32[]{:S(2)}, u32[]{:S(2)}) collective-permute-start(bf16[4,48,768]{2,1,0:T(8,128)(2,1)S(1)} %collective-permute-done.15.refs_5_), channel_id=1, source_target_pairs={{0,1},{1,0},{2,3},{3,2},{4,5},{5,4},{6,7},{7,6},{8,9},{9,8},{10,11... | collective-permute-start | bytes 884744 | tf_op jit(solution)/shard_map/ppermute | solution.py:228
  106.5 2.5 %collective-permute-start.16 = (bf16[4,48,768]{2,1,0:T(8,128)(2,1)S(1)}, bf16[4,48,768]{2,1,0:T(8,128)(2,1)S(1)}, u32[]{:S(2)}, u32[]{:S(2)}) collective-permute-start(bf16[4,48,768]{2,1,0:T(8,128)(2,1)S(1)} %collective-permute-done.14.refs_4_), channel_id=1, source_target_pairs={{0,1},{1,0},{2,3},{3,2},{4,5},{5,4},{6,7},{7,6},{8,9},{9,8},{10,11... | collective-permute-start | bytes 884744 | tf_op jit(solution)/shard_map/ppermute | solution.py:228
  (8 other events, 49.8 us)

commit v6 on v5

--- a/solution.py
+++ b/solution.py
@@ -20,6 +20,7 @@
 BLOCK = 256
 QUARTER = ROWS // 4
 PIECE = (48, 768)
+NEAR, FAR = (0, 1, 7, 2), (6, 3, 5, 4)
 SHARE = DEPTH // 4
 EARLY = 1024
 VMEM = pl.BlockSpec(memory_space=pltpu.VMEM)
@@ -87,8 +88,9 @@
     return ma, ra, mb, rb, (t[4:5] - ma * mb) * ra * rb
 
 
-def embed(place, sums, v, w0, w1, w2, w2b, w3, w3b, y, na, nb):
-    q = place[0]
+def embed(place, sums, v, w0, w1, w2, w2b, w3, w3b, *refs):
+    ys, (na, nb, y) = refs[:8], refs[8:]
+    q, z = place[0], place[2]
     half = EARLY
     ws = ((w0,), (w1,), (w2, w2b), (w3, w3b))
     for j, wj in enumerate(ws):
@@ -112,13 +114,22 @@
         acc = acc.astype(bf16)
         for i in range(4):
             y[2 * i + k // 3, :, (k % 3) * 256 : (k % 3 + 1) * 256] = acc[48 * i : 48 * i + 48]
-
-
-def add_copies(parts, ready, out):
-    total = parts[0].astype(f32)
-    for d in range(1, 8):
-        total = total + parts[d].astype(f32)
-    out[...] = jnp.broadcast_to(total.astype(bf16)[None], out.shape)
+    for s in range(8):
+        ys[s][...] = y[(z + s) & 7]
+
+
+def add(ready, *refs):
+    parts, out = refs[:8], refs[8]
+    total = parts[0][...].astype(f32)
+    for t in parts[1:]:
+        total = total + t[...].astype(f32)
+    out[...] = total.astype(bf16)
+
+
+def join(p0, p1, p2, p3, *refs):
+    out = refs[-1]
+    for i, t in enumerate((p0, p1, p2, p3)):
+        out[i] = t[...]
 
 
 def turn(place, va, vb, ta, tb, quarter):
@@ -175,24 +186,24 @@
 
 
 def combine(place, sums, pa, pb, *refs):
-    ys, us, (out_a, out_b, ya, yb) = refs[:8], refs[8:16], refs[16:]
-    q, yy = place[0], place[1]
-    for j in range(4):
-        for i in range(4):
-            at = pl.multiple_of((q ^ j) * QUARTER + (i & 1) * 48, 16)
-            for h in range(2):
-                to = ya if i < 2 else yb
-                to[pl.ds(at, 48), h * 768 : (h + 1) * 768] = ys[2 * j + i // 2][2 * (i & 1) + h]
+    ys, us, (out_a, out_b, y) = refs[:8], refs[8:16], refs[16:]
+    q, yy, z = place[0], place[1], place[2]
+    for n, s in enumerate(NEAR + FAR):
+        piece = (z + 8 - s) & 7
+        cols = pl.ds(pl.multiple_of((piece & 1) * 768, 128), 768)
+        for j in range(4):
+            rows = pl.multiple_of((q ^ j) * QUARTER + ((piece >> 1) & 1) * 48, 16)
+            y[piece >> 2, pl.ds(rows, 48), cols] = ys[2 * j + n // 4][n % 4]
     ma, ra, mb, rb, corr = moments(sums, q)
-    for first, y, p, m, r, out in (
-        (0, yb, pb, mb, rb, out_a),
-        (BLOCK, ya, pa, ma, ra, out_b),
+    for first, view, p, m, r, out in (
+        (0, 1, pb, mb, rb, out_a),
+        (BLOCK, 0, pa, ma, ra, out_b),
     ):
         acc = (p[...] - m) * (r * (corr - 2.0))
         cols = slice(first, first + BLOCK)
         for s in range(4):
             at = pl.ds(pl.multiple_of(((yy + 4 - s) & 3) * SHARE, 128), SHARE)
-            part = y[:, at]
+            part = y[view, :, at]
             acc = acc + (dot(part, us[2 * s][:, cols], 1, 0) + dot(part, us[2 * s + 1][:, cols], 1, 0))
         out[...] = acc
 
@@ -212,20 +223,18 @@
     )(t)
 
 
-def halve(whole, ready, first, second):
-    first[...] = whole[:4]
-    second[...] = whole[4:]
-
-
 def local(va, vb, w):
     q = lax.axis_index("xl") * 2 + lax.axis_index("c")
-    place = jnp.stack([q, lax.axis_index("y")]).astype(jnp.int32)
+    place = jnp.stack([q, lax.axis_index("y"), lax.axis_index("z")]).astype(jnp.int32)
     shape = jax.ShapeDtypeStruct
     sems = pltpu.SemaphoreType.DMA
     half = EARLY
 
     def swap(t, axis):
         return lax.ppermute(t, axis, SWAP)
+
+    def along_z(t, s):
+        return lax.ppermute(t, "z", [(i, (i + s) % 8) for i in range(8)])
 
     def along_y(t, s):
         return lax.ppermute(t, "y", [(i, (i + s) % 4) for i in range(4)])
@@ -297,34 +306,40 @@
     u = lax.optimization_barrier(u.astype(f16))
     us = [u] + [along_y(u, s) for s in (1, 2, 3)]
 
-    y_part = call(
+    y_parts = call(
         embed,
-        shape((8,) + PIECE, bf16),
+        (shape(PIECE, bf16),) * 8,
         [SMEM] + [VMEM] * 8,
         16 * ROWS * DEPTH * BLOCK // 2,
         7 * 2**20,
-        [pltpu.VMEM((QUARTER, 4 * BLOCK), bf16)] * 2,
+        [pltpu.VMEM((QUARTER, 4 * BLOCK), bf16)] * 2 + [pltpu.VMEM((8,) + PIECE, bf16)],
         name="embed",
         vmem=20,
     )(place, sums, v_quarter, w, w_c, w_x, w_xb, w_xc, w_xcb)
-    y_copies = call(
-        add_copies,
-        shape((8,) + PIECE, bf16),
-        [VMEM] * 2,
+    y_own = call(
+        add,
+        shape(PIECE, bf16),
+        [ANY] + [VMEM] * 8,
         10 * 2**20,
         2**20,
-        name="add_copies",
+        name="add",
         vmem=4,
-    )(exchange(y_part, "z"), u_near)
-    y0 = call(
-        halve,
-        (shape((4,) + PIECE, bf16),) * 2,
-        [VMEM] * 2,
-        0,
-        2**20,
-        name="halve",
-        vmem=4,
-    )(exchange(y_copies, "z"), u_far)
+    )(u_near, *[along_z(y_parts[s], s) if s else y_parts[0] for s in NEAR + FAR])
+    y0 = []
+    for group in (NEAR, FAR):
+        pieces = [along_z(y_own, s) if s else y_own for s in group]
+        ready = [u_far] if group == FAR else []
+        y0.append(
+            call(
+                join,
+                shape((4,) + PIECE, bf16),
+                [VMEM] * 4 + [ANY] * len(ready),
+                0,
+                2**20,
+                name="join",
+                vmem=4,
+            )(*pieces, *ready)
+        )
     y2 = [swap(t, "xl") for t in y0]
     *y0, us[1], us[2], us[3] = lax.optimization_barrier((*y0, *us[1:]))
     split = []
@@ -342,7 +357,7 @@
         [SMEM] + [VMEM] * 19,
         8 * ROWS * DEPTH * BLOCK,
         8 * 2**20,
-        [pltpu.VMEM((ROWS, DEPTH), bf16)] * 2,
+        [pltpu.VMEM((2, ROWS, DEPTH), bf16)],
         name="combine",
         vmem=20,
     )(place, sums, pa, pb, *y0, *y1, *y2, *y3, *split)

time: 113 us -> 116 us (1.027)
  starting transfers between devices: 38.9 us -> 63.9 us
  waiting for transfers between devices: 41.6 us -> 25.2 us
  other arithmetic: 4.67 us -> 1.63 us
  Pallas kernels: 20.7 us -> 19.1 us
    ppermute x0 -> x14, starting transfers between devices: none -> 36.1 us  [along_z(): return lax.ppermute(t, 'z', [(i, (i + s) % 8) for i in range(8)])]
    all_to_all x3 -> x1, waiting for transfers between devices: 28.6 us -> 3.95 us  [exchange(): return lax.all_to_all(blocks, axes, split_axis=0, concat_axis=0, tiled=True)]
    ppermute x6, waiting for transfers between devices: 3.71 us -> 15.9 us  [along_y(): return lax.ppermute(t, 'y', [(i, (i + s) % 4) for i in range(4)])]
    all_to_all x3 -> x1, starting transfers between devices: 18.4 us -> 6.57 us  [exchange(): return lax.all_to_all(blocks, axes, split_axis=0, concat_axis=0, tiled=True)]
    ppermute x12, waiting for transfers between devices: 9.37 us -> 2.72 us  [swap(): return lax.ppermute(t, axis, SWAP)]
    ppermute x0 -> x14, waiting for transfers between devices: none -> 2.65 us  [along_z(): return lax.ppermute(t, 'z', [(i, (i + s) % 8) for i in range(8)])]
    convert_element_type x3, other arithmetic: 2.56 us -> 0.58 us  [local(): split += [high.astype(bf16), (t - high).astype(bf16)]]
    ppermute x12, starting transfers between devices: 13.8 us -> 15.7 us  [swap(): return lax.ppermute(t, axis, SWAP)]
  transfers between devices with their start and end apart: 21 -> 33, of which waited for: 9 -> 10; matrix products, arithmetic and copies ran while one was open for 6% -> 2% of each run, Pallas kernels for 15% -> 14%
where the time goes in v6:
time: 116 us
  starting transfers between devices  63.9 us (55%)
  waiting for transfers between devices  25.2 us (22%)
  Pallas kernels  19.1 us (16%)
  local copies, waits for them, and re-layouts  5.02 us (4%)
  other arithmetic  1.63 us (1%)
    ppermute x14, starting transfers between devices, along_z(): return lax.ppermute(t, 'z', [(i, (i + s) % 8) for i in range(8)])  36.1 us
    ppermute x6, waiting for transfers between devices, along_y(): return lax.ppermute(t, 'y', [(i, (i + s) % 4) for i in range(4)])  15.9 us
    ppermute x12, starting transfers between devices, swap(): return lax.ppermute(t, axis, SWAP)  15.7 us
    all_to_all x1, starting transfers between devices, exchange(): return lax.all_to_all(blocks, axes, split_axis=0, concat_axis=0, tiled=True)  6.57 us
    ppermute x6, starting transfers between devices, along_y(): return lax.ppermute(t, 'y', [(i, (i + s) % 4) for i in range(4)])  5.55 us
    pallas_call x1, Pallas kernels, local(): call(correlate, (shape((SHARE, 2 * BLOCK), f32),) + (shape((SHARE, 2 * BL...  4.73 us
    all_to_all x1, waiting for transfers between devices, exchange(): return lax.all_to_all(blocks, axes, split_axis=0, concat_axis=0, tiled=True)  3.95 us
    pallas_call x1, Pallas kernels, local(): call(turn, (shape((DEPTH, 512), bf16),) * 2 + (shape((2 * QUARTER, DEPTH)...  3.91 us
  transfers between devices with their start and end apart: 33, of which 10 were waited for; matrix products, arithmetic and copies ran while one was open for 2% of the time, Pallas kernels for 14%

profile of v6, /device:TPU:1, one launch (start us, length us, event | category | flops | bytes accessed | tf_op | source)
XLA Modules:
  0.0 115.7 jit_solution(9635541962093466386)
XLA Ops:
  1.7 2.1 %collective-permute-start = (bf16[1024,256]{1,0:T(8,128)(2,1)S(1)}, bf16[1024,256]{1,0:T(8,128)(2,1)S(1)}, u32[]{:S(2)}, u32[]{:S(2)}) collective-permute-start(bf16[1024,256]{1,0:T(8,128)(2,1)S(1)} %slice.13), channel_id=1, source_target_pairs={{0,2},{2,0},{1,3},{3,1},{4,6},{6,4},{5,7},{7,5},{8,10},{10,8},{9,1... | collective-permute-start | bytes 1572872 | tf_op jit(solution)/shard_map/ppermute | solution.py:234
  5.2 3.4 %project.1 = (f32[384,256]{1,0:T(8,128)}, f32[384,256]{1,0:T(8,128)}, f32[32,8,256]{2,1,0:T(8,128)}) custom-call(bf16[384,1536]{1,0:T(8,128)(2,1)} %va.2, bf16[384,1536]{1,0:T(8,128)(2,1)} %vb.2, bf16[1536,256]{1,0:T(8,128)(2,1)} %w0.1), custom_call_target="tpu_custom_call" | custom-call | flops 603979776 | bytes 4194304 | tf_op jit(solution)/shard_map/project/pallas_call | solution.py:245
  8.5 6.6 %all-to-all-start = ((f32[32,8,256]{2,1,0:T(8,128)}), f32[32,8,256]{2,1,0:T(8,128)S(1)}, u32[]{:S(2)}, u32[]{:S(2)}) async-start(f32[32,8,256]{2,1,0:T(8,128)} %get-tuple-element.48), calls=%async_computation | async-start | bytes 524288 | tf_op jit(solution)/shard_map/all_to_all | solution.py:32
  15.8 3.9 %turn.1 = (bf16[1536,512]{1,0:T(8,128)(2,1)}, bf16[1536,512]{1,0:T(8,128)(2,1)}, bf16[192,1536]{1,0:T(8,128)(2,1)}) custom-call(s32[3]{0:T(128)} %pad_add_fusion.place, bf16[384,1536]{1,0:T(8,128)(2,1)} %va.2, bf16[384,1536]{1,0:T(8,128)(2,1)} %vb.2), custom_call_target="tpu_custom_call" | custom-call | flops 10485760 | bytes 6291456 | tf_op jit(solution)/shard_map/turn/pallas_call | solution.py:261
  19.7 3.9 %all-to-all-done.sums = f32[32,8,256]{2,1,0:T(8,128)S(1)} async-done(((f32[32,8,256]{2,1,0:T(8,128)}), f32[32,8,256]{2,1,0:T(8,128)S(1)}, u32[]{:S(2)}, u32[]{:S(2)}) %all-to-all-start) | async-done | bytes 262176 | tf_op jit(solution)/shard_map/all_to_all | solution.py:32
  24.4 4.7 %correlate.1 = (f32[384,512]{1,0:T(8,128)}, bf16[384,512]{1,0:T(8,128)(2,1)}, bf16[384,512]{1,0:T(8,128)(2,1)}, bf16[384,512]{1,0:T(8,128)(2,1)}) custom-call(s32[3]{0:T(128)} %pad_add_fusion.place, f32[32,8,256]{2,1,0:T(8,128)} %copy-done.1, f32[384,256]{1,0:T(8,128)} %get-tuple-element.56.pa, f32[384,256]{1,0:T(8,128)} %get-tuple-element.57.pb, ...), custom_call_target="tpu_custom_call" | custom-call | flops 603979776 | bytes 6291456 | tf_op jit(solution)/shard_map/correlate/pallas_call | solution.py:275
  35.9 2.4 %embed.1 = (bf16[48,768]{1,0:T(8,128)(2,1)S(1)}, bf16[48,768]{1,0:T(8,128)(2,1)S(1)}, bf16[48,768]{1,0:T(8,128)(2,1)S(1)}, bf16[48,768]{1,0:T(8,128)(2,1)S(1)}, ...) custom-call(s32[3]{0:T(128)S(1)} %copy-done.6, ...), custom_call_target="tpu_custom_call" | custom-call | flops 1207959552 | bytes 7340032 | tf_op jit(solution)/shard_map/embed/pallas_call | solution.py:309
  38.4 3.1 %collective-permute-start.10 = (bf16[48,768]{1,0:T(8,128)(2,1)S(1)}, bf16[48,768]{1,0:T(8,128)(2,1)S(1)}, u32[]{:S(2)}, u32[]{:S(2)}) collective-permute-start(bf16[48,768]{1,0:T(8,128)(2,1)S(1)} %get-tuple-element.75), channel_id=1, source_target_pairs={{0,8},{4,12},{8,16},{12,20},{16,24},{20,28},{24,0},{28,4},{1,9},{5... | collective-permute-start | bytes 221192 | tf_op jit(solution)/shard_map/ppermute | solution.py:237
  41.4 3.1 %collective-permute-start.11 = (bf16[48,768]{1,0:T(8,128)(2,1)S(1)}, bf16[48,768]{1,0:T(8,128)(2,1)S(1)}, u32[]{:S(2)}, u32[]{:S(2)}) collective-permute-start(bf16[48,768]{1,0:T(8,128)(2,1)S(1)} %get-tuple-element.76), channel_id=1, source_target_pairs={{0,24},{4,28},{8,0},{12,4},{16,8},{20,12},{24,16},{28,20},{1,25},{... | collective-permute-start | bytes 221192 | tf_op jit(solution)/shard_map/ppermute | solution.py:237
  44.6 6.2 %collective-permute-done.1 = bf16[384,512]{1,0:T(8,128)(2,1)S(1)} collective-permute-done((bf16[384,512]{1,0:T(8,128)(2,1)}, bf16[384,512]{1,0:T(8,128)(2,1)S(1)}, u32[]{:S(2)}, u32[]{:S(2)}) %collective-permute-start.1) | collective-permute-done | bytes 393248 | tf_op jit(solution)/shard_map/ppermute | solution.py:240
  50.8 4.3 %collective-permute-start.12 = (bf16[48,768]{1,0:T(8,128)(2,1)S(1)}, bf16[48,768]{1,0:T(8,128)(2,1)S(1)}, u32[]{:S(2)}, u32[]{:S(2)}) collective-permute-start(bf16[48,768]{1,0:T(8,128)(2,1)S(1)} %get-tuple-element.77), channel_id=1, source_target_pairs={{0,12},{4,16},{8,20},{12,24},{16,28},{20,0},{24,4},{28,8},{1,13},{... | collective-permute-start | bytes 221192 | tf_op jit(solution)/shard_map/ppermute | solution.py:237
  57.9 2.4 %collective-permute-start.13 = (bf16[48,768]{1,0:T(8,128)(2,1)S(1)}, bf16[48,768]{1,0:T(8,128)(2,1)S(1)}, u32[]{:S(2)}, u32[]{:S(2)}) collective-permute-start(bf16[48,768]{1,0:T(8,128)(2,1)S(1)} %get-tuple-element.78), channel_id=1, source_target_pairs={{0,20},{4,24},{8,28},{12,0},{16,4},{20,8},{24,12},{28,16},{1,21},{... | collective-permute-start | bytes 221192 | tf_op jit(solution)/shard_map/ppermute | solution.py:237
  60.3 4.6 %collective-permute-start.14 = (bf16[48,768]{1,0:T(8,128)(2,1)S(1)}, bf16[48,768]{1,0:T(8,128)(2,1)S(1)}, u32[]{:S(2)}, u32[]{:S(2)}) collective-permute-start(bf16[48,768]{1,0:T(8,128)(2,1)S(1)} %get-tuple-element.79), channel_id=1, source_target_pairs={{0,16},{4,20},{8,24},{12,28},{16,0},{20,4},{24,8},{28,12},{1,17},{... | collective-permute-start | bytes 221192 | tf_op jit(solution)/shard_map/ppermute | solution.py:237
  68.2 2.3 %collective-permute-done.8.refs_1_ = bf16[48,768]{1,0:T(8,128)(2,1)S(1)} collective-permute-done((bf16[48,768]{1,0:T(8,128)(2,1)S(1)}, bf16[48,768]{1,0:T(8,128)(2,1)S(1)}, u32[]{:S(2)}, u32[]{:S(2)}) %collective-permute-start.8) | collective-permute-done | bytes 73760 | tf_op jit(solution)/shard_map/ppermute | solution.py:237
  71.2 2.0 %collective-permute-start.15 = (bf16[48,768]{1,0:T(8,128)(2,1)S(1)}, bf16[48,768]{1,0:T(8,128)(2,1)S(1)}, u32[]{:S(2)}, u32[]{:S(2)}) collective-permute-start(bf16[48,768]{1,0:T(8,128)(2,1)S(1)} %add.34.p0), channel_id=1, source_target_pairs={{0,4},{4,8},{8,12},{12,16},{16,20},{20,24},{24,28},{28,0},{1,5},{5... | collective-permute-start | bytes 221192 | tf_op jit(solution)/shard_map/ppermute | solution.py:237
  74.6 2.2 %collective-permute-start.17 = (bf16[48,768]{1,0:T(8,128)(2,1)S(1)}, bf16[48,768]{1,0:T(8,128)(2,1)S(1)}, u32[]{:S(2)}, u32[]{:S(2)}) collective-permute-start(bf16[48,768]{1,0:T(8,128)(2,1)S(1)} %add.34.p0), channel_id=1, source_target_pairs={{0,8},{4,12},{8,16},{12,20},{16,24},{20,28},{24,0},{28,4},{1,9},{5... | collective-permute-start | bytes 221192 | tf_op jit(solution)/shard_map/ppermute | solution.py:237
  78.2 2.2 %collective-permute-start.19 = (bf16[48,768]{1,0:T(8,128)(2,1)S(1)}, bf16[48,768]{1,0:T(8,128)(2,1)S(1)}, u32[]{:S(2)}, u32[]{:S(2)}) collective-permute-start(bf16[48,768]{1,0:T(8,128)(2,1)S(1)} %add.34.p0), channel_id=1, source_target_pairs={{0,12},{4,16},{8,20},{12,24},{16,28},{20,0},{24,4},{28,8},{1,13},{... | collective-permute-start | bytes 221192 | tf_op jit(solution)/shard_map/ppermute | solution.py:237
  80.4 2.3 %collective-permute-start.20 = (bf16[48,768]{1,0:T(8,128)(2,1)S(1)}, bf16[48,768]{1,0:T(8,128)(2,1)S(1)}, u32[]{:S(2)}, u32[]{:S(2)}) collective-permute-start(bf16[48,768]{1,0:T(8,128)(2,1)S(1)} %add.34.p0), channel_id=1, source_target_pairs={{0,20},{4,24},{8,28},{12,0},{16,4},{20,8},{24,12},{28,16},{1,21},{... | collective-permute-start | bytes 221192 | tf_op jit(solution)/shard_map/ppermute | solution.py:237
  82.7 4.4 %collective-permute-start.21 = (bf16[48,768]{1,0:T(8,128)(2,1)S(1)}, bf16[48,768]{1,0:T(8,128)(2,1)S(1)}, u32[]{:S(2)}, u32[]{:S(2)}) collective-permute-start(bf16[48,768]{1,0:T(8,128)(2,1)S(1)} %add.34.p0), channel_id=1, source_target_pairs={{0,16},{4,20},{8,24},{12,28},{16,0},{20,4},{24,8},{28,12},{1,17},{... | collective-permute-start | bytes 221192 | tf_op jit(solution)/shard_map/ppermute | solution.py:237
  93.8 4.3 %collective-permute-start.30 = (bf16[4,48,768]{2,1,0:T(8,128)(2,1)S(1)}, bf16[4,48,768]{2,1,0:T(8,128)(2,1)S(1)}, u32[]{:S(2)}, u32[]{:S(2)}) collective-permute-start(bf16[4,48,768]{2,1,0:T(8,128)(2,1)S(1)} %collective-permute-done.28.refs_4_), channel_id=1, source_target_pairs={{0,1},{1,0},{2,3},{3,2},{4,5},{5,4},{6,7},{7,6},{8,9},{9,8},{10,11... | collective-permute-start | bytes 884744 | tf_op jit(solution)/shard_map/ppermute | solution.py:234
  98.1 6.2 %collective-permute-done.24 = f16[384,512]{1,0:T(8,128)(2,1)S(1)} collective-permute-done((f16[384,512]{1,0:T(8,128)(2,1)S(1)}, f16[384,512]{1,0:T(8,128)(2,1)S(1)}, u32[]{:S(2)}, u32[]{:S(2)}) %collective-permute-start.24) | collective-permute-done | bytes 393248 | tf_op jit(solution)/shard_map/ppermute | solution.py:240
  104.3 3.5 %collective-permute-done.25 = f16[384,512]{1,0:T(8,128)(2,1)S(1)} collective-permute-done((f16[384,512]{1,0:T(8,128)(2,1)S(1)}, f16[384,512]{1,0:T(8,128)(2,1)S(1)}, u32[]{:S(2)}, u32[]{:S(2)}) %collective-permute-start.25) | collective-permute-done | bytes 393248 | tf_op jit(solution)/shard_map/ppermute | solution.py:240
  108.3 2.1 %collective-permute-start.31 = (bf16[4,48,768]{2,1,0:T(8,128)(2,1)S(1)}, bf16[4,48,768]{2,1,0:T(8,128)(2,1)S(1)}, u32[]{:S(2)}, u32[]{:S(2)}) collective-permute-start(bf16[4,48,768]{2,1,0:T(8,128)(2,1)S(1)} %collective-permute-done.29.refs_5_), channel_id=1, source_target_pairs={{0,1},{1,0},{2,3},{3,2},{4,5},{5,4},{6,7},{7,6},{8,9},{9,8},{10,11... | collective-permute-start | bytes 884744 | tf_op jit(solution)/shard_map/ppermute | solution.py:234
  112.4 3.4 %combine.1 = (f32[384,256]{1,0:T(8,128)}, f32[384,256]{1,0:T(8,128)}) custom-call(s32[3]{0:T(128)S(1)} %copy-done.6, f32[32,8,256]{2,1,0:T(8,128)S(1)} %copy-done.3, f32[384,256]{1,0:T(8,128)S(1)} %copy-done.4, f32[384,256]{1,0:T(8,128)S(1)} %copy-done.5, bf16[4,48,768]{2,1,0:T(8,128)(2,1)S(1)} %join.2.refs_0_, bf16[4,48,768]{2,1,0:T(8,128)(2,1)S(1)} %join.3.refs_1_, ...), custom_call_target="tpu_custom_call" | custom-call | flops 1207959552 | bytes 8388608 | tf_op jit(solution)/shard_map/combine/pallas_call | solution.py:354
  (84 shorter events, 29.2 us)
Async XLA Ops:
  1.7 22.0 %collective-permute-start = (bf16[1024,256]{1,0:T(8,128)(2,1)S(1)}, bf16[1024,256]{1,0:T(8,128)(2,1)S(1)}, u32[]{:S(2)}, u32[]{:S(2)}) collective-permute-start(bf16[1024,256]{1,0:T(8,128)(2,1)S(1)} %slice.13), channel_id=1, source_target_pairs={{0,2},{2,0},{1,3},{3,1},{4,6},{6,4},{5,7},{7,5},{8,10},{10,8},{9,1... | collective-permute-start | bytes 1572872 | tf_op jit(solution)/shard_map/ppermute | solution.py:234
  3.9 29.2 %collective-permute-start.4 = (bf16[1536,256]{1,0:T(8,128)(2,1)}, bf16[1536,256]{1,0:T(8,128)(2,1)S(1)}, u32[]{:S(2)}, u32[]{:S(2)}) collective-permute-start(bf16[1536,256]{1,0:T(8,128)(2,1)} %w0.1), channel_id=1, source_target_pairs={{0,1},{1,0},{2,3},{3,2},{4,5},{5,4},{6,7},{7,6},{8,9},{9,8},{10,11... | collective-permute-start | bytes 2359304 | tf_op jit(solution)/shard_map/ppermute | solution.py:234
  8.5 15.1 %all-to-all-start = ((f32[32,8,256]{2,1,0:T(8,128)}), f32[32,8,256]{2,1,0:T(8,128)S(1)}, u32[]{:S(2)}, u32[]{:S(2)}) async-start(f32[32,8,256]{2,1,0:T(8,128)} %get-tuple-element.48), calls=%async_computation | async-start | bytes 524288 | tf_op jit(solution)/shard_map/all_to_all | solution.py:32
  23.7 8.1 %collective-permute-start.5 = (bf16[512,256]{1,0:T(8,128)(2,1)S(1)}, bf16[512,256]{1,0:T(8,128)(2,1)S(1)}, u32[]{:S(2)}, u32[]{:S(2)}) collective-permute-start(bf16[512,256]{1,0:T(8,128)(2,1)S(1)} %slice.12), channel_id=1, source_target_pairs={{0,2},{2,0},{1,3},{3,1},{4,6},{6,4},{5,7},{7,5},{8,10},{10,8},{9,1... | collective-permute-start | bytes 786440 | tf_op jit(solution)/shard_map/ppermute | solution.py:234
  30.3 20.5 %collective-permute-start.1 = (bf16[384,512]{1,0:T(8,128)(2,1)}, bf16[384,512]{1,0:T(8,128)(2,1)S(1)}, u32[]{:S(2)}, u32[]{:S(2)}) collective-permute-start(bf16[384,512]{1,0:T(8,128)(2,1)} %get-tuple-element.66), channel_id=1, source_target_pairs={{0,32},{32,64},{64,96},{96,0},{1,33},{33,65},{65,97},{97,1},{2,34}... | collective-permute-start | bytes 1179656 | tf_op jit(solution)/shard_map/ppermute | solution.py:240
  30.7 24.5 %collective-permute-start.2 = (bf16[384,512]{1,0:T(8,128)(2,1)}, bf16[384,512]{1,0:T(8,128)(2,1)S(1)}, u32[]{:S(2)}, u32[]{:S(2)}) collective-permute-start(bf16[384,512]{1,0:T(8,128)(2,1)} %get-tuple-element.67), channel_id=1, source_target_pairs={{0,64},{32,96},{64,0},{96,32},{1,65},{33,97},{65,1},{97,33},{2,66}... | collective-permute-start | bytes 1179656 | tf_op jit(solution)/shard_map/ppermute | solution.py:240
  31.8 23.4 %collective-permute-start.3 = (bf16[384,512]{1,0:T(8,128)(2,1)}, bf16[384,512]{1,0:T(8,128)(2,1)S(1)}, u32[]{:S(2)}, u32[]{:S(2)}) collective-permute-start(bf16[384,512]{1,0:T(8,128)(2,1)} %get-tuple-element.68), channel_id=1, source_target_pairs={{0,96},{32,0},{64,32},{96,64},{1,97},{33,1},{65,33},{97,65},{2,98}... | collective-permute-start | bytes 1179656 | tf_op jit(solution)/shard_map/ppermute | solution.py:240
  38.4 21.9 %collective-permute-start.10 = (bf16[48,768]{1,0:T(8,128)(2,1)S(1)}, bf16[48,768]{1,0:T(8,128)(2,1)S(1)}, u32[]{:S(2)}, u32[]{:S(2)}) collective-permute-start(bf16[48,768]{1,0:T(8,128)(2,1)S(1)} %get-tuple-element.75), channel_id=1, source_target_pairs={{0,8},{4,12},{8,16},{12,20},{16,24},{20,28},{24,0},{28,4},{1,9},{5... | collective-permute-start | bytes 221192 | tf_op jit(solution)/shard_map/ppermute | solution.py:237
  41.4 23.5 %collective-permute-start.11 = (bf16[48,768]{1,0:T(8,128)(2,1)S(1)}, bf16[48,768]{1,0:T(8,128)(2,1)S(1)}, u32[]{:S(2)}, u32[]{:S(2)}) collective-permute-start(bf16[48,768]{1,0:T(8,128)(2,1)S(1)} %get-tuple-element.76), channel_id=1, source_target_pairs={{0,24},{4,28},{8,0},{12,4},{16,8},{20,12},{24,16},{28,20},{1,25},{... | collective-permute-start | bytes 221192 | tf_op jit(solution)/shard_map/ppermute | solution.py:237
  50.8 14.9 %collective-permute-start.12 = (bf16[48,768]{1,0:T(8,128)(2,1)S(1)}, bf16[48,768]{1,0:T(8,128)(2,1)S(1)}, u32[]{:S(2)}, u32[]{:S(2)}) collective-permute-start(bf16[48,768]{1,0:T(8,128)(2,1)S(1)} %get-tuple-element.77), channel_id=1, source_target_pairs={{0,12},{4,16},{8,20},{12,24},{16,28},{20,0},{24,4},{28,8},{1,13},{... | collective-permute-start | bytes 221192 | tf_op jit(solution)/shard_map/ppermute | solution.py:237
  55.4 31.7 %collective-permute-start.22 = (f16[384,512]{1,0:T(8,128)(2,1)S(1)}, f16[384,512]{1,0:T(8,128)(2,1)S(1)}, u32[]{:S(2)}, u32[]{:S(2)}) collective-permute-start(f16[384,512]{1,0:T(8,128)(2,1)S(1)} %get-tuple-element.94), channel_id=1, source_target_pairs={{0,128},{128,0},{1,129},{129,1},{2,130},{130,2},{3,131},{131,3},{4... | collective-permute-start | bytes 1179656 | tf_op jit(solution)/shard_map/ppermute | solution.py:234
  57.9 10.3 %collective-permute-start.13 = (bf16[48,768]{1,0:T(8,128)(2,1)S(1)}, bf16[48,768]{1,0:T(8,128)(2,1)S(1)}, u32[]{:S(2)}, u32[]{:S(2)}) collective-permute-start(bf16[48,768]{1,0:T(8,128)(2,1)S(1)} %get-tuple-element.78), channel_id=1, source_target_pairs={{0,20},{4,24},{8,28},{12,0},{16,4},{20,8},{24,12},{28,16},{1,21},{... | collective-permute-start | bytes 221192 | tf_op jit(solution)/shard_map/ppermute | solution.py:237
  60.3 7.9 %collective-permute-start.14 = (bf16[48,768]{1,0:T(8,128)(2,1)S(1)}, bf16[48,768]{1,0:T(8,128)(2,1)S(1)}, u32[]{:S(2)}, u32[]{:S(2)}) collective-permute-start(bf16[48,768]{1,0:T(8,128)(2,1)S(1)} %get-tuple-element.79), channel_id=1, source_target_pairs={{0,16},{4,20},{8,24},{12,28},{16,0},{20,4},{24,8},{28,12},{1,17},{... | collective-permute-start | bytes 221192 | tf_op jit(solution)/shard_map/ppermute | solution.py:237
  73.2 7.2 %collective-permute-start.16 = (bf16[48,768]{1,0:T(8,128)(2,1)S(1)}, bf16[48,768]{1,0:T(8,128)(2,1)S(1)}, u32[]{:S(2)}, u32[]{:S(2)}) collective-permute-start(bf16[48,768]{1,0:T(8,128)(2,1)S(1)} %add.34.p0), channel_id=1, source_target_pairs={{0,28},{4,0},{8,4},{12,8},{16,12},{20,16},{24,20},{28,24},{1,29},{... | collective-permute-start | bytes 221192 | tf_op jit(solution)/shard_map/ppermute | solution.py:237
  74.6 8.1 %collective-permute-start.17 = (bf16[48,768]{1,0:T(8,128)(2,1)S(1)}, bf16[48,768]{1,0:T(8,128)(2,1)S(1)}, u32[]{:S(2)}, u32[]{:S(2)}) collective-permute-start(bf16[48,768]{1,0:T(8,128)(2,1)S(1)} %add.34.p0), channel_id=1, source_target_pairs={{0,8},{4,12},{8,16},{12,20},{16,24},{20,28},{24,0},{28,4},{1,9},{5... | collective-permute-start | bytes 221192 | tf_op jit(solution)/shard_map/ppermute | solution.py:237
  76.8 11.1 %collective-permute-start.18 = (bf16[48,768]{1,0:T(8,128)(2,1)S(1)}, bf16[48,768]{1,0:T(8,128)(2,1)S(1)}, u32[]{:S(2)}, u32[]{:S(2)}) collective-permute-start(bf16[48,768]{1,0:T(8,128)(2,1)S(1)} %add.34.p0), channel_id=1, source_target_pairs={{0,24},{4,28},{8,0},{12,4},{16,8},{20,12},{24,16},{28,20},{1,25},{... | collective-permute-start | bytes 221192 | tf_op jit(solution)/shard_map/ppermute | solution.py:237
  78.2 9.8 %collective-permute-start.19 = (bf16[48,768]{1,0:T(8,128)(2,1)S(1)}, bf16[48,768]{1,0:T(8,128)(2,1)S(1)}, u32[]{:S(2)}, u32[]{:S(2)}) collective-permute-start(bf16[48,768]{1,0:T(8,128)(2,1)S(1)} %add.34.p0), channel_id=1, source_target_pairs={{0,12},{4,16},{8,20},{12,24},{16,28},{20,0},{24,4},{28,8},{1,13},{... | collective-permute-start | bytes 221192 | tf_op jit(solution)/shard_map/ppermute | solution.py:237
  80.4 9.1 %collective-permute-start.20 = (bf16[48,768]{1,0:T(8,128)(2,1)S(1)}, bf16[48,768]{1,0:T(8,128)(2,1)S(1)}, u32[]{:S(2)}, u32[]{:S(2)}) collective-permute-start(bf16[48,768]{1,0:T(8,128)(2,1)S(1)} %add.34.p0), channel_id=1, source_target_pairs={{0,20},{4,24},{8,28},{12,0},{16,4},{20,8},{24,12},{28,16},{1,21},{... | collective-permute-start | bytes 221192 | tf_op jit(solution)/shard_map/ppermute | solution.py:237
  82.7 9.0 %collective-permute-start.21 = (bf16[48,768]{1,0:T(8,128)(2,1)S(1)}, bf16[48,768]{1,0:T(8,128)(2,1)S(1)}, u32[]{:S(2)}, u32[]{:S(2)}) collective-permute-start(bf16[48,768]{1,0:T(8,128)(2,1)S(1)} %add.34.p0), channel_id=1, source_target_pairs={{0,16},{4,20},{8,24},{12,28},{16,0},{20,4},{24,8},{28,12},{1,17},{... | collective-permute-start | bytes 221192 | tf_op jit(solution)/shard_map/ppermute | solution.py:237
  88.0 10.1 %collective-permute-start.23 = (f16[384,512]{1,0:T(8,128)(2,1)S(1)}, f16[384,512]{1,0:T(8,128)(2,1)S(1)}, u32[]{:S(2)}, u32[]{:S(2)}) collective-permute-start(f16[384,512]{1,0:T(8,128)(2,1)S(1)} %get-tuple-element.96), channel_id=1, source_target_pairs={{0,32},{32,64},{64,96},{96,0},{1,33},{33,65},{65,97},{97,1},{2,34}... | collective-permute-start | bytes 1179656 | tf_op jit(solution)/shard_map/ppermute | solution.py:240
  88.0 16.4 %collective-permute-start.24 = (f16[384,512]{1,0:T(8,128)(2,1)S(1)}, f16[384,512]{1,0:T(8,128)(2,1)S(1)}, u32[]{:S(2)}, u32[]{:S(2)}) collective-permute-start(f16[384,512]{1,0:T(8,128)(2,1)S(1)} %get-tuple-element.96), channel_id=1, source_target_pairs={{0,64},{32,96},{64,0},{96,32},{1,65},{33,97},{65,1},{97,33},{2,66}... | collective-permute-start | bytes 1179656 | tf_op jit(solution)/shard_map/ppermute | solution.py:240
  89.5 18.3 %collective-permute-start.25 = (f16[384,512]{1,0:T(8,128)(2,1)S(1)}, f16[384,512]{1,0:T(8,128)(2,1)S(1)}, u32[]{:S(2)}, u32[]{:S(2)}) collective-permute-start(f16[384,512]{1,0:T(8,128)(2,1)S(1)} %get-tuple-element.96), channel_id=1, source_target_pairs={{0,96},{32,0},{64,32},{96,64},{1,97},{33,1},{65,33},{97,65},{2,98}... | collective-permute-start | bytes 1179656 | tf_op jit(solution)/shard_map/ppermute | solution.py:240
  92.4 15.9 %collective-permute-start.29 = (bf16[4,48,768]{2,1,0:T(8,128)(2,1)S(1)}, bf16[4,48,768]{2,1,0:T(8,128)(2,1)S(1)}, u32[]{:S(2)}, u32[]{:S(2)}) collective-permute-start(bf16[4,48,768]{2,1,0:T(8,128)(2,1)S(1)} %join.3.refs_1_), channel_id=1, source_target_pairs={{0,2},{2,0},{1,3},{3,1},{4,6},{6,4},{5,7},{7,5},{8,10},{10,8},{9,1... | collective-permute-start | bytes 884744 | tf_op jit(solution)/shard_map/ppermute | solution.py:234
  93.8 17.1 %collective-permute-start.30 = (bf16[4,48,768]{2,1,0:T(8,128)(2,1)S(1)}, bf16[4,48,768]{2,1,0:T(8,128)(2,1)S(1)}, u32[]{:S(2)}, u32[]{:S(2)}) collective-permute-start(bf16[4,48,768]{2,1,0:T(8,128)(2,1)S(1)} %collective-permute-done.28.refs_4_), channel_id=1, source_target_pairs={{0,1},{1,0},{2,3},{3,2},{4,5},{5,4},{6,7},{7,6},{8,9},{9,8},{10,11... | collective-permute-start | bytes 884744 | tf_op jit(solution)/shard_map/ppermute | solution.py:234
  (20 other events, 150.2 us)

commit v7 on v5

--- a/solution.py
+++ b/solution.py
@@ -21,7 +21,6 @@
 QUARTER = ROWS // 4
 PIECE = (48, 768)
 SHARE = DEPTH // 4
-EARLY = 1024
 VMEM = pl.BlockSpec(memory_space=pltpu.VMEM)
 SMEM = pl.BlockSpec(memory_space=pltpu.SMEM)
 ANY = pl.BlockSpec(memory_space=pl.ANY)
@@ -87,16 +86,12 @@
     return ma, ra, mb, rb, (t[4:5] - ma * mb) * ra * rb
 
 
-def embed(place, sums, v, w0, w1, w2, w2b, w3, w3b, y, na, nb):
+def embed(place, sums, v, w0, w1, w2, w3, y, na, nb):
     q = place[0]
-    half = EARLY
-    ws = ((w0,), (w1,), (w2, w2b), (w3, w3b))
+    ws = (w0, w1, w2, w3)
     for j, wj in enumerate(ws):
         ma, ra, mb, rb, _ = moments(sums, q ^ j)
-        if len(wj) == 1:
-            p = dot(v[...], wj[0][...], 1, 0)
-        else:
-            p = dot(v[:, :half], wj[0][...], 1, 0) + dot(v[:, half:], wj[1][...], 1, 0)
+        p = dot(v[...], wj[...], 1, 0)
         cols = slice(j * BLOCK, (j + 1) * BLOCK)
         na[:, cols] = ((p[:QUARTER] - ma) * (ra * ra)).astype(bf16)
         nb[:, cols] = ((p[QUARTER:] - mb) * (rb * rb)).astype(bf16)
@@ -104,11 +99,8 @@
     for k in range(6):
         acc = 0.0
         for j, wj in enumerate(ws):
-            late = len(wj) == 2 and k * 256 >= EARLY
-            part = wj[1] if late else wj[0]
-            first = k * 256 - (EARLY if late else 0)
             nj = n[:, j * BLOCK : (j + 1) * BLOCK]
-            acc = acc + dot(nj, part[first : first + 256, :], 1, 1)
+            acc = acc + dot(nj, wj[k * 256 : (k + 1) * 256, :], 1, 1)
         acc = acc.astype(bf16)
         for i in range(4):
             y[2 * i + k // 3, :, (k % 3) * 256 : (k % 3 + 1) * 256] = acc[48 * i : 48 * i + 48]
@@ -132,7 +124,7 @@
         out[...] = jnp.concatenate([v, centre, jnp.zeros((112, DEPTH), bf16)], axis=0).T
 
 
-def correlate(place, sums, pa, pb, ta, tb, u0, u1, u2, u3, xs, xpa, xpb, xa, xb, x0, x1, x2, x3, sem, out_sem):
+def correlate(place, sums, pa, pb, ta, tb, ready, u0, u1, u2, u3, xs, xpa, xpb, xa, xb, x0, x1, x2, x3, sem, out_sem):
     q, yy = place[0], place[1]
     stats = [
         pltpu.make_async_copy(src, dst, sem.at[8 + i])
@@ -222,7 +214,6 @@
     place = jnp.stack([q, lax.axis_index("y")]).astype(jnp.int32)
     shape = jax.ShapeDtypeStruct
     sems = pltpu.SemaphoreType.DMA
-    half = EARLY
 
     def swap(t, axis):
         return lax.ppermute(t, axis, SWAP)
@@ -230,8 +221,8 @@
     def along_y(t, s):
         return lax.ppermute(t, "y", [(i, (i + s) % 4) for i in range(4)])
 
+    w_x = swap(w, "xl")
     w_c = swap(w, "c")
-    w_x = swap(w[:half], "xl")
 
     pa, pb, own = call(
         project,
@@ -257,16 +248,25 @@
         6 * 2**20,
         name="turn",
     )(place, va, vb)
-    sums, ta, tb, v_quarter, w_late, w_x = lax.optimization_barrier(
-        (sums, ta, tb, v_quarter, w[half:], w_x)
-    )
-    w_xb = swap(w_late, "xl")
-    w_xcb = swap(w_xb, "c")
+    sums, ta, tb, v_quarter, w_x = lax.optimization_barrier((sums, ta, tb, v_quarter, w_x))
+    w_xc = swap(w_x, "c")
+
+    y_part = call(
+        embed,
+        shape((8,) + PIECE, bf16),
+        [SMEM] + [VMEM] * 6,
+        16 * ROWS * DEPTH * BLOCK // 2,
+        7 * 2**20,
+        [pltpu.VMEM((QUARTER, 4 * BLOCK), bf16)] * 2,
+        name="embed",
+        vmem=20,
+    )(place, sums, v_quarter, w, w_c, w_x, w_xc)
+    y_parts = exchange(y_part, "z")
 
     u_parts = call(
         correlate,
         (shape((SHARE, 2 * BLOCK), f32),) + (shape((SHARE, 2 * BLOCK), bf16),) * 3,
-        [SMEM] + [ANY] * 5,
+        [SMEM] + [ANY] * 6,
         4 * ROWS * DEPTH * BLOCK,
         6 * 2**20,
         [
@@ -284,29 +284,17 @@
         ],
         out_specs=(ANY,) * 4,
         name="correlate",
-    )(place, sums, pa, pb, ta, tb)
-    *u_parts, w_x = lax.optimization_barrier((*u_parts, w_x))
-    w_xc = swap(w_x, "c")
+    )(place, sums, pa, pb, ta, tb, y_part)
     u = u_parts[0]
     for s in (1, 2, 3):
         u = u + along_y(u_parts[s], s).astype(f32)
-    u_near = arrival(u[:8, :128], 8)
+    u_near = arrival(u[:8, :128], 2)
     u = u.astype(f16)
     u = u.astype(f32) + swap(u, "xh").astype(f32)
     u_far = arrival(u[:8, :128], 4)
     u = lax.optimization_barrier(u.astype(f16))
     us = [u] + [along_y(u, s) for s in (1, 2, 3)]
 
-    y_part = call(
-        embed,
-        shape((8,) + PIECE, bf16),
-        [SMEM] + [VMEM] * 8,
-        16 * ROWS * DEPTH * BLOCK // 2,
-        7 * 2**20,
-        [pltpu.VMEM((QUARTER, 4 * BLOCK), bf16)] * 2,
-        name="embed",
-        vmem=20,
-    )(place, sums, v_quarter, w, w_c, w_x, w_xb, w_xc, w_xcb)
     y_copies = call(
         add_copies,
         shape((8,) + PIECE, bf16),
@@ -315,7 +303,7 @@
         2**20,
         name="add_copies",
         vmem=4,
-    )(exchange(y_part, "z"), u_near)
+    )(y_parts, u_near)
     y0 = call(
         halve,
         (shape((4,) + PIECE, bf16),) * 2,

time: 113 us -> 121 us (1.071); the launches traced: 112 us -> 119 us
  waiting for transfers between devices: 41.6 us -> 50.5 us
  local copies, waits for them, and re-layouts: 5.71 us -> 3.63 us
  other arithmetic: 4.67 us -> 2.64 us
  starting transfers between devices: 38.9 us -> 40.9 us
    ppermute x6, waiting for transfers between devices: 3.71 us -> 23.4 us  [along_y(): return lax.ppermute(t, 'y', [(i, (i + s) % 4) for i in range(4)])]
    all_to_all x3, waiting for transfers between devices: 28.6 us -> 19.4 us  [exchange(): return lax.all_to_all(blocks, axes, split_axis=0, concat_axis=0, tiled=True)]
    all_to_all x3, starting transfers between devices: 18.4 us -> 22.6 us  [exchange(): return lax.all_to_all(blocks, axes, split_axis=0, concat_axis=0, tiled=True)]
    ppermute x12 -> x10, starting transfers between devices: 13.8 us -> 10.2 us  [swap(): return lax.ppermute(t, axis, SWAP)]
    convert_element_type x3, other arithmetic: 2.56 us -> 0.53 us  [local(): split += [high.astype(bf16), (t - high).astype(bf16)]]
    slice x3 -> x1, local copies, waits for them, and re-layouts: 2.39 us -> 0.59 us  [local(): u_near = arrival(u[:8, :128], 2)]
    ppermute x12 -> x10, waiting for transfers between devices: 9.37 us -> 7.74 us  [swap(): return lax.ppermute(t, axis, SWAP)]
    ppermute x6, starting transfers between devices: 6.69 us -> 8.16 us  [along_y(): return lax.ppermute(t, 'y', [(i, (i + s) % 4) for i in range(4)])]
  transfers between devices with their start and end apart: 21 -> 19, of which waited for: 9 -> 12; matrix products, arithmetic and copies ran while one was open for 6% -> 3% of each run, Pallas kernels for 15% -> 12%
where the time goes in v7:
time: 121 us; the launch traced here: 119 us
  waiting for transfers between devices  50.5 us (42%)
  starting transfers between devices  40.9 us (34%)
  Pallas kernels  20.5 us (17%)
  local copies, waits for them, and re-layouts  3.63 us (3%)
  other arithmetic  2.64 us (2%)
    ppermute x6, waiting for transfers between devices, along_y(): return lax.ppermute(t, 'y', [(i, (i + s) % 4) for i in range(4)])  23.4 us
    all_to_all x3, starting transfers between devices, exchange(): return lax.all_to_all(blocks, axes, split_axis=0, concat_axis=0, tiled=True)  22.6 us
    all_to_all x3, waiting for transfers between devices, exchange(): return lax.all_to_all(blocks, axes, split_axis=0, concat_axis=0, tiled=True)  19.4 us
    ppermute x10, starting transfers between devices, swap(): return lax.ppermute(t, axis, SWAP)  10.2 us
    ppermute x6, starting transfers between devices, along_y(): return lax.ppermute(t, 'y', [(i, (i + s) % 4) for i in range(4)])  8.16 us
    ppermute x10, waiting for transfers between devices, swap(): return lax.ppermute(t, axis, SWAP)  7.74 us
    pallas_call x1, Pallas kernels, local(): call(correlate, (shape((SHARE, 2 * BLOCK), f32),) + (shape((SHARE, 2 * BL...  4.59 us
    pallas_call x1, Pallas kernels, local(): call(turn, (shape((DEPTH, 512), bf16),) * 2 + (shape((2 * QUARTER, DEPTH)...  3.92 us
  transfers between devices with their start and end apart: 19, of which 12 were waited for; matrix products, arithmetic and copies ran while one was open for 3% of the time, Pallas kernels for 12%

profile of v7, /device:TPU:1, one launch (start us, length us, event | category | flops | bytes accessed | tf_op | source)
XLA Modules:
  0.0 119.0 jit_solution(9401283164881200015)
XLA Ops:
  0.6 2.1 %collective-permute-start = (bf16[1536,256]{1,0:T(8,128)(2,1)}, bf16[1536,256]{1,0:T(8,128)(2,1)S(1)}, u32[]{:S(2)}, u32[]{:S(2)}) collective-permute-start(bf16[1536,256]{1,0:T(8,128)(2,1)} %w0.1), channel_id=1, source_target_pairs={{0,2},{2,0},{1,3},{3,1},{4,6},{6,4},{5,7},{7,5},{8,10},{10,8},{9,1... | collective-permute-start | bytes 2359304 | tf_op jit(solution)/shard_map/ppermute | solution.py:219
  2.8 3.4 %project.1 = (f32[384,256]{1,0:T(8,128)}, f32[384,256]{1,0:T(8,128)}, f32[32,8,256]{2,1,0:T(8,128)}) custom-call(bf16[384,1536]{1,0:T(8,128)(2,1)} %va.2, bf16[384,1536]{1,0:T(8,128)(2,1)} %vb.2, bf16[1536,256]{1,0:T(8,128)(2,1)} %w0.1), custom_call_target="tpu_custom_call" | custom-call | flops 603979776 | bytes 4194304 | tf_op jit(solution)/shard_map/project/pallas_call | solution.py:227
  6.2 7.8 %all-to-all-start = ((f32[32,8,256]{2,1,0:T(8,128)}), f32[32,8,256]{2,1,0:T(8,128)S(1)}, u32[]{:S(2)}, u32[]{:S(2)}) async-start(f32[32,8,256]{2,1,0:T(8,128)} %get-tuple-element.36), calls=%async_computation | async-start | bytes 524288 | tf_op jit(solution)/shard_map/all_to_all | solution.py:30
  14.9 3.9 %turn.1 = (bf16[1536,512]{1,0:T(8,128)(2,1)}, bf16[1536,512]{1,0:T(8,128)(2,1)}, bf16[192,1536]{1,0:T(8,128)(2,1)}) custom-call(s32[2]{0:T(128)} %pad_add_fusion.place, bf16[384,1536]{1,0:T(8,128)(2,1)} %va.2, bf16[384,1536]{1,0:T(8,128)(2,1)} %vb.2), custom_call_target="tpu_custom_call" | custom-call | flops 10485760 | bytes 6291456 | tf_op jit(solution)/shard_map/turn/pallas_call | solution.py:243
  18.8 9.5 %all-to-all-done.sums = f32[32,8,256]{2,1,0:T(8,128)S(1)} async-done(((f32[32,8,256]{2,1,0:T(8,128)}), f32[32,8,256]{2,1,0:T(8,128)S(1)}, u32[]{:S(2)}, u32[]{:S(2)}) %all-to-all-start) | async-done | bytes 262176 | tf_op jit(solution)/shard_map/all_to_all | solution.py:30
  29.1 1.9 %collective-permute-done.2.w3 = bf16[1536,256]{1,0:T(8,128)(2,1)S(1)} collective-permute-done((bf16[1536,256]{1,0:T(8,128)(2,1)S(1)}, bf16[1536,256]{1,0:T(8,128)(2,1)S(1)}, u32[]{:S(2)}, u32[]{:S(2)}) %collective-permute-start.2) | collective-permute-done | bytes 786464 | tf_op jit(solution)/shard_map/ppermute | solution.py:219
  32.1 3.2 %embed.1.ready = bf16[8,48,768]{2,1,0:T(8,128)(2,1)} custom-call(s32[2]{0:T(128)S(1)} %copy-done.6, f32[32,8,256]{2,1,0:T(8,128)S(1)} %all-to-all-done.sums, bf16[192,1536]{1,0:T(8,128)(2,1)S(1)} %copy-done.5, bf16[1536,256]{1,0:T(8,128)(2,1)S(1)} %copy-done.2, bf16[1536,256]{1,0:T(8,128)(2,1)S(1)} %collective-permute-done.1.w1, ...), custom_call_target="tpu_custom_call" | custom-call | flops 1207959552 | bytes 7340032 | tf_op jit(solution)/shard_map/embed/pallas_call | solution.py:254
  35.3 8.2 %all-to-all-start.1 = ((bf16[8,48,768]{2,1,0:T(8,128)(2,1)}), bf16[8,48,768]{2,1,0:T(8,128)(2,1)S(1)}, u32[]{:S(2)}, u32[]{:S(2)}) async-start(bf16[8,48,768]{2,1,0:T(8,128)(2,1)} %embed.1.ready), calls=%async_computation.1 | async-start | bytes 1179648 | tf_op jit(solution)/shard_map/all_to_all | solution.py:30
  43.4 4.6 %correlate.1 = (f32[384,512]{1,0:T(8,128)}, bf16[384,512]{1,0:T(8,128)(2,1)}, bf16[384,512]{1,0:T(8,128)(2,1)}, bf16[384,512]{1,0:T(8,128)(2,1)}) custom-call(s32[2]{0:T(128)} %pad_add_fusion.place, f32[32,8,256]{2,1,0:T(8,128)} %copy-done, f32[384,256]{1,0:T(8,128)} %get-tuple-element.44.pa, f32[384,256]{1,0:T(8,128)} %get-tuple-element.45.pb, ...), custom_call_target="tpu_custom_call" | custom-call | flops 603979776 | bytes 6291456 | tf_op jit(solution)/shard_map/correlate/pallas_call | solution.py:266
  48.6 1.1 collective-permute-start.4
  49.7 1.4 %collective-permute-start.5 = (bf16[384,512]{1,0:T(8,128)(2,1)}, bf16[384,512]{1,0:T(8,128)(2,1)S(1)}, u32[]{:S(2)}, u32[]{:S(2)}) collective-permute-start(bf16[384,512]{1,0:T(8,128)(2,1)} %get-tuple-element.53), channel_id=1, source_target_pairs={{0,96},{32,0},{64,32},{96,64},{1,97},{33,1},{65,33},{97,65},{2,98}... | collective-permute-start | bytes 1179656 | tf_op jit(solution)/shard_map/ppermute | solution.py:222
  51.1 9.5 %collective-permute-done.3 = bf16[384,512]{1,0:T(8,128)(2,1)S(1)} collective-permute-done((bf16[384,512]{1,0:T(8,128)(2,1)}, bf16[384,512]{1,0:T(8,128)(2,1)S(1)}, u32[]{:S(2)}, u32[]{:S(2)}) %collective-permute-start.3) | collective-permute-done | bytes 393248 | tf_op jit(solution)/shard_map/ppermute | solution.py:222
  60.6 6.3 %collective-permute-done.4 = bf16[384,512]{1,0:T(8,128)(2,1)S(1)} collective-permute-done((bf16[384,512]{1,0:T(8,128)(2,1)}, bf16[384,512]{1,0:T(8,128)(2,1)S(1)}, u32[]{:S(2)}, u32[]{:S(2)}) %collective-permute-start.4) | collective-permute-done | bytes 393248 | tf_op jit(solution)/shard_map/ppermute | solution.py:222
  66.9 1.8 %collective-permute-done.5 = bf16[384,512]{1,0:T(8,128)(2,1)S(1)} collective-permute-done((bf16[384,512]{1,0:T(8,128)(2,1)}, bf16[384,512]{1,0:T(8,128)(2,1)S(1)}, u32[]{:S(2)}, u32[]{:S(2)}) %collective-permute-start.5) | collective-permute-done | bytes 393248 | tf_op jit(solution)/shard_map/ppermute | solution.py:222
  68.7 1.4 %fusion.5 = (f16[384,512]{1,0:T(8,128)(2,1)S(1)}, f32[384,512]{1,0:T(8,128)S(1)}) fusion(bf16[384,512]{1,0:T(8,128)(2,1)S(1)} %collective-permute-done.5, bf16[384,512]{1,0:T(8,128)(2,1)S(1)} %collective-permute-done.4, f32[384,512]{1,0:T(8,128)} %get-tuple-element.50, bf16[384,512]{1,0:T(8,128)(2,1)S(1)} %collective-permute-done.3), kind=kLoop, calls=%fused_computation.20 | loop fusion | flops 1376256 | bytes 3145728 | tf_op jit(solution)/shard_map/convert_element_type | solution.py:292
  73.4 6.6 %all-to-all-start.2 = ((bf16[8,48,768]{2,1,0:T(8,128)(2,1)}), bf16[8,48,768]{2,1,0:T(8,128)(2,1)S(1)}, u32[]{:S(2)}, u32[]{:S(2)}) async-start(bf16[8,48,768]{2,1,0:T(8,128)(2,1)} %add_copies.1), calls=%async_computation.2 | async-start | bytes 1179648 | tf_op jit(solution)/shard_map/all_to_all | solution.py:30
  80.9 4.4 %collective-permute-start.9 = (f16[384,512]{1,0:T(8,128)(2,1)S(1)}, f16[384,512]{1,0:T(8,128)(2,1)S(1)}, u32[]{:S(2)}, u32[]{:S(2)}) collective-permute-start(f16[384,512]{1,0:T(8,128)(2,1)S(1)} %get-tuple-element.72), channel_id=1, source_target_pairs={{0,96},{32,0},{64,32},{96,64},{1,97},{33,1},{65,33},{97,65},{2,98}... | collective-permute-start | bytes 1179656 | tf_op jit(solution)/shard_map/ppermute | solution.py:222
  87.3 10.0 %all-to-all-done.2.whole = bf16[8,48,768]{2,1,0:T(8,128)(2,1)S(1)} async-done(((bf16[8,48,768]{2,1,0:T(8,128)(2,1)}), bf16[8,48,768]{2,1,0:T(8,128)(2,1)S(1)}, u32[]{:S(2)}, u32[]{:S(2)}) %all-to-all-start.2) | async-done | bytes 589856 | tf_op jit(solution)/shard_map/all_to_all | solution.py:30
  98.6 1.2 %collective-permute-start.13 = (bf16[4,48,768]{2,1,0:T(8,128)(2,1)S(1)}, bf16[4,48,768]{2,1,0:T(8,128)(2,1)S(1)}, u32[]{:S(2)}, u32[]{:S(2)}) collective-permute-start(bf16[4,48,768]{2,1,0:T(8,128)(2,1)S(1)} %get-tuple-element.57.refs_1_), channel_id=1, source_target_pairs={{0,2},{2,0},{1,3},{3,1},{4,6},{6,4},{5,7},{7,5},{8,10},{10,8},{9,1... | collective-permute-start | bytes 884744 | tf_op jit(solution)/shard_map/ppermute | solution.py:219
  100.7 5.0 %collective-permute-done.7 = f16[384,512]{1,0:T(8,128)(2,1)S(1)} collective-permute-done((f16[384,512]{1,0:T(8,128)(2,1)S(1)}, f16[384,512]{1,0:T(8,128)(2,1)S(1)}, u32[]{:S(2)}, u32[]{:S(2)}) %collective-permute-start.7) | collective-permute-done | bytes 393248 | tf_op jit(solution)/shard_map/ppermute | solution.py:222
  106.9 3.5 %collective-permute-done.13.refs_5_ = bf16[4,48,768]{2,1,0:T(8,128)(2,1)S(1)} collective-permute-done((bf16[4,48,768]{2,1,0:T(8,128)(2,1)S(1)}, bf16[4,48,768]{2,1,0:T(8,128)(2,1)S(1)}, u32[]{:S(2)}, u32[]{:S(2)}) %collective-permute-start.13) | collective-permute-done | bytes 294944 | tf_op jit(solution)/shard_map/ppermute | solution.py:219
  110.4 3.6 %collective-permute-start.14 = (bf16[4,48,768]{2,1,0:T(8,128)(2,1)S(1)}, bf16[4,48,768]{2,1,0:T(8,128)(2,1)S(1)}, u32[]{:S(2)}, u32[]{:S(2)}) collective-permute-start(bf16[4,48,768]{2,1,0:T(8,128)(2,1)S(1)} %collective-permute-done.12.refs_4_), channel_id=1, source_target_pairs={{0,1},{1,0},{2,3},{3,2},{4,5},{5,4},{6,7},{7,6},{8,9},{9,8},{10,11... | collective-permute-start | bytes 884744 | tf_op jit(solution)/shard_map/ppermute | solution.py:219
  114.0 1.2 %collective-permute-done.14.refs_6_ = bf16[4,48,768]{2,1,0:T(8,128)(2,1)S(1)} collective-permute-done((bf16[4,48,768]{2,1,0:T(8,128)(2,1)S(1)}, bf16[4,48,768]{2,1,0:T(8,128)(2,1)S(1)}, u32[]{:S(2)}, u32[]{:S(2)}) %collective-permute-start.14) | collective-permute-done | bytes 294944 | tf_op jit(solution)/shard_map/ppermute | solution.py:219
  115.7 3.4 %combine.1 = (f32[384,256]{1,0:T(8,128)}, f32[384,256]{1,0:T(8,128)}) custom-call(s32[2]{0:T(128)S(1)} %copy-done.7, f32[32,8,256]{2,1,0:T(8,128)S(1)} %copy-done.1, f32[384,256]{1,0:T(8,128)S(1)} %copy-done.3, f32[384,256]{1,0:T(8,128)S(1)} %copy-done.4, bf16[4,48,768]{2,1,0:T(8,128)(2,1)S(1)} %get-tuple-element.56.refs_0_, ...), custom_call_target="tpu_custom_call" | custom-call | flops 1207959552 | bytes 8388608 | tf_op jit(solution)/shard_map/combine/pallas_call | solution.py:327
  (51 shorter events, 13.5 us)
Async XLA Ops:
  0.6 27.6 %collective-permute-start = (bf16[1536,256]{1,0:T(8,128)(2,1)}, bf16[1536,256]{1,0:T(8,128)(2,1)S(1)}, u32[]{:S(2)}, u32[]{:S(2)}) collective-permute-start(bf16[1536,256]{1,0:T(8,128)(2,1)} %w0.1), channel_id=1, source_target_pairs={{0,2},{2,0},{1,3},{3,1},{4,6},{6,4},{5,7},{7,5},{8,10},{10,8},{9,1... | collective-permute-start | bytes 2359304 | tf_op jit(solution)/shard_map/ppermute | solution.py:219
  6.2 22.1 %all-to-all-start = ((f32[32,8,256]{2,1,0:T(8,128)}), f32[32,8,256]{2,1,0:T(8,128)S(1)}, u32[]{:S(2)}, u32[]{:S(2)}) async-start(f32[32,8,256]{2,1,0:T(8,128)} %get-tuple-element.36), calls=%async_computation | async-start | bytes 524288 | tf_op jit(solution)/shard_map/all_to_all | solution.py:30
  13.9 15.2 %collective-permute-start.1 = (bf16[1536,256]{1,0:T(8,128)(2,1)S(1)}, bf16[1536,256]{1,0:T(8,128)(2,1)S(1)}, u32[]{:S(2)}, u32[]{:S(2)}) collective-permute-start(bf16[1536,256]{1,0:T(8,128)(2,1)S(1)} %copy-done.2), channel_id=1, source_target_pairs={{0,1},{1,0},{2,3},{3,2},{4,5},{5,4},{6,7},{7,6},{8,9},{9,8},{10,11... | collective-permute-start | bytes 2359304 | tf_op jit(solution)/shard_map/ppermute | solution.py:219
  14.9 16.1 %copy-start.6 = (s32[2]{0:T(128)S(1)}, s32[2]{0:T(128)}, u32[]{:S(2)}) copy-start(s32[2]{0:T(128)} %pad_add_fusion.place) | copy-start | bytes 28
  28.3 2.8 %collective-permute-start.2 = (bf16[1536,256]{1,0:T(8,128)(2,1)S(1)}, bf16[1536,256]{1,0:T(8,128)(2,1)S(1)}, u32[]{:S(2)}, u32[]{:S(2)}) collective-permute-start(bf16[1536,256]{1,0:T(8,128)(2,1)S(1)} %collective-permute-done.w2), channel_id=1, source_target_pairs={{0,1},{1,0},{2,3},{3,2},{4,5},{5,4},{6,7},{7,6},{8,9},{9,8},{10,11... | collective-permute-start | bytes 2359304 | tf_op jit(solution)/shard_map/ppermute | solution.py:219
  35.3 36.6 %all-to-all-start.1 = ((bf16[8,48,768]{2,1,0:T(8,128)(2,1)}), bf16[8,48,768]{2,1,0:T(8,128)(2,1)S(1)}, u32[]{:S(2)}, u32[]{:S(2)}) async-start(bf16[8,48,768]{2,1,0:T(8,128)(2,1)} %embed.1.ready), calls=%async_computation.1 | async-start | bytes 1179648 | tf_op jit(solution)/shard_map/all_to_all | solution.py:30
  48.0 12.6 %collective-permute-start.3 = (bf16[384,512]{1,0:T(8,128)(2,1)}, bf16[384,512]{1,0:T(8,128)(2,1)S(1)}, u32[]{:S(2)}, u32[]{:S(2)}) collective-permute-start(bf16[384,512]{1,0:T(8,128)(2,1)} %get-tuple-element.51), channel_id=1, source_target_pairs={{0,32},{32,64},{64,96},{96,0},{1,33},{33,65},{65,97},{97,1},{2,34}... | collective-permute-start | bytes 1179656 | tf_op jit(solution)/shard_map/ppermute | solution.py:222
  48.6 18.3 %collective-permute-start.4 = (bf16[384,512]{1,0:T(8,128)(2,1)}, bf16[384,512]{1,0:T(8,128)(2,1)S(1)}, u32[]{:S(2)}, u32[]{:S(2)}) collective-permute-start(bf16[384,512]{1,0:T(8,128)(2,1)} %get-tuple-element.52), channel_id=1, source_target_pairs={{0,64},{32,96},{64,0},{96,32},{1,65},{33,97},{65,1},{97,33},{2,66}... | collective-permute-start | bytes 1179656 | tf_op jit(solution)/shard_map/ppermute | solution.py:222
  49.7 19.0 %collective-permute-start.5 = (bf16[384,512]{1,0:T(8,128)(2,1)}, bf16[384,512]{1,0:T(8,128)(2,1)S(1)}, u32[]{:S(2)}, u32[]{:S(2)}) collective-permute-start(bf16[384,512]{1,0:T(8,128)(2,1)} %get-tuple-element.53), channel_id=1, source_target_pairs={{0,96},{32,0},{64,32},{96,64},{1,97},{33,1},{65,33},{97,65},{2,98}... | collective-permute-start | bytes 1179656 | tf_op jit(solution)/shard_map/ppermute | solution.py:222
  70.0 10.7 %collective-permute-start.6 = (f16[384,512]{1,0:T(8,128)(2,1)S(1)}, f16[384,512]{1,0:T(8,128)(2,1)S(1)}, u32[]{:S(2)}, u32[]{:S(2)}) collective-permute-start(f16[384,512]{1,0:T(8,128)(2,1)S(1)} %get-tuple-element.70), channel_id=1, source_target_pairs={{0,128},{128,0},{1,129},{129,1},{2,130},{130,2},{3,131},{131,3},{4... | collective-permute-start | bytes 1179656 | tf_op jit(solution)/shard_map/ppermute | solution.py:219
  73.4 23.9 %all-to-all-start.2 = ((bf16[8,48,768]{2,1,0:T(8,128)(2,1)}), bf16[8,48,768]{2,1,0:T(8,128)(2,1)S(1)}, u32[]{:S(2)}, u32[]{:S(2)}) async-start(bf16[8,48,768]{2,1,0:T(8,128)(2,1)} %add_copies.1), calls=%async_computation.2 | async-start | bytes 1179648 | tf_op jit(solution)/shard_map/all_to_all | solution.py:30
  80.9 19.8 %collective-permute-start.9 = (f16[384,512]{1,0:T(8,128)(2,1)S(1)}, f16[384,512]{1,0:T(8,128)(2,1)S(1)}, u32[]{:S(2)}, u32[]{:S(2)}) collective-permute-start(f16[384,512]{1,0:T(8,128)(2,1)S(1)} %get-tuple-element.72), channel_id=1, source_target_pairs={{0,96},{32,0},{64,32},{96,64},{1,97},{33,1},{65,33},{97,65},{2,98}... | collective-permute-start | bytes 1179656 | tf_op jit(solution)/shard_map/ppermute | solution.py:222
  85.3 15.4 %collective-permute-start.8 = (f16[384,512]{1,0:T(8,128)(2,1)S(1)}, f16[384,512]{1,0:T(8,128)(2,1)S(1)}, u32[]{:S(2)}, u32[]{:S(2)}) collective-permute-start(f16[384,512]{1,0:T(8,128)(2,1)S(1)} %get-tuple-element.72), channel_id=1, source_target_pairs={{0,64},{32,96},{64,0},{96,32},{1,65},{33,97},{65,1},{97,33},{2,66}... | collective-permute-start | bytes 1179656 | tf_op jit(solution)/shard_map/ppermute | solution.py:222
  85.3 20.3 %collective-permute-start.7 = (f16[384,512]{1,0:T(8,128)(2,1)S(1)}, f16[384,512]{1,0:T(8,128)(2,1)S(1)}, u32[]{:S(2)}, u32[]{:S(2)}) collective-permute-start(f16[384,512]{1,0:T(8,128)(2,1)S(1)} %get-tuple-element.72), channel_id=1, source_target_pairs={{0,32},{32,64},{64,96},{96,0},{1,33},{33,65},{65,97},{97,1},{2,34}... | collective-permute-start | bytes 1179656 | tf_op jit(solution)/shard_map/ppermute | solution.py:222
  98.0 12.4 %collective-permute-start.12 = (bf16[4,48,768]{2,1,0:T(8,128)(2,1)S(1)}, bf16[4,48,768]{2,1,0:T(8,128)(2,1)S(1)}, u32[]{:S(2)}, u32[]{:S(2)}) collective-permute-start(bf16[4,48,768]{2,1,0:T(8,128)(2,1)S(1)} %get-tuple-element.56.refs_0_), channel_id=1, source_target_pairs={{0,2},{2,0},{1,3},{3,1},{4,6},{6,4},{5,7},{7,5},{8,10},{10,8},{9,1... | collective-permute-start | bytes 884744 | tf_op jit(solution)/shard_map/ppermute | solution.py:219
  98.6 17.1 %copy-start.1 = (f32[32,8,256]{2,1,0:T(8,128)S(1)}, f32[32,8,256]{2,1,0:T(8,128)}, u32[]{:S(2)}) copy-start(f32[32,8,256]{2,1,0:T(8,128)} %copy-done) | copy-start | bytes 786436
  98.6 17.1 %copy-start.3 = (f32[384,256]{1,0:T(8,128)S(1)}, f32[384,256]{1,0:T(8,128)}, u32[]{:S(2)}) copy-start(f32[384,256]{1,0:T(8,128)} %get-tuple-element.44.pa) | copy-start | bytes 1179652
  98.6 17.1 %copy-start.4 = (f32[384,256]{1,0:T(8,128)S(1)}, f32[384,256]{1,0:T(8,128)}, u32[]{:S(2)}) copy-start(f32[384,256]{1,0:T(8,128)} %get-tuple-element.45.pb) | copy-start | bytes 1179652
  98.6 17.1 %copy-start.7 = (s32[2]{0:T(128)S(1)}, s32[2]{0:T(128)}, u32[]{:S(2)}) copy-start(s32[2]{0:T(128)} %pad_add_fusion.place) | copy-start | bytes 28
  98.6 11.8 %collective-permute-start.13 = (bf16[4,48,768]{2,1,0:T(8,128)(2,1)S(1)}, bf16[4,48,768]{2,1,0:T(8,128)(2,1)S(1)}, u32[]{:S(2)}, u32[]{:S(2)}) collective-permute-start(bf16[4,48,768]{2,1,0:T(8,128)(2,1)S(1)} %get-tuple-element.57.refs_1_), channel_id=1, source_target_pairs={{0,2},{2,0},{1,3},{3,1},{4,6},{6,4},{5,7},{7,5},{8,10},{10,8},{9,1... | collective-permute-start | bytes 884744 | tf_op jit(solution)/shard_map/ppermute | solution.py:219
  105.7 8.4 %collective-permute-start.10 = (bf16[4,48,768]{2,1,0:T(8,128)(2,1)S(1)}, bf16[4,48,768]{2,1,0:T(8,128)(2,1)S(1)}, u32[]{:S(2)}, u32[]{:S(2)}) collective-permute-start(bf16[4,48,768]{2,1,0:T(8,128)(2,1)S(1)} %get-tuple-element.56.refs_0_), channel_id=1, source_target_pairs={{0,1},{1,0},{2,3},{3,2},{4,5},{5,4},{6,7},{7,6},{8,9},{9,8},{10,11... | collective-permute-start | bytes 884744 | tf_op jit(solution)/shard_map/ppermute | solution.py:219
  106.5 7.5 %collective-permute-start.11 = (bf16[4,48,768]{2,1,0:T(8,128)(2,1)S(1)}, bf16[4,48,768]{2,1,0:T(8,128)(2,1)S(1)}, u32[]{:S(2)}, u32[]{:S(2)}) collective-permute-start(bf16[4,48,768]{2,1,0:T(8,128)(2,1)S(1)} %get-tuple-element.57.refs_1_), channel_id=1, source_target_pairs={{0,1},{1,0},{2,3},{3,2},{4,5},{5,4},{6,7},{7,6},{8,9},{9,8},{10,11... | collective-permute-start | bytes 884744 | tf_op jit(solution)/shard_map/ppermute | solution.py:219
  110.4 4.8 %collective-permute-start.14 = (bf16[4,48,768]{2,1,0:T(8,128)(2,1)S(1)}, bf16[4,48,768]{2,1,0:T(8,128)(2,1)S(1)}, u32[]{:S(2)}, u32[]{:S(2)}) collective-permute-start(bf16[4,48,768]{2,1,0:T(8,128)(2,1)S(1)} %collective-permute-done.12.refs_4_), channel_id=1, source_target_pairs={{0,1},{1,0},{2,3},{3,2},{4,5},{5,4},{6,7},{7,6},{8,9},{9,8},{10,11... | collective-permute-start | bytes 884744 | tf_op jit(solution)/shard_map/ppermute | solution.py:219
  114.0 1.6 %collective-permute-start.15 = (bf16[4,48,768]{2,1,0:T(8,128)(2,1)S(1)}, bf16[4,48,768]{2,1,0:T(8,128)(2,1)S(1)}, u32[]{:S(2)}, u32[]{:S(2)}) collective-permute-start(bf16[4,48,768]{2,1,0:T(8,128)(2,1)S(1)} %collective-permute-done.13.refs_5_), channel_id=1, source_target_pairs={{0,1},{1,0},{2,3},{3,2},{4,5},{5,4},{6,7},{7,6},{8,9},{9,8},{10,11... | collective-permute-start | bytes 884744 | tf_op jit(solution)/shard_map/ppermute | solution.py:219
  (5 other events, 22.7 us)

commit v8 on v7

--- a/solution.py
+++ b/solution.py
@@ -86,7 +86,7 @@
     return ma, ra, mb, rb, (t[4:5] - ma * mb) * ra * rb
 
 
-def embed(place, sums, v, w0, w1, w2, w3, y, na, nb):
+def embed(place, sums, v, w0, w1, w2, w3, ready, y, na, nb):
     q = place[0]
     ws = (w0, w1, w2, w3)
     for j, wj in enumerate(ws):
@@ -124,7 +124,7 @@
         out[...] = jnp.concatenate([v, centre, jnp.zeros((112, DEPTH), bf16)], axis=0).T
 
 
-def correlate(place, sums, pa, pb, ta, tb, ready, u0, u1, u2, u3, xs, xpa, xpb, xa, xb, x0, x1, x2, x3, sem, out_sem):
+def correlate(place, sums, pa, pb, ta, tb, u0, u1, u2, u3, xs, xpa, xpb, xa, xb, x0, x1, x2, x3, sem, out_sem):
     q, yy = place[0], place[1]
     stats = [
         pltpu.make_async_copy(src, dst, sem.at[8 + i])
@@ -251,22 +251,10 @@
     sums, ta, tb, v_quarter, w_x = lax.optimization_barrier((sums, ta, tb, v_quarter, w_x))
     w_xc = swap(w_x, "c")
 
-    y_part = call(
-        embed,
-        shape((8,) + PIECE, bf16),
-        [SMEM] + [VMEM] * 6,
-        16 * ROWS * DEPTH * BLOCK // 2,
-        7 * 2**20,
-        [pltpu.VMEM((QUARTER, 4 * BLOCK), bf16)] * 2,
-        name="embed",
-        vmem=20,
-    )(place, sums, v_quarter, w, w_c, w_x, w_xc)
-    y_parts = exchange(y_part, "z")
-
     u_parts = call(
         correlate,
         (shape((SHARE, 2 * BLOCK), f32),) + (shape((SHARE, 2 * BLOCK), bf16),) * 3,
-        [SMEM] + [ANY] * 6,
+        [SMEM] + [ANY] * 5,
         4 * ROWS * DEPTH * BLOCK,
         6 * 2**20,
         [
@@ -284,7 +272,19 @@
         ],
         out_specs=(ANY,) * 4,
         name="correlate",
-    )(place, sums, pa, pb, ta, tb, y_part)
+    )(place, sums, pa, pb, ta, tb)
+    y_part = call(
+        embed,
+        shape((8,) + PIECE, bf16),
+        [SMEM] + [VMEM] * 6 + [ANY],
+        16 * ROWS * DEPTH * BLOCK // 2,
+        7 * 2**20,
+        [pltpu.VMEM((QUARTER, 4 * BLOCK), bf16)] * 2,
+        name="embed",
+        vmem=20,
+    )(place, sums, v_quarter, w, w_c, w_x, w_xc, u_parts[0])
+    y_parts = exchange(y_part, "z")
+
     u = u_parts[0]
     for s in (1, 2, 3):
         u = u + along_y(u_parts[s], s).astype(f32)

time: 121 us -> 120 us (level)
  the two profiles are of different devices: /device:TPU:1 before, /device:TPU:25 now
where the time goes in v8:
time: 120 us
  waiting for transfers between devices  52.3 us (44%)
  starting transfers between devices  36.6 us (30%)
  Pallas kernels  20.7 us (17%)
  local copies, waits for them, and re-layouts  5.71 us (5%)
  other arithmetic  3.57 us (3%)
    all_to_all x3, starting transfers between devices, exchange(): return lax.all_to_all(blocks, axes, split_axis=0, concat_axis=0, tiled=True)  22.6 us
    all_to_all x3, waiting for transfers between devices, exchange(): return lax.all_to_all(blocks, axes, split_axis=0, concat_axis=0, tiled=True)  21.8 us
    ppermute x6, waiting for transfers between devices, along_y(): return lax.ppermute(t, 'y', [(i, (i + s) % 4) for i in range(4)])  21.4 us
    ppermute x10, starting transfers between devices, swap(): return lax.ppermute(t, axis, SWAP)  9.14 us
    ppermute x10, waiting for transfers between devices, swap(): return lax.ppermute(t, axis, SWAP)  9.11 us
    ppermute x6, starting transfers between devices, along_y(): return lax.ppermute(t, 'y', [(i, (i + s) % 4) for i in range(4)])  4.91 us
    pallas_call x1, Pallas kernels, local(): call(correlate, (shape((SHARE, 2 * BLOCK), f32),) + (shape((SHARE, 2 * BL...  4.7 us
    unnamed x24, local copies, waits for them, and re-layouts  4.52 us
  transfers between devices with their start and end apart: 19, of which 10 were waited for; matrix products, arithmetic and copies ran while one was open for 4% of the time, Pallas kernels for 12%

profile of v8, /device:TPU:25, one launch (start us, length us, event | category | flops | bytes accessed | tf_op | source)
XLA Modules:
  0.0 119.7 jit_solution(2659727947884147581)
XLA Ops:
  0.6 1.3 %collective-permute-start = (bf16[1536,256]{1,0:T(8,128)(2,1)}, bf16[1536,256]{1,0:T(8,128)(2,1)S(1)}, u32[]{:S(2)}, u32[]{:S(2)}) collective-permute-start(bf16[1536,256]{1,0:T(8,128)(2,1)} %w0.1), channel_id=1, source_target_pairs={{0,2},{2,0},{1,3},{3,1},{4,6},{6,4},{5,7},{7,5},{8,10},{10,8},{9,1... | collective-permute-start | bytes 2359304 | tf_op jit(solution)/shard_map/ppermute | solution.py:219
  1.9 3.4 %project.1 = (f32[384,256]{1,0:T(8,128)}, f32[384,256]{1,0:T(8,128)}, f32[32,8,256]{2,1,0:T(8,128)}) custom-call(bf16[384,1536]{1,0:T(8,128)(2,1)} %va.2, bf16[384,1536]{1,0:T(8,128)(2,1)} %vb.2, bf16[1536,256]{1,0:T(8,128)(2,1)} %w0.1), custom_call_target="tpu_custom_call" | custom-call | flops 603979776 | bytes 4194304 | tf_op jit(solution)/shard_map/project/pallas_call | solution.py:227
  5.3 7.6 %all-to-all-start = ((f32[32,8,256]{2,1,0:T(8,128)}), f32[32,8,256]{2,1,0:T(8,128)S(1)}, u32[]{:S(2)}, u32[]{:S(2)}) async-start(f32[32,8,256]{2,1,0:T(8,128)} %get-tuple-element.36), calls=%async_computation | async-start | bytes 524288 | tf_op jit(solution)/shard_map/all_to_all | solution.py:30
  14.1 4.0 %turn.1 = (bf16[1536,512]{1,0:T(8,128)(2,1)}, bf16[1536,512]{1,0:T(8,128)(2,1)}, bf16[192,1536]{1,0:T(8,128)(2,1)}) custom-call(s32[2]{0:T(128)} %pad_add_fusion.place, bf16[384,1536]{1,0:T(8,128)(2,1)} %va.2, bf16[384,1536]{1,0:T(8,128)(2,1)} %vb.2), custom_call_target="tpu_custom_call" | custom-call | flops 10485760 | bytes 6291456 | tf_op jit(solution)/shard_map/turn/pallas_call | solution.py:243
  18.1 7.2 %all-to-all-done.sums = f32[32,8,256]{2,1,0:T(8,128)S(1)} async-done(((f32[32,8,256]{2,1,0:T(8,128)}), f32[32,8,256]{2,1,0:T(8,128)S(1)}, u32[]{:S(2)}, u32[]{:S(2)}) %all-to-all-start) | async-done | bytes 262176 | tf_op jit(solution)/shard_map/all_to_all | solution.py:30
  25.9 4.7 %correlate.1 = (f32[384,512]{1,0:T(8,128)}, bf16[384,512]{1,0:T(8,128)(2,1)}, bf16[384,512]{1,0:T(8,128)(2,1)}, bf16[384,512]{1,0:T(8,128)(2,1)}) custom-call(s32[2]{0:T(128)} %pad_add_fusion.place, f32[32,8,256]{2,1,0:T(8,128)} %copy-done, f32[384,256]{1,0:T(8,128)} %get-tuple-element.44.pa, f32[384,256]{1,0:T(8,128)} %get-tuple-element.45.pb, ...), custom_call_target="tpu_custom_call" | custom-call | flops 603979776 | bytes 6291456 | tf_op jit(solution)/shard_map/correlate/pallas_call | solution.py:254
  31.6 1.1 copy-done.4
  33.8 3.2 %embed.1 = bf16[8,48,768]{2,1,0:T(8,128)(2,1)} custom-call(s32[2]{0:T(128)S(1)} %copy-done.9, f32[32,8,256]{2,1,0:T(8,128)S(1)} %copy-done.1, bf16[192,1536]{1,0:T(8,128)(2,1)S(1)} %copy-done.8, bf16[1536,256]{1,0:T(8,128)(2,1)S(1)} %copy-done.3, bf16[1536,256]{1,0:T(8,128)(2,1)S(1)} %collective-permute-done.1.w1, ...), custom_call_target="tpu_custom_call" | custom-call | flops 1207959552 | bytes 7340032 | tf_op jit(solution)/shard_map/embed/pallas_call | solution.py:276
  37.0 8.3 %all-to-all-start.1 = ((bf16[8,48,768]{2,1,0:T(8,128)(2,1)}), bf16[8,48,768]{2,1,0:T(8,128)(2,1)S(1)}, u32[]{:S(2)}, u32[]{:S(2)}) async-start(bf16[8,48,768]{2,1,0:T(8,128)(2,1)} %embed.1), calls=%async_computation.1 | async-start | bytes 1179648 | tf_op jit(solution)/shard_map/all_to_all | solution.py:30
  45.3 2.3 %collective-permute-start.3 = (bf16[384,512]{1,0:T(8,128)(2,1)}, bf16[384,512]{1,0:T(8,128)(2,1)S(1)}, u32[]{:S(2)}, u32[]{:S(2)}) collective-permute-start(bf16[384,512]{1,0:T(8,128)(2,1)} %get-tuple-element.51), channel_id=1, source_target_pairs={{0,32},{32,64},{64,96},{96,0},{1,33},{33,65},{65,97},{97,1},{2,34}... | collective-permute-start | bytes 1179656 | tf_op jit(solution)/shard_map/ppermute | solution.py:222
  48.7 7.3 %collective-permute-done.3 = bf16[384,512]{1,0:T(8,128)(2,1)S(1)} collective-permute-done((bf16[384,512]{1,0:T(8,128)(2,1)}, bf16[384,512]{1,0:T(8,128)(2,1)S(1)}, u32[]{:S(2)}, u32[]{:S(2)}) %collective-permute-start.3) | collective-permute-done | bytes 393248 | tf_op jit(solution)/shard_map/ppermute | solution.py:222
  56.0 2.8 %collective-permute-done.4 = bf16[384,512]{1,0:T(8,128)(2,1)S(1)} collective-permute-done((bf16[384,512]{1,0:T(8,128)(2,1)}, bf16[384,512]{1,0:T(8,128)(2,1)S(1)}, u32[]{:S(2)}, u32[]{:S(2)}) %collective-permute-start.4) | collective-permute-done | bytes 393248 | tf_op jit(solution)/shard_map/ppermute | solution.py:222
  58.7 10.0 %collective-permute-done.5 = bf16[384,512]{1,0:T(8,128)(2,1)S(1)} collective-permute-done((bf16[384,512]{1,0:T(8,128)(2,1)}, bf16[384,512]{1,0:T(8,128)(2,1)S(1)}, u32[]{:S(2)}, u32[]{:S(2)}) %collective-permute-start.5) | collective-permute-done | bytes 393248 | tf_op jit(solution)/shard_map/ppermute | solution.py:222
  72.4 6.6 %all-to-all-start.2 = ((bf16[8,48,768]{2,1,0:T(8,128)(2,1)}), bf16[8,48,768]{2,1,0:T(8,128)(2,1)S(1)}, u32[]{:S(2)}, u32[]{:S(2)}) async-start(bf16[8,48,768]{2,1,0:T(8,128)(2,1)} %add_copies.1), calls=%async_computation.2 | async-start | bytes 1179648 | tf_op jit(solution)/shard_map/all_to_all | solution.py:30
  79.1 1.7 %collective-permute-done.6 = f16[384,512]{1,0:T(8,128)(2,1)S(1)} collective-permute-done((f16[384,512]{1,0:T(8,128)(2,1)S(1)}, f16[384,512]{1,0:T(8,128)(2,1)S(1)}, u32[]{:S(2)}, u32[]{:S(2)}) %collective-permute-start.6) | collective-permute-done | bytes 393248 | tf_op jit(solution)/shard_map/ppermute | solution.py:219
  83.8 14.6 %all-to-all-done.2.whole = bf16[8,48,768]{2,1,0:T(8,128)(2,1)S(1)} async-done(((bf16[8,48,768]{2,1,0:T(8,128)(2,1)}), bf16[8,48,768]{2,1,0:T(8,128)(2,1)S(1)}, u32[]{:S(2)}, u32[]{:S(2)}) %all-to-all-start.2) | async-done | bytes 589856 | tf_op jit(solution)/shard_map/all_to_all | solution.py:30
  100.9 1.3 %collective-permute-done.9 = f16[384,512]{1,0:T(8,128)(2,1)} collective-permute-done((f16[384,512]{1,0:T(8,128)(2,1)S(1)}, f16[384,512]{1,0:T(8,128)(2,1)}, u32[]{:S(2)}, u32[]{:S(2)}) %collective-permute-start.9) | collective-permute-done | bytes 393248 | tf_op jit(solution)/shard_map/ppermute | solution.py:222
  104.0 1.3 %fusion.1 = (bf16[384,512]{1,0:T(8,128)(2,1)S(1)}, bf16[384,512]{1,0:T(8,128)(2,1)S(1)}, bf16[384,512]{1,0:T(8,128)(2,1)S(1)}, bf16[384,512]{1,0:T(8,128)(2,1)S(1)}) fusion(f16[384,512]{1,0:T(8,128)(2,1)S(1)} %collective-permute-done.7, f16[384,512]{1,0:T(8,128)(2,1)} %collective-permute-done.8), kind=kLoop, calls=%fused_computation.9 | loop fusion | flops 2359296 | bytes 2359296 | tf_op jit(solution)/shard_map/convert_element_type | solution.py:322
  105.3 2.2 %collective-permute-done.13.refs_5_ = bf16[4,48,768]{2,1,0:T(8,128)(2,1)S(1)} collective-permute-done((bf16[4,48,768]{2,1,0:T(8,128)(2,1)S(1)}, bf16[4,48,768]{2,1,0:T(8,128)(2,1)S(1)}, u32[]{:S(2)}, u32[]{:S(2)}) %collective-permute-start.13) | collective-permute-done | bytes 294944 | tf_op jit(solution)/shard_map/ppermute | solution.py:219
  107.5 2.3 %collective-permute-start.15 = (bf16[4,48,768]{2,1,0:T(8,128)(2,1)S(1)}, bf16[4,48,768]{2,1,0:T(8,128)(2,1)S(1)}, u32[]{:S(2)}, u32[]{:S(2)}) collective-permute-start(bf16[4,48,768]{2,1,0:T(8,128)(2,1)S(1)} %collective-permute-done.13.refs_5_), channel_id=1, source_target_pairs={{0,1},{1,0},{2,3},{3,2},{4,5},{5,4},{6,7},{7,6},{8,9},{9,8},{10,11... | collective-permute-start | bytes 884744 | tf_op jit(solution)/shard_map/ppermute | solution.py:219
  109.8 4.0 %collective-permute-done.12.refs_4_ = bf16[4,48,768]{2,1,0:T(8,128)(2,1)S(1)} collective-permute-done((bf16[4,48,768]{2,1,0:T(8,128)(2,1)S(1)}, bf16[4,48,768]{2,1,0:T(8,128)(2,1)S(1)}, u32[]{:S(2)}, u32[]{:S(2)}) %collective-permute-start.12) | collective-permute-done | bytes 294944 | tf_op jit(solution)/shard_map/ppermute | solution.py:219
  113.8 1.4 %collective-permute-start.14 = (bf16[4,48,768]{2,1,0:T(8,128)(2,1)S(1)}, bf16[4,48,768]{2,1,0:T(8,128)(2,1)S(1)}, u32[]{:S(2)}, u32[]{:S(2)}) collective-permute-start(bf16[4,48,768]{2,1,0:T(8,128)(2,1)S(1)} %collective-permute-done.12.refs_4_), channel_id=1, source_target_pairs={{0,1},{1,0},{2,3},{3,2},{4,5},{5,4},{6,7},{7,6},{8,9},{9,8},{10,11... | collective-permute-start | bytes 884744 | tf_op jit(solution)/shard_map/ppermute | solution.py:219
  115.2 1.2 collective-permute-done.14.refs_6_
  116.4 3.3 %combine.1 = (f32[384,256]{1,0:T(8,128)}, f32[384,256]{1,0:T(8,128)}) custom-call(s32[2]{0:T(128)S(1)} %copy-done.9, f32[32,8,256]{2,1,0:T(8,128)S(1)} %copy-done.2, f32[384,256]{1,0:T(8,128)S(1)} %copy-done.6, f32[384,256]{1,0:T(8,128)S(1)} %copy-done.7, bf16[4,48,768]{2,1,0:T(8,128)(2,1)S(1)} %get-tuple-element.56.refs_0_, ...), custom_call_target="tpu_custom_call" | custom-call | flops 1207959552 | bytes 8388608 | tf_op jit(solution)/shard_map/combine/pallas_call | solution.py:327
  (55 shorter events, 15.8 us)
Async XLA Ops:
  0.6 12.3 %copy-start.3 = (bf16[1536,256]{1,0:T(8,128)(2,1)S(1)}, bf16[1536,256]{1,0:T(8,128)(2,1)}, u32[]{:S(2)}) copy-start(bf16[1536,256]{1,0:T(8,128)(2,1)} %w0.1) | copy-start | bytes 2359300
  0.6 24.6 %collective-permute-start = (bf16[1536,256]{1,0:T(8,128)(2,1)}, bf16[1536,256]{1,0:T(8,128)(2,1)S(1)}, u32[]{:S(2)}, u32[]{:S(2)}) collective-permute-start(bf16[1536,256]{1,0:T(8,128)(2,1)} %w0.1), channel_id=1, source_target_pairs={{0,2},{2,0},{1,3},{3,1},{4,6},{6,4},{5,7},{7,5},{8,10},{10,8},{9,1... | collective-permute-start | bytes 2359304 | tf_op jit(solution)/shard_map/ppermute | solution.py:219
  5.3 19.9 %all-to-all-start = ((f32[32,8,256]{2,1,0:T(8,128)}), f32[32,8,256]{2,1,0:T(8,128)S(1)}, u32[]{:S(2)}, u32[]{:S(2)}) async-start(f32[32,8,256]{2,1,0:T(8,128)} %get-tuple-element.36), calls=%async_computation | async-start | bytes 524288 | tf_op jit(solution)/shard_map/all_to_all | solution.py:30
  13.0 17.6 %collective-permute-start.1 = (bf16[1536,256]{1,0:T(8,128)(2,1)S(1)}, bf16[1536,256]{1,0:T(8,128)(2,1)S(1)}, u32[]{:S(2)}, u32[]{:S(2)}) collective-permute-start(bf16[1536,256]{1,0:T(8,128)(2,1)S(1)} %copy-done.3), channel_id=1, source_target_pairs={{0,1},{1,0},{2,3},{3,2},{4,5},{5,4},{6,7},{7,6},{8,9},{9,8},{10,11... | collective-permute-start | bytes 2359304 | tf_op jit(solution)/shard_map/ppermute | solution.py:219
  25.2 5.4 %collective-permute-start.2 = (bf16[1536,256]{1,0:T(8,128)(2,1)S(1)}, bf16[1536,256]{1,0:T(8,128)(2,1)S(1)}, u32[]{:S(2)}, u32[]{:S(2)}) collective-permute-start(bf16[1536,256]{1,0:T(8,128)(2,1)S(1)} %collective-permute-done.w2), channel_id=1, source_target_pairs={{0,1},{1,0},{2,3},{3,2},{4,5},{5,4},{6,7},{7,6},{8,9},{9,8},{10,11... | collective-permute-start | bytes 2359304 | tf_op jit(solution)/shard_map/ppermute | solution.py:219
  37.0 31.8 %copy-start.5 = (f32[384,512]{1,0:T(8,128)S(1)}, f32[384,512]{1,0:T(8,128)}, u32[]{:S(2)}) copy-start(f32[384,512]{1,0:T(8,128)} %get-tuple-element.50.ready) | copy-start | bytes 2359300
  37.0 33.8 %all-to-all-start.1 = ((bf16[8,48,768]{2,1,0:T(8,128)(2,1)}), bf16[8,48,768]{2,1,0:T(8,128)(2,1)S(1)}, u32[]{:S(2)}, u32[]{:S(2)}) async-start(bf16[8,48,768]{2,1,0:T(8,128)(2,1)} %embed.1), calls=%async_computation.1 | async-start | bytes 1179648 | tf_op jit(solution)/shard_map/all_to_all | solution.py:30
  45.3 10.7 %collective-permute-start.3 = (bf16[384,512]{1,0:T(8,128)(2,1)}, bf16[384,512]{1,0:T(8,128)(2,1)S(1)}, u32[]{:S(2)}, u32[]{:S(2)}) collective-permute-start(bf16[384,512]{1,0:T(8,128)(2,1)} %get-tuple-element.51), channel_id=1, source_target_pairs={{0,32},{32,64},{64,96},{96,0},{1,33},{33,65},{65,97},{97,1},{2,34}... | collective-permute-start | bytes 1179656 | tf_op jit(solution)/shard_map/ppermute | solution.py:222
  47.6 11.1 %collective-permute-start.4 = (bf16[384,512]{1,0:T(8,128)(2,1)}, bf16[384,512]{1,0:T(8,128)(2,1)S(1)}, u32[]{:S(2)}, u32[]{:S(2)}) collective-permute-start(bf16[384,512]{1,0:T(8,128)(2,1)} %get-tuple-element.52), channel_id=1, source_target_pairs={{0,64},{32,96},{64,0},{96,32},{1,65},{33,97},{65,1},{97,33},{2,66}... | collective-permute-start | bytes 1179656 | tf_op jit(solution)/shard_map/ppermute | solution.py:222
  47.9 20.9 %collective-permute-start.5 = (bf16[384,512]{1,0:T(8,128)(2,1)}, bf16[384,512]{1,0:T(8,128)(2,1)S(1)}, u32[]{:S(2)}, u32[]{:S(2)}) collective-permute-start(bf16[384,512]{1,0:T(8,128)(2,1)} %get-tuple-element.53), channel_id=1, source_target_pairs={{0,96},{32,0},{64,32},{96,64},{1,97},{33,1},{65,33},{97,65},{2,98}... | collective-permute-start | bytes 1179656 | tf_op jit(solution)/shard_map/ppermute | solution.py:222
  69.0 11.8 %collective-permute-start.6 = (f16[384,512]{1,0:T(8,128)(2,1)S(1)}, f16[384,512]{1,0:T(8,128)(2,1)S(1)}, u32[]{:S(2)}, u32[]{:S(2)}) collective-permute-start(f16[384,512]{1,0:T(8,128)(2,1)S(1)} %get-tuple-element.70), channel_id=1, source_target_pairs={{0,128},{128,0},{1,129},{129,1},{2,130},{130,2},{3,131},{131,3},{4... | collective-permute-start | bytes 1179656 | tf_op jit(solution)/shard_map/ppermute | solution.py:219
  72.4 26.0 %all-to-all-start.2 = ((bf16[8,48,768]{2,1,0:T(8,128)(2,1)}), bf16[8,48,768]{2,1,0:T(8,128)(2,1)S(1)}, u32[]{:S(2)}, u32[]{:S(2)}) async-start(bf16[8,48,768]{2,1,0:T(8,128)(2,1)} %add_copies.1), calls=%async_computation.2 | async-start | bytes 1179648 | tf_op jit(solution)/shard_map/all_to_all | solution.py:30
  80.9 19.9 %collective-permute-start.7 = (f16[384,512]{1,0:T(8,128)(2,1)S(1)}, f16[384,512]{1,0:T(8,128)(2,1)S(1)}, u32[]{:S(2)}, u32[]{:S(2)}) collective-permute-start(f16[384,512]{1,0:T(8,128)(2,1)S(1)} %get-tuple-element.72), channel_id=1, source_target_pairs={{0,32},{32,64},{64,96},{96,0},{1,33},{33,65},{65,97},{97,1},{2,34}... | collective-permute-start | bytes 1179656 | tf_op jit(solution)/shard_map/ppermute | solution.py:222
  81.0 19.8 %collective-permute-start.8 = (f16[384,512]{1,0:T(8,128)(2,1)S(1)}, f16[384,512]{1,0:T(8,128)(2,1)}, u32[]{:S(2)}, u32[]{:S(2)}) collective-permute-start(f16[384,512]{1,0:T(8,128)(2,1)S(1)} %get-tuple-element.72), channel_id=1, source_target_pairs={{0,64},{32,96},{64,0},{96,32},{1,65},{33,97},{65,1},{97,33},{2,66}... | collective-permute-start | bytes 1179656 | tf_op jit(solution)/shard_map/ppermute | solution.py:222
  81.4 20.8 %collective-permute-start.9 = (f16[384,512]{1,0:T(8,128)(2,1)S(1)}, f16[384,512]{1,0:T(8,128)(2,1)}, u32[]{:S(2)}, u32[]{:S(2)}) collective-permute-start(f16[384,512]{1,0:T(8,128)(2,1)S(1)} %get-tuple-element.72), channel_id=1, source_target_pairs={{0,96},{32,0},{64,32},{96,64},{1,97},{33,1},{65,33},{97,65},{2,98}... | collective-permute-start | bytes 1179656 | tf_op jit(solution)/shard_map/ppermute | solution.py:222
  99.1 8.3 %collective-permute-start.13 = (bf16[4,48,768]{2,1,0:T(8,128)(2,1)S(1)}, bf16[4,48,768]{2,1,0:T(8,128)(2,1)S(1)}, u32[]{:S(2)}, u32[]{:S(2)}) collective-permute-start(bf16[4,48,768]{2,1,0:T(8,128)(2,1)S(1)} %get-tuple-element.57.refs_1_), channel_id=1, source_target_pairs={{0,2},{2,0},{1,3},{3,1},{4,6},{6,4},{5,7},{7,5},{8,10},{10,8},{9,1... | collective-permute-start | bytes 884744 | tf_op jit(solution)/shard_map/ppermute | solution.py:219
  99.7 16.6 %copy-start.2 = (f32[32,8,256]{2,1,0:T(8,128)S(1)}, f32[32,8,256]{2,1,0:T(8,128)}, u32[]{:S(2)}) copy-start(f32[32,8,256]{2,1,0:T(8,128)} %copy-done) | copy-start | bytes 786436
  99.7 16.6 %copy-start.6 = (f32[384,256]{1,0:T(8,128)S(1)}, f32[384,256]{1,0:T(8,128)}, u32[]{:S(2)}) copy-start(f32[384,256]{1,0:T(8,128)} %get-tuple-element.44.pa) | copy-start | bytes 1179652
  99.7 16.6 %copy-start.7 = (f32[384,256]{1,0:T(8,128)S(1)}, f32[384,256]{1,0:T(8,128)}, u32[]{:S(2)}) copy-start(f32[384,256]{1,0:T(8,128)} %get-tuple-element.45.pb) | copy-start | bytes 1179652
  99.7 14.0 %collective-permute-start.12 = (bf16[4,48,768]{2,1,0:T(8,128)(2,1)S(1)}, bf16[4,48,768]{2,1,0:T(8,128)(2,1)S(1)}, u32[]{:S(2)}, u32[]{:S(2)}) collective-permute-start(bf16[4,48,768]{2,1,0:T(8,128)(2,1)S(1)} %get-tuple-element.56.refs_0_), channel_id=1, source_target_pairs={{0,2},{2,0},{1,3},{3,1},{4,6},{6,4},{5,7},{7,5},{8,10},{10,8},{9,1... | collective-permute-start | bytes 884744 | tf_op jit(solution)/shard_map/ppermute | solution.py:219
  103.3 11.8 %collective-permute-start.10 = (bf16[4,48,768]{2,1,0:T(8,128)(2,1)S(1)}, bf16[4,48,768]{2,1,0:T(8,128)(2,1)S(1)}, u32[]{:S(2)}, u32[]{:S(2)}) collective-permute-start(bf16[4,48,768]{2,1,0:T(8,128)(2,1)S(1)} %get-tuple-element.56.refs_0_), channel_id=1, source_target_pairs={{0,1},{1,0},{2,3},{3,2},{4,5},{5,4},{6,7},{7,6},{8,9},{9,8},{10,11... | collective-permute-start | bytes 884744 | tf_op jit(solution)/shard_map/ppermute | solution.py:219
  103.9 11.2 %collective-permute-start.11 = (bf16[4,48,768]{2,1,0:T(8,128)(2,1)S(1)}, bf16[4,48,768]{2,1,0:T(8,128)(2,1)S(1)}, u32[]{:S(2)}, u32[]{:S(2)}) collective-permute-start(bf16[4,48,768]{2,1,0:T(8,128)(2,1)S(1)} %get-tuple-element.57.refs_1_), channel_id=1, source_target_pairs={{0,1},{1,0},{2,3},{3,2},{4,5},{5,4},{6,7},{7,6},{8,9},{9,8},{10,11... | collective-permute-start | bytes 884744 | tf_op jit(solution)/shard_map/ppermute | solution.py:219
  107.5 7.7 %collective-permute-start.15 = (bf16[4,48,768]{2,1,0:T(8,128)(2,1)S(1)}, bf16[4,48,768]{2,1,0:T(8,128)(2,1)S(1)}, u32[]{:S(2)}, u32[]{:S(2)}) collective-permute-start(bf16[4,48,768]{2,1,0:T(8,128)(2,1)S(1)} %collective-permute-done.13.refs_5_), channel_id=1, source_target_pairs={{0,1},{1,0},{2,3},{3,2},{4,5},{5,4},{6,7},{7,6},{8,9},{9,8},{10,11... | collective-permute-start | bytes 884744 | tf_op jit(solution)/shard_map/ppermute | solution.py:219
  113.8 2.6 %collective-permute-start.14 = (bf16[4,48,768]{2,1,0:T(8,128)(2,1)S(1)}, bf16[4,48,768]{2,1,0:T(8,128)(2,1)S(1)}, u32[]{:S(2)}, u32[]{:S(2)}) collective-permute-start(bf16[4,48,768]{2,1,0:T(8,128)(2,1)S(1)} %collective-permute-done.12.refs_4_), channel_id=1, source_target_pairs={{0,1},{1,0},{2,3},{3,2},{4,5},{5,4},{6,7},{7,6},{8,9},{9,8},{10,11... | collective-permute-start | bytes 884744 | tf_op jit(solution)/shard_map/ppermute | solution.py:219
  (7 other events, 9.9 us)

commit v9 on v5

--- a/solution.py
+++ b/solution.py
@@ -207,6 +207,7 @@
         out_shape=jax.ShapeDtypeStruct((8, 128), f32),
         in_specs=[ANY],
         out_specs=VMEM,
+        compiler_params=pltpu.CompilerParams(vmem_limit_bytes=4 * 2**20),
         cost_estimate=pl.CostEstimate(flops=us * 10**9, bytes_accessed=0, transcendentals=0),
         name="mark",
     )(t)

time: 113 us -> 112 us (level)
  waiting for transfers between devices: 41.6 us -> 44.3 us
  local copies, waits for them, and re-layouts: 5.71 us -> 3.18 us
  Pallas kernels: 20.7 us -> 19.5 us
    all_to_all x3, waiting for transfers between devices: 28.6 us -> 30.9 us  [exchange(): return lax.all_to_all(blocks, axes, split_axis=0, concat_axis=0, tiled=True)]
    unnamed x22 -> x18, local copies, waits for them, and re-layouts: 2.73 us -> 1.37 us
    pallas_call x2, Pallas kernels: 1.19 us -> 0.01 us  [arrival(): pl.pallas_call(mark, out_shape=jax.ShapeDtypeStruct((8, 128), f32), in_sp...]
  transfers between devices with their start and end apart: 21 -> 21, of which waited for: 9 -> 10; matrix products, arithmetic and copies ran while one was open for 6% -> 5% of each run, Pallas kernels for 15% -> 15%
where the time goes in v9:
time: 112 us; the launch traced here: 111 us
  waiting for transfers between devices  44.3 us (40%)
  starting transfers between devices  38.5 us (34%)
  Pallas kernels  19.5 us (17%)
  other arithmetic  4.72 us (4%)
  local copies, waits for them, and re-layouts  3.18 us (3%)
    all_to_all x3, waiting for transfers between devices, exchange(): return lax.all_to_all(blocks, axes, split_axis=0, concat_axis=0, tiled=True)  30.9 us
    all_to_all x3, starting transfers between devices, exchange(): return lax.all_to_all(blocks, axes, split_axis=0, concat_axis=0, tiled=True)  18.4 us
    ppermute x12, starting transfers between devices, swap(): return lax.ppermute(t, axis, SWAP)  13.4 us
    ppermute x12, waiting for transfers between devices, swap(): return lax.ppermute(t, axis, SWAP)  9.37 us
    ppermute x6, starting transfers between devices, along_y(): return lax.ppermute(t, 'y', [(i, (i + s) % 4) for i in range(4)])  6.7 us
    pallas_call x1, Pallas kernels, local(): call(correlate, (shape((SHARE, 2 * BLOCK), f32),) + (shape((SHARE, 2 * BL...  4.71 us
    ppermute x6, waiting for transfers between devices, along_y(): return lax.ppermute(t, 'y', [(i, (i + s) % 4) for i in range(4)])  4.12 us
    pallas_call x1, Pallas kernels, local(): call(turn, (shape((DEPTH, 512), bf16),) * 2 + (shape((2 * QUARTER, DEPTH)...  3.95 us
  transfers between devices with their start and end apart: 21, of which 10 were waited for; matrix products, arithmetic and copies ran while one was open for 5% of the time, Pallas kernels for 15%

profile of v9, /device:TPU:1, one launch (start us, length us, event | category | flops | bytes accessed | tf_op | source)
XLA Modules:
  0.0 111.0 jit_solution(1441160836955480580)
XLA Ops:
  1.7 2.1 %collective-permute-start = (bf16[1024,256]{1,0:T(8,128)(2,1)S(1)}, bf16[1024,256]{1,0:T(8,128)(2,1)S(1)}, u32[]{:S(2)}, u32[]{:S(2)}) collective-permute-start(bf16[1024,256]{1,0:T(8,128)(2,1)S(1)} %slice.13), channel_id=1, source_target_pairs={{0,2},{2,0},{1,3},{3,1},{4,6},{6,4},{5,7},{7,5},{8,10},{10,8},{9,1... | collective-permute-start | bytes 1572872 | tf_op jit(solution)/shard_map/ppermute | solution.py:229
  3.9 1.3 %collective-permute-start.1 = (bf16[1536,256]{1,0:T(8,128)(2,1)}, bf16[1536,256]{1,0:T(8,128)(2,1)S(1)}, u32[]{:S(2)}, u32[]{:S(2)}) collective-permute-start(bf16[1536,256]{1,0:T(8,128)(2,1)} %w0.1), channel_id=1, source_target_pairs={{0,1},{1,0},{2,3},{3,2},{4,5},{5,4},{6,7},{7,6},{8,9},{9,8},{10,11... | collective-permute-start | bytes 2359304 | tf_op jit(solution)/shard_map/ppermute | solution.py:229
  5.2 3.4 %project.1 = (f32[384,256]{1,0:T(8,128)}, f32[384,256]{1,0:T(8,128)}, f32[32,8,256]{2,1,0:T(8,128)}) custom-call(bf16[384,1536]{1,0:T(8,128)(2,1)} %va.2, bf16[384,1536]{1,0:T(8,128)(2,1)} %vb.2, bf16[1536,256]{1,0:T(8,128)(2,1)} %w0.1), custom_call_target="tpu_custom_call" | custom-call | flops 603979776 | bytes 4194304 | tf_op jit(solution)/shard_map/project/pallas_call | solution.py:237
  8.5 6.6 %all-to-all-start = ((f32[32,8,256]{2,1,0:T(8,128)}), f32[32,8,256]{2,1,0:T(8,128)S(1)}, u32[]{:S(2)}, u32[]{:S(2)}) async-start(f32[32,8,256]{2,1,0:T(8,128)} %get-tuple-element.42), calls=%async_computation | async-start | bytes 524288 | tf_op jit(solution)/shard_map/all_to_all | solution.py:31
  16.5 3.9 %turn.1 = (bf16[1536,512]{1,0:T(8,128)(2,1)}, bf16[1536,512]{1,0:T(8,128)(2,1)}, bf16[192,1536]{1,0:T(8,128)(2,1)}) custom-call(s32[2]{0:T(128)} %pad_add_fusion.place, bf16[384,1536]{1,0:T(8,128)(2,1)} %va.2, bf16[384,1536]{1,0:T(8,128)(2,1)} %vb.2), custom_call_target="tpu_custom_call" | custom-call | flops 10485760 | bytes 6291456 | tf_op jit(solution)/shard_map/turn/pallas_call | solution.py:253
  20.5 3.2 %all-to-all-done.sums = f32[32,8,256]{2,1,0:T(8,128)S(1)} async-done(((f32[32,8,256]{2,1,0:T(8,128)}), f32[32,8,256]{2,1,0:T(8,128)S(1)}, u32[]{:S(2)}, u32[]{:S(2)}) %all-to-all-start) | async-done | bytes 262176 | tf_op jit(solution)/shard_map/all_to_all | solution.py:31
  24.4 4.7 %correlate.1 = (f32[384,512]{1,0:T(8,128)}, bf16[384,512]{1,0:T(8,128)(2,1)}, bf16[384,512]{1,0:T(8,128)(2,1)}, bf16[384,512]{1,0:T(8,128)(2,1)}) custom-call(s32[2]{0:T(128)} %pad_add_fusion.place, f32[32,8,256]{2,1,0:T(8,128)} %copy-done.1, f32[384,256]{1,0:T(8,128)} %get-tuple-element.50.pa, f32[384,256]{1,0:T(8,128)} %get-tuple-element.51.pb, ...), custom_call_target="tpu_custom_call" | custom-call | flops 603979776 | bytes 6291456 | tf_op jit(solution)/shard_map/correlate/pallas_call | solution.py:267
  31.7 1.3 %collective-permute-start.7 = (bf16[384,512]{1,0:T(8,128)(2,1)}, bf16[384,512]{1,0:T(8,128)(2,1)}, u32[]{:S(2)}, u32[]{:S(2)}) collective-permute-start(bf16[384,512]{1,0:T(8,128)(2,1)} %get-tuple-element.65), channel_id=1, source_target_pairs={{0,96},{32,0},{64,32},{96,64},{1,97},{33,1},{65,33},{97,65},{2,98}... | collective-permute-start | bytes 1179656 | tf_op jit(solution)/shard_map/ppermute | solution.py:232
  36.0 3.2 %embed.1 = bf16[8,48,768]{2,1,0:T(8,128)(2,1)} custom-call(s32[2]{0:T(128)S(1)} %copy-done.7, f32[32,8,256]{2,1,0:T(8,128)S(1)} %copy-done.2, bf16[192,1536]{1,0:T(8,128)(2,1)S(1)} %copy-done.6, bf16[1536,256]{1,0:T(8,128)(2,1)S(1)} %copy-done, bf16[1536,256]{1,0:T(8,128)(2,1)S(1)} %collective-permute-done.1.w1, ...), custom_call_target="tpu_custom_call" | custom-call | flops 1207959552 | bytes 7340032 | tf_op jit(solution)/shard_map/embed/pallas_call | solution.py:301
  39.1 8.3 %all-to-all-start.1 = ((bf16[8,48,768]{2,1,0:T(8,128)(2,1)}), bf16[8,48,768]{2,1,0:T(8,128)(2,1)S(1)}, u32[]{:S(2)}, u32[]{:S(2)}) async-start(bf16[8,48,768]{2,1,0:T(8,128)(2,1)} %embed.1), calls=%async_computation.1 | async-start | bytes 1179648 | tf_op jit(solution)/shard_map/all_to_all | solution.py:31
  47.5 3.3 %collective-permute-done.5 = bf16[384,512]{1,0:T(8,128)(2,1)S(1)} collective-permute-done((bf16[384,512]{1,0:T(8,128)(2,1)}, bf16[384,512]{1,0:T(8,128)(2,1)S(1)}, u32[]{:S(2)}, u32[]{:S(2)}) %collective-permute-start.5) | collective-permute-done | bytes 393248 | tf_op jit(solution)/shard_map/ppermute | solution.py:232
  51.2 1.4 %fusion.5 = (f16[384,512]{1,0:T(8,128)(2,1)S(1)}, f32[384,512]{1,0:T(8,128)S(1)}) fusion(bf16[384,512]{1,0:T(8,128)(2,1)} %collective-permute-done.7, bf16[384,512]{1,0:T(8,128)(2,1)} %collective-permute-done.6, f32[384,512]{1,0:T(8,128)S(1)} %copy-done.8, bf16[384,512]{1,0:T(8,128)(2,1)S(1)} %collective-permute-done.5), kind=kLoop, calls=%fused_computation.20 | loop fusion | flops 1376256 | bytes 3145728 | tf_op jit(solution)/shard_map/convert_element_type | solution.py:295
  52.5 1.7 %collective-permute-start.8 = (f16[384,512]{1,0:T(8,128)(2,1)S(1)}, f16[384,512]{1,0:T(8,128)(2,1)S(1)}, u32[]{:S(2)}, u32[]{:S(2)}) collective-permute-start(f16[384,512]{1,0:T(8,128)(2,1)S(1)} %get-tuple-element.82), channel_id=1, source_target_pairs={{0,128},{128,0},{1,129},{129,1},{2,130},{130,2},{3,131},{131,3},{4... | collective-permute-start | bytes 1179656 | tf_op jit(solution)/shard_map/ppermute | solution.py:229
  54.3 12.6 %all-to-all-done.1.parts = bf16[8,48,768]{2,1,0:T(8,128)(2,1)S(1)} async-done(((bf16[8,48,768]{2,1,0:T(8,128)(2,1)}), bf16[8,48,768]{2,1,0:T(8,128)(2,1)S(1)}, u32[]{:S(2)}, u32[]{:S(2)}) %all-to-all-start.1) | async-done | bytes 589856 | tf_op jit(solution)/shard_map/all_to_all | solution.py:31
  67.7 3.5 %all-to-all-start.2 = ((bf16[8,48,768]{2,1,0:T(8,128)(2,1)}), bf16[8,48,768]{2,1,0:T(8,128)(2,1)S(1)}, u32[]{:S(2)}, u32[]{:S(2)}) async-start(bf16[8,48,768]{2,1,0:T(8,128)(2,1)} %add_copies.1), calls=%async_computation.2 | async-start | bytes 1179648 | tf_op jit(solution)/shard_map/all_to_all | solution.py:31
  71.4 2.4 %collective-permute-start.10 = (f16[384,512]{1,0:T(8,128)(2,1)S(1)}, f16[384,512]{1,0:T(8,128)(2,1)S(1)}, u32[]{:S(2)}, u32[]{:S(2)}) collective-permute-start(f16[384,512]{1,0:T(8,128)(2,1)S(1)} %get-tuple-element.84), channel_id=1, source_target_pairs={{0,64},{32,96},{64,0},{96,32},{1,65},{33,97},{65,1},{97,33},{2,66}... | collective-permute-start | bytes 1179656 | tf_op jit(solution)/shard_map/ppermute | solution.py:232
  75.5 15.1 %all-to-all-done.2.whole = bf16[8,48,768]{2,1,0:T(8,128)(2,1)S(1)} async-done(((bf16[8,48,768]{2,1,0:T(8,128)(2,1)}), bf16[8,48,768]{2,1,0:T(8,128)(2,1)S(1)}, u32[]{:S(2)}, u32[]{:S(2)}) %all-to-all-start.2) | async-done | bytes 589856 | tf_op jit(solution)/shard_map/all_to_all | solution.py:31
  94.6 1.3 %fusion.1 = (bf16[384,512]{1,0:T(8,128)(2,1)S(1)}, bf16[384,512]{1,0:T(8,128)(2,1)S(1)}, bf16[384,512]{1,0:T(8,128)(2,1)S(1)}, bf16[384,512]{1,0:T(8,128)(2,1)S(1)}) fusion(f16[384,512]{1,0:T(8,128)(2,1)} %collective-permute-done.9, f16[384,512]{1,0:T(8,128)(2,1)S(1)} %collective-permute-done.10), kind=kLoop, calls=%fused_computation.9 | loop fusion | flops 2359296 | bytes 2359296 | tf_op jit(solution)/shard_map/convert_element_type | solution.py:335
  95.8 2.9 %collective-permute-done.15.refs_5_ = bf16[4,48,768]{2,1,0:T(8,128)(2,1)S(1)} collective-permute-done((bf16[4,48,768]{2,1,0:T(8,128)(2,1)S(1)}, bf16[4,48,768]{2,1,0:T(8,128)(2,1)S(1)}, u32[]{:S(2)}, u32[]{:S(2)}) %collective-permute-start.15) | collective-permute-done | bytes 294944 | tf_op jit(solution)/shard_map/ppermute | solution.py:229
  98.8 2.3 %collective-permute-start.17 = (bf16[4,48,768]{2,1,0:T(8,128)(2,1)S(1)}, bf16[4,48,768]{2,1,0:T(8,128)(2,1)S(1)}, u32[]{:S(2)}, u32[]{:S(2)}) collective-permute-start(bf16[4,48,768]{2,1,0:T(8,128)(2,1)S(1)} %collective-permute-done.15.refs_5_), channel_id=1, source_target_pairs={{0,1},{1,0},{2,3},{3,2},{4,5},{5,4},{6,7},{7,6},{8,9},{9,8},{10,11... | collective-permute-start | bytes 884744 | tf_op jit(solution)/shard_map/ppermute | solution.py:229
  101.1 4.1 %collective-permute-done.14.refs_4_ = bf16[4,48,768]{2,1,0:T(8,128)(2,1)S(1)} collective-permute-done((bf16[4,48,768]{2,1,0:T(8,128)(2,1)S(1)}, bf16[4,48,768]{2,1,0:T(8,128)(2,1)S(1)}, u32[]{:S(2)}, u32[]{:S(2)}) %collective-permute-start.14) | collective-permute-done | bytes 294944 | tf_op jit(solution)/shard_map/ppermute | solution.py:229
  105.1 1.3 %collective-permute-start.16 = (bf16[4,48,768]{2,1,0:T(8,128)(2,1)S(1)}, bf16[4,48,768]{2,1,0:T(8,128)(2,1)S(1)}, u32[]{:S(2)}, u32[]{:S(2)}) collective-permute-start(bf16[4,48,768]{2,1,0:T(8,128)(2,1)S(1)} %collective-permute-done.14.refs_4_), channel_id=1, source_target_pairs={{0,1},{1,0},{2,3},{3,2},{4,5},{5,4},{6,7},{7,6},{8,9},{9,8},{10,11... | collective-permute-start | bytes 884744 | tf_op jit(solution)/shard_map/ppermute | solution.py:229
  106.5 1.2 %collective-permute-done.16.refs_6_ = bf16[4,48,768]{2,1,0:T(8,128)(2,1)S(1)} collective-permute-done((bf16[4,48,768]{2,1,0:T(8,128)(2,1)S(1)}, bf16[4,48,768]{2,1,0:T(8,128)(2,1)S(1)}, u32[]{:S(2)}, u32[]{:S(2)}) %collective-permute-start.16) | collective-permute-done | bytes 294944 | tf_op jit(solution)/shard_map/ppermute | solution.py:229
  107.7 3.3 %combine.1 = (f32[384,256]{1,0:T(8,128)}, f32[384,256]{1,0:T(8,128)}) custom-call(s32[2]{0:T(128)S(1)} %copy-done.7, f32[32,8,256]{2,1,0:T(8,128)S(1)} %copy-done.3, f32[384,256]{1,0:T(8,128)S(1)} %copy-done.4, f32[384,256]{1,0:T(8,128)S(1)} %copy-done.5, bf16[4,48,768]{2,1,0:T(8,128)(2,1)S(1)} %get-tuple-element.68.refs_0_, ...), custom_call_target="tpu_custom_call" | custom-call | flops 1207959552 | bytes 8388608 | tf_op jit(solution)/shard_map/combine/pallas_call | solution.py:340
  (55 shorter events, 15.8 us)
Async XLA Ops:
  1.7 22.0 %collective-permute-start = (bf16[1024,256]{1,0:T(8,128)(2,1)S(1)}, bf16[1024,256]{1,0:T(8,128)(2,1)S(1)}, u32[]{:S(2)}, u32[]{:S(2)}) collective-permute-start(bf16[1024,256]{1,0:T(8,128)(2,1)S(1)} %slice.13), channel_id=1, source_target_pairs={{0,2},{2,0},{1,3},{3,1},{4,6},{6,4},{5,7},{7,5},{8,10},{10,8},{9,1... | collective-permute-start | bytes 1572872 | tf_op jit(solution)/shard_map/ppermute | solution.py:229
  3.9 29.2 %collective-permute-start.1 = (bf16[1536,256]{1,0:T(8,128)(2,1)}, bf16[1536,256]{1,0:T(8,128)(2,1)S(1)}, u32[]{:S(2)}, u32[]{:S(2)}) collective-permute-start(bf16[1536,256]{1,0:T(8,128)(2,1)} %w0.1), channel_id=1, source_target_pairs={{0,1},{1,0},{2,3},{3,2},{4,5},{5,4},{6,7},{7,6},{8,9},{9,8},{10,11... | collective-permute-start | bytes 2359304 | tf_op jit(solution)/shard_map/ppermute | solution.py:229
  8.5 15.1 %all-to-all-start = ((f32[32,8,256]{2,1,0:T(8,128)}), f32[32,8,256]{2,1,0:T(8,128)S(1)}, u32[]{:S(2)}, u32[]{:S(2)}) async-start(f32[32,8,256]{2,1,0:T(8,128)} %get-tuple-element.42), calls=%async_computation | async-start | bytes 524288 | tf_op jit(solution)/shard_map/all_to_all | solution.py:31
  23.7 8.1 %collective-permute-start.2 = (bf16[512,256]{1,0:T(8,128)(2,1)}, bf16[512,256]{1,0:T(8,128)(2,1)S(1)}, u32[]{:S(2)}, u32[]{:S(2)}) collective-permute-start(bf16[512,256]{1,0:T(8,128)(2,1)} %slice.12), channel_id=1, source_target_pairs={{0,2},{2,0},{1,3},{3,1},{4,6},{6,4},{5,7},{7,5},{8,10},{10,8},{9,1... | collective-permute-start | bytes 786440 | tf_op jit(solution)/shard_map/ppermute | solution.py:229
  29.1 4.8 %collective-permute-start.3 = (bf16[1024,256]{1,0:T(8,128)(2,1)S(1)}, bf16[1024,256]{1,0:T(8,128)(2,1)S(1)}, u32[]{:S(2)}, u32[]{:S(2)}) collective-permute-start(bf16[1024,256]{1,0:T(8,128)(2,1)S(1)} %collective-permute-done.w2), channel_id=1, source_target_pairs={{0,1},{1,0},{2,3},{3,2},{4,5},{5,4},{6,7},{7,6},{8,9},{9,8},{10,11... | collective-permute-start | bytes 1572872 | tf_op jit(solution)/shard_map/ppermute | solution.py:229
  30.2 20.5 %collective-permute-start.5 = (bf16[384,512]{1,0:T(8,128)(2,1)}, bf16[384,512]{1,0:T(8,128)(2,1)S(1)}, u32[]{:S(2)}, u32[]{:S(2)}) collective-permute-start(bf16[384,512]{1,0:T(8,128)(2,1)} %get-tuple-element.63), channel_id=1, source_target_pairs={{0,32},{32,64},{64,96},{96,0},{1,33},{33,65},{65,97},{97,1},{2,34}... | collective-permute-start | bytes 1179656 | tf_op jit(solution)/shard_map/ppermute | solution.py:232
  30.6 20.1 %collective-permute-start.6 = (bf16[384,512]{1,0:T(8,128)(2,1)}, bf16[384,512]{1,0:T(8,128)(2,1)}, u32[]{:S(2)}, u32[]{:S(2)}) collective-permute-start(bf16[384,512]{1,0:T(8,128)(2,1)} %get-tuple-element.64), channel_id=1, source_target_pairs={{0,64},{32,96},{64,0},{96,32},{1,65},{33,97},{65,1},{97,33},{2,66}... | collective-permute-start | bytes 1179656 | tf_op jit(solution)/shard_map/ppermute | solution.py:232
  31.7 19.4 %collective-permute-start.7 = (bf16[384,512]{1,0:T(8,128)(2,1)}, bf16[384,512]{1,0:T(8,128)(2,1)}, u32[]{:S(2)}, u32[]{:S(2)}) collective-permute-start(bf16[384,512]{1,0:T(8,128)(2,1)} %get-tuple-element.65), channel_id=1, source_target_pairs={{0,96},{32,0},{64,32},{96,64},{1,97},{33,1},{65,33},{97,65},{2,98}... | collective-permute-start | bytes 1179656 | tf_op jit(solution)/shard_map/ppermute | solution.py:232
  33.0 2.0 %collective-permute-start.4 = (bf16[512,256]{1,0:T(8,128)(2,1)S(1)}, bf16[512,256]{1,0:T(8,128)(2,1)S(1)}, u32[]{:S(2)}, u32[]{:S(2)}) collective-permute-start(bf16[512,256]{1,0:T(8,128)(2,1)S(1)} %collective-permute-done.2.w2b), channel_id=1, source_target_pairs={{0,1},{1,0},{2,3},{3,2},{4,5},{5,4},{6,7},{7,6},{8,9},{9,8},{10,11... | collective-permute-start | bytes 786440 | tf_op jit(solution)/shard_map/ppermute | solution.py:229
  39.1 27.7 %all-to-all-start.1 = ((bf16[8,48,768]{2,1,0:T(8,128)(2,1)}), bf16[8,48,768]{2,1,0:T(8,128)(2,1)S(1)}, u32[]{:S(2)}, u32[]{:S(2)}) async-start(bf16[8,48,768]{2,1,0:T(8,128)(2,1)} %embed.1), calls=%async_computation.1 | async-start | bytes 1179648 | tf_op jit(solution)/shard_map/all_to_all | solution.py:31
  52.5 18.7 %collective-permute-start.8 = (f16[384,512]{1,0:T(8,128)(2,1)S(1)}, f16[384,512]{1,0:T(8,128)(2,1)S(1)}, u32[]{:S(2)}, u32[]{:S(2)}) collective-permute-start(f16[384,512]{1,0:T(8,128)(2,1)S(1)} %get-tuple-element.82), channel_id=1, source_target_pairs={{0,128},{128,0},{1,129},{129,1},{2,130},{130,2},{3,131},{131,3},{4... | collective-permute-start | bytes 1179656 | tf_op jit(solution)/shard_map/ppermute | solution.py:229
  67.7 22.9 %all-to-all-start.2 = ((bf16[8,48,768]{2,1,0:T(8,128)(2,1)}), bf16[8,48,768]{2,1,0:T(8,128)(2,1)S(1)}, u32[]{:S(2)}, u32[]{:S(2)}) async-start(bf16[8,48,768]{2,1,0:T(8,128)(2,1)} %add_copies.1), calls=%async_computation.2 | async-start | bytes 1179648 | tf_op jit(solution)/shard_map/all_to_all | solution.py:31
  71.4 20.8 %collective-permute-start.10 = (f16[384,512]{1,0:T(8,128)(2,1)S(1)}, f16[384,512]{1,0:T(8,128)(2,1)S(1)}, u32[]{:S(2)}, u32[]{:S(2)}) collective-permute-start(f16[384,512]{1,0:T(8,128)(2,1)S(1)} %get-tuple-element.84), channel_id=1, source_target_pairs={{0,64},{32,96},{64,0},{96,32},{1,65},{33,97},{65,1},{97,33},{2,66}... | collective-permute-start | bytes 1179656 | tf_op jit(solution)/shard_map/ppermute | solution.py:232
  73.9 18.3 %collective-permute-start.11 = (f16[384,512]{1,0:T(8,128)(2,1)S(1)}, f16[384,512]{1,0:T(8,128)(2,1)}, u32[]{:S(2)}, u32[]{:S(2)}) collective-permute-start(f16[384,512]{1,0:T(8,128)(2,1)S(1)} %get-tuple-element.84), channel_id=1, source_target_pairs={{0,96},{32,0},{64,32},{96,64},{1,97},{33,1},{65,33},{97,65},{2,98}... | collective-permute-start | bytes 1179656 | tf_op jit(solution)/shard_map/ppermute | solution.py:232
  74.4 18.2 %collective-permute-start.9 = (f16[384,512]{1,0:T(8,128)(2,1)S(1)}, f16[384,512]{1,0:T(8,128)(2,1)}, u32[]{:S(2)}, u32[]{:S(2)}) collective-permute-start(f16[384,512]{1,0:T(8,128)(2,1)S(1)} %get-tuple-element.84), channel_id=1, source_target_pairs={{0,32},{32,64},{64,96},{96,0},{1,33},{33,65},{65,97},{97,1},{2,34}... | collective-permute-start | bytes 1179656 | tf_op jit(solution)/shard_map/ppermute | solution.py:232
  90.6 8.2 %collective-permute-start.15 = (bf16[4,48,768]{2,1,0:T(8,128)(2,1)S(1)}, bf16[4,48,768]{2,1,0:T(8,128)(2,1)S(1)}, u32[]{:S(2)}, u32[]{:S(2)}) collective-permute-start(bf16[4,48,768]{2,1,0:T(8,128)(2,1)S(1)} %get-tuple-element.69.refs_1_), channel_id=1, source_target_pairs={{0,2},{2,0},{1,3},{3,1},{4,6},{6,4},{5,7},{7,5},{8,10},{10,8},{9,1... | collective-permute-start | bytes 884744 | tf_op jit(solution)/shard_map/ppermute | solution.py:229
  91.7 16.0 %copy-start.3 = (f32[32,8,256]{2,1,0:T(8,128)S(1)}, f32[32,8,256]{2,1,0:T(8,128)}, u32[]{:S(2)}) copy-start(f32[32,8,256]{2,1,0:T(8,128)} %copy-done.1) | copy-start | bytes 786436
  91.7 16.0 %copy-start.4 = (f32[384,256]{1,0:T(8,128)S(1)}, f32[384,256]{1,0:T(8,128)}, u32[]{:S(2)}) copy-start(f32[384,256]{1,0:T(8,128)} %get-tuple-element.50.pa) | copy-start | bytes 1179652
  91.7 16.0 %copy-start.5 = (f32[384,256]{1,0:T(8,128)S(1)}, f32[384,256]{1,0:T(8,128)}, u32[]{:S(2)}) copy-start(f32[384,256]{1,0:T(8,128)} %get-tuple-element.51.pb) | copy-start | bytes 1179652
  91.7 13.4 %collective-permute-start.14 = (bf16[4,48,768]{2,1,0:T(8,128)(2,1)S(1)}, bf16[4,48,768]{2,1,0:T(8,128)(2,1)S(1)}, u32[]{:S(2)}, u32[]{:S(2)}) collective-permute-start(bf16[4,48,768]{2,1,0:T(8,128)(2,1)S(1)} %get-tuple-element.68.refs_0_), channel_id=1, source_target_pairs={{0,2},{2,0},{1,3},{3,1},{4,6},{6,4},{5,7},{7,5},{8,10},{10,8},{9,1... | collective-permute-start | bytes 884744 | tf_op jit(solution)/shard_map/ppermute | solution.py:229
  93.7 12.7 %collective-permute-start.12 = (bf16[4,48,768]{2,1,0:T(8,128)(2,1)S(1)}, bf16[4,48,768]{2,1,0:T(8,128)(2,1)S(1)}, u32[]{:S(2)}, u32[]{:S(2)}) collective-permute-start(bf16[4,48,768]{2,1,0:T(8,128)(2,1)S(1)} %get-tuple-element.68.refs_0_), channel_id=1, source_target_pairs={{0,1},{1,0},{2,3},{3,2},{4,5},{5,4},{6,7},{7,6},{8,9},{9,8},{10,11... | collective-permute-start | bytes 884744 | tf_op jit(solution)/shard_map/ppermute | solution.py:229
  94.5 12.0 %collective-permute-start.13 = (bf16[4,48,768]{2,1,0:T(8,128)(2,1)S(1)}, bf16[4,48,768]{2,1,0:T(8,128)(2,1)S(1)}, u32[]{:S(2)}, u32[]{:S(2)}) collective-permute-start(bf16[4,48,768]{2,1,0:T(8,128)(2,1)S(1)} %get-tuple-element.69.refs_1_), channel_id=1, source_target_pairs={{0,1},{1,0},{2,3},{3,2},{4,5},{5,4},{6,7},{7,6},{8,9},{9,8},{10,11... | collective-permute-start | bytes 884744 | tf_op jit(solution)/shard_map/ppermute | solution.py:229
  98.8 7.7 %collective-permute-start.17 = (bf16[4,48,768]{2,1,0:T(8,128)(2,1)S(1)}, bf16[4,48,768]{2,1,0:T(8,128)(2,1)S(1)}, u32[]{:S(2)}, u32[]{:S(2)}) collective-permute-start(bf16[4,48,768]{2,1,0:T(8,128)(2,1)S(1)} %collective-permute-done.15.refs_5_), channel_id=1, source_target_pairs={{0,1},{1,0},{2,3},{3,2},{4,5},{5,4},{6,7},{7,6},{8,9},{9,8},{10,11... | collective-permute-start | bytes 884744 | tf_op jit(solution)/shard_map/ppermute | solution.py:229
  105.1 2.5 %collective-permute-start.16 = (bf16[4,48,768]{2,1,0:T(8,128)(2,1)S(1)}, bf16[4,48,768]{2,1,0:T(8,128)(2,1)S(1)}, u32[]{:S(2)}, u32[]{:S(2)}) collective-permute-start(bf16[4,48,768]{2,1,0:T(8,128)(2,1)S(1)} %collective-permute-done.14.refs_4_), channel_id=1, source_target_pairs={{0,1},{1,0},{2,3},{3,2},{4,5},{5,4},{6,7},{7,6},{8,9},{9,8},{10,11... | collective-permute-start | bytes 884744 | tf_op jit(solution)/shard_map/ppermute | solution.py:229
  (6 other events, 48.4 us)

commit v10 on v9

--- a/solution.py
+++ b/solution.py
@@ -10,7 +10,7 @@
 FEAT = ("z", "xl", "c")
 PARTS = {"xh": 2, "y": 4, "z": 8, "xl": 2, "c": 2}
 SWAP = [(0, 1), (1, 0)]
-U_SCALE = 1024.0
+U_SCALE = 1536.0
 EPS = 1e-05
 f32, bf16, f16 = jnp.float32, jnp.bfloat16, jnp.float16
 
@@ -139,7 +139,7 @@
         for i, (src, dst) in enumerate(((sums, xs), (pa, xpa), (pb, xpb)))
     ]
     copies = {}
-    for s in (1, 2, 3, 0):
+    for s in range(4):
         at = pl.ds(pl.multiple_of(((yy + s) & 3) * SHARE, SHARE), SHARE)
         copies[s] = (
             pltpu.make_async_copy(ta.at[at, :], xa.at[s], sem.at[2 * s]),
@@ -159,14 +159,14 @@
         rounded = n.astype(bf16)
         excess = jnp.sum(n - rounded.astype(f32), axis=0, keepdims=True)
         excess = jnp.concatenate([excess, jnp.zeros((15, BLOCK), f32)], axis=0).astype(bf16)
-        ns.append(jnp.concatenate([rounded, excess, jnp.zeros((112, BLOCK), bf16)], axis=0))
-    scale = U_SCALE / TOTAL
+        n = jnp.concatenate([rounded, excess, jnp.zeros((112, BLOCK), bf16)], axis=0)
+        ns.append(n * (U_SCALE / TOTAL))
     done = []
-    for s, x, u in ((1, x1, u1), (2, x2, u2), (3, x3, u3), (0, x0, u0)):
+    for s, x, u in ((0, x0, u0), (1, x1, u1), (2, x2, u2), (3, x3, u3)):
         for t in copies[s]:
             t.wait()
-        x[:, :BLOCK] = (dot(xb[s], ns[0], 1, 0) * scale).astype(x.dtype)
-        x[:, BLOCK:] = (dot(xa[s], ns[1], 1, 0) * scale).astype(x.dtype)
+        x[:, :BLOCK] = dot(xb[s], ns[0], 1, 0).astype(x.dtype)
+        x[:, BLOCK:] = dot(xa[s], ns[1], 1, 0).astype(x.dtype)
         out = pltpu.make_async_copy(x, u, out_sem.at[s])
         out.start()
         done.append(out)

time: 112 us -> 112 us (level)
  transfers between devices with their start and end apart: 21 -> 21, of which waited for: 10 -> 10; matrix products, arithmetic and copies ran while one was open for 5% -> 5% of each run, Pallas kernels for 15% -> 14%
where the time goes in v10:
time: 112 us; the launch traced here: 111 us
  waiting for transfers between devices  44.4 us (40%)
  starting transfers between devices  38.6 us (34%)
  Pallas kernels  19.3 us (17%)
  other arithmetic  4.73 us (4%)
  local copies, waits for them, and re-layouts  3.18 us (3%)
    all_to_all x3, waiting for transfers between devices, exchange(): return lax.all_to_all(blocks, axes, split_axis=0, concat_axis=0, tiled=True)  31.1 us
    all_to_all x3, starting transfers between devices, exchange(): return lax.all_to_all(blocks, axes, split_axis=0, concat_axis=0, tiled=True)  18.4 us
    ppermute x12, starting transfers between devices, swap(): return lax.ppermute(t, axis, SWAP)  13.5 us
    ppermute x12, waiting for transfers between devices, swap(): return lax.ppermute(t, axis, SWAP)  9.37 us
    ppermute x6, starting transfers between devices, along_y(): return lax.ppermute(t, 'y', [(i, (i + s) % 4) for i in range(4)])  6.58 us
    pallas_call x1, Pallas kernels, local(): call(correlate, (shape((SHARE, 2 * BLOCK), f32),) + (shape((SHARE, 2 * BL...  4.57 us
    ppermute x6, waiting for transfers between devices, along_y(): return lax.ppermute(t, 'y', [(i, (i + s) % 4) for i in range(4)])  3.98 us
    pallas_call x1, Pallas kernels, local(): call(turn, (shape((DEPTH, 512), bf16),) * 2 + (shape((2 * QUARTER, DEPTH)...  3.95 us
  transfers between devices with their start and end apart: 21, of which 10 were waited for; matrix products, arithmetic and copies ran while one was open for 5% of the time, Pallas kernels for 14%

profile of v10, /device:TPU:1, one launch (start us, length us, event | category | flops | bytes accessed | tf_op | source)
XLA Modules:
  0.0 111.0 jit_solution(16803084738974217136)
XLA Ops:
  1.7 2.1 %collective-permute-start = (bf16[1024,256]{1,0:T(8,128)(2,1)S(1)}, bf16[1024,256]{1,0:T(8,128)(2,1)S(1)}, u32[]{:S(2)}, u32[]{:S(2)}) collective-permute-start(bf16[1024,256]{1,0:T(8,128)(2,1)S(1)} %slice.13), channel_id=1, source_target_pairs={{0,2},{2,0},{1,3},{3,1},{4,6},{6,4},{5,7},{7,5},{8,10},{10,8},{9,1... | collective-permute-start | bytes 1572872 | tf_op jit(solution)/shard_map/ppermute | solution.py:229
  3.9 1.3 %collective-permute-start.1 = (bf16[1536,256]{1,0:T(8,128)(2,1)}, bf16[1536,256]{1,0:T(8,128)(2,1)S(1)}, u32[]{:S(2)}, u32[]{:S(2)}) collective-permute-start(bf16[1536,256]{1,0:T(8,128)(2,1)} %w0.1), channel_id=1, source_target_pairs={{0,1},{1,0},{2,3},{3,2},{4,5},{5,4},{6,7},{7,6},{8,9},{9,8},{10,11... | collective-permute-start | bytes 2359304 | tf_op jit(solution)/shard_map/ppermute | solution.py:229
  5.2 3.4 %project.1 = (f32[384,256]{1,0:T(8,128)}, f32[384,256]{1,0:T(8,128)}, f32[32,8,256]{2,1,0:T(8,128)}) custom-call(bf16[384,1536]{1,0:T(8,128)(2,1)} %va.2, bf16[384,1536]{1,0:T(8,128)(2,1)} %vb.2, bf16[1536,256]{1,0:T(8,128)(2,1)} %w0.1), custom_call_target="tpu_custom_call" | custom-call | flops 603979776 | bytes 4194304 | tf_op jit(solution)/shard_map/project/pallas_call | solution.py:237
  8.5 6.6 %all-to-all-start = ((f32[32,8,256]{2,1,0:T(8,128)}), f32[32,8,256]{2,1,0:T(8,128)S(1)}, u32[]{:S(2)}, u32[]{:S(2)}) async-start(f32[32,8,256]{2,1,0:T(8,128)} %get-tuple-element.42), calls=%async_computation | async-start | bytes 524288 | tf_op jit(solution)/shard_map/all_to_all | solution.py:31
  16.5 3.9 %turn.1 = (bf16[1536,512]{1,0:T(8,128)(2,1)}, bf16[1536,512]{1,0:T(8,128)(2,1)}, bf16[192,1536]{1,0:T(8,128)(2,1)}) custom-call(s32[2]{0:T(128)} %pad_add_fusion.place, bf16[384,1536]{1,0:T(8,128)(2,1)} %va.2, bf16[384,1536]{1,0:T(8,128)(2,1)} %vb.2), custom_call_target="tpu_custom_call" | custom-call | flops 10485760 | bytes 6291456 | tf_op jit(solution)/shard_map/turn/pallas_call | solution.py:253
  20.5 3.2 %all-to-all-done.sums = f32[32,8,256]{2,1,0:T(8,128)S(1)} async-done(((f32[32,8,256]{2,1,0:T(8,128)}), f32[32,8,256]{2,1,0:T(8,128)S(1)}, u32[]{:S(2)}, u32[]{:S(2)}) %all-to-all-start) | async-done | bytes 262176 | tf_op jit(solution)/shard_map/all_to_all | solution.py:31
  24.4 4.6 %correlate.1 = (f32[384,512]{1,0:T(8,128)}, bf16[384,512]{1,0:T(8,128)(2,1)}, bf16[384,512]{1,0:T(8,128)(2,1)}, bf16[384,512]{1,0:T(8,128)(2,1)}) custom-call(s32[2]{0:T(128)} %pad_add_fusion.place, f32[32,8,256]{2,1,0:T(8,128)} %copy-done.1, f32[384,256]{1,0:T(8,128)} %get-tuple-element.50.pa, f32[384,256]{1,0:T(8,128)} %get-tuple-element.51.pb, ...), custom_call_target="tpu_custom_call" | custom-call | flops 603979776 | bytes 6291456 | tf_op jit(solution)/shard_map/correlate/pallas_call | solution.py:267
  31.6 1.3 %collective-permute-start.7 = (bf16[384,512]{1,0:T(8,128)(2,1)}, bf16[384,512]{1,0:T(8,128)(2,1)}, u32[]{:S(2)}, u32[]{:S(2)}) collective-permute-start(bf16[384,512]{1,0:T(8,128)(2,1)} %get-tuple-element.65), channel_id=1, source_target_pairs={{0,96},{32,0},{64,32},{96,64},{1,97},{33,1},{65,33},{97,65},{2,98}... | collective-permute-start | bytes 1179656 | tf_op jit(solution)/shard_map/ppermute | solution.py:232
  36.0 3.2 %embed.1 = bf16[8,48,768]{2,1,0:T(8,128)(2,1)} custom-call(s32[2]{0:T(128)S(1)} %copy-done.7, f32[32,8,256]{2,1,0:T(8,128)S(1)} %copy-done.2, bf16[192,1536]{1,0:T(8,128)(2,1)S(1)} %copy-done.6, bf16[1536,256]{1,0:T(8,128)(2,1)S(1)} %copy-done, bf16[1536,256]{1,0:T(8,128)(2,1)S(1)} %collective-permute-done.1.w1, ...), custom_call_target="tpu_custom_call" | custom-call | flops 1207959552 | bytes 7340032 | tf_op jit(solution)/shard_map/embed/pallas_call | solution.py:301
  39.1 8.3 %all-to-all-start.1 = ((bf16[8,48,768]{2,1,0:T(8,128)(2,1)}), bf16[8,48,768]{2,1,0:T(8,128)(2,1)S(1)}, u32[]{:S(2)}, u32[]{:S(2)}) async-start(bf16[8,48,768]{2,1,0:T(8,128)(2,1)} %embed.1), calls=%async_computation.1 | async-start | bytes 1179648 | tf_op jit(solution)/shard_map/all_to_all | solution.py:31
  47.5 3.2 %collective-permute-done.5 = bf16[384,512]{1,0:T(8,128)(2,1)S(1)} collective-permute-done((bf16[384,512]{1,0:T(8,128)(2,1)}, bf16[384,512]{1,0:T(8,128)(2,1)S(1)}, u32[]{:S(2)}, u32[]{:S(2)}) %collective-permute-start.5) | collective-permute-done | bytes 393248 | tf_op jit(solution)/shard_map/ppermute | solution.py:232
  51.0 1.4 %fusion.5 = (f16[384,512]{1,0:T(8,128)(2,1)S(1)}, f32[384,512]{1,0:T(8,128)S(1)}) fusion(bf16[384,512]{1,0:T(8,128)(2,1)} %collective-permute-done.7, bf16[384,512]{1,0:T(8,128)(2,1)} %collective-permute-done.6, f32[384,512]{1,0:T(8,128)S(1)} %copy-done.8, bf16[384,512]{1,0:T(8,128)(2,1)S(1)} %collective-permute-done.5), kind=kLoop, calls=%fused_computation.20 | loop fusion | flops 1376256 | bytes 3145728 | tf_op jit(solution)/shard_map/convert_element_type | solution.py:295
  52.4 1.7 %collective-permute-start.8 = (f16[384,512]{1,0:T(8,128)(2,1)S(1)}, f16[384,512]{1,0:T(8,128)(2,1)S(1)}, u32[]{:S(2)}, u32[]{:S(2)}) collective-permute-start(f16[384,512]{1,0:T(8,128)(2,1)S(1)} %get-tuple-element.82), channel_id=1, source_target_pairs={{0,128},{128,0},{1,129},{129,1},{2,130},{130,2},{3,131},{131,3},{4... | collective-permute-start | bytes 1179656 | tf_op jit(solution)/shard_map/ppermute | solution.py:229
  54.1 12.7 %all-to-all-done.1.parts = bf16[8,48,768]{2,1,0:T(8,128)(2,1)S(1)} async-done(((bf16[8,48,768]{2,1,0:T(8,128)(2,1)}), bf16[8,48,768]{2,1,0:T(8,128)(2,1)S(1)}, u32[]{:S(2)}, u32[]{:S(2)}) %all-to-all-start.1) | async-done | bytes 589856 | tf_op jit(solution)/shard_map/all_to_all | solution.py:31
  67.7 3.5 %all-to-all-start.2 = ((bf16[8,48,768]{2,1,0:T(8,128)(2,1)}), bf16[8,48,768]{2,1,0:T(8,128)(2,1)S(1)}, u32[]{:S(2)}, u32[]{:S(2)}) async-start(bf16[8,48,768]{2,1,0:T(8,128)(2,1)} %add_copies.1), calls=%async_computation.2 | async-start | bytes 1179648 | tf_op jit(solution)/shard_map/all_to_all | solution.py:31
  71.4 2.3 %collective-permute-start.10 = (f16[384,512]{1,0:T(8,128)(2,1)S(1)}, f16[384,512]{1,0:T(8,128)(2,1)S(1)}, u32[]{:S(2)}, u32[]{:S(2)}) collective-permute-start(f16[384,512]{1,0:T(8,128)(2,1)S(1)} %get-tuple-element.84), channel_id=1, source_target_pairs={{0,64},{32,96},{64,0},{96,32},{1,65},{33,97},{65,1},{97,33},{2,66}... | collective-permute-start | bytes 1179656 | tf_op jit(solution)/shard_map/ppermute | solution.py:232
  75.4 15.2 %all-to-all-done.2.whole = bf16[8,48,768]{2,1,0:T(8,128)(2,1)S(1)} async-done(((bf16[8,48,768]{2,1,0:T(8,128)(2,1)}), bf16[8,48,768]{2,1,0:T(8,128)(2,1)S(1)}, u32[]{:S(2)}, u32[]{:S(2)}) %all-to-all-start.2) | async-done | bytes 589856 | tf_op jit(solution)/shard_map/all_to_all | solution.py:31
  94.6 1.3 %fusion.1 = (bf16[384,512]{1,0:T(8,128)(2,1)S(1)}, bf16[384,512]{1,0:T(8,128)(2,1)S(1)}, bf16[384,512]{1,0:T(8,128)(2,1)S(1)}, bf16[384,512]{1,0:T(8,128)(2,1)S(1)}) fusion(f16[384,512]{1,0:T(8,128)(2,1)} %collective-permute-done.9, f16[384,512]{1,0:T(8,128)(2,1)S(1)} %collective-permute-done.10), kind=kLoop, calls=%fused_computation.9 | loop fusion | flops 2359296 | bytes 2359296 | tf_op jit(solution)/shard_map/convert_element_type | solution.py:335
  95.9 2.9 %collective-permute-done.15.refs_5_ = bf16[4,48,768]{2,1,0:T(8,128)(2,1)S(1)} collective-permute-done((bf16[4,48,768]{2,1,0:T(8,128)(2,1)S(1)}, bf16[4,48,768]{2,1,0:T(8,128)(2,1)S(1)}, u32[]{:S(2)}, u32[]{:S(2)}) %collective-permute-start.15) | collective-permute-done | bytes 294944 | tf_op jit(solution)/shard_map/ppermute | solution.py:229
  98.8 2.3 %collective-permute-start.17 = (bf16[4,48,768]{2,1,0:T(8,128)(2,1)S(1)}, bf16[4,48,768]{2,1,0:T(8,128)(2,1)S(1)}, u32[]{:S(2)}, u32[]{:S(2)}) collective-permute-start(bf16[4,48,768]{2,1,0:T(8,128)(2,1)S(1)} %collective-permute-done.15.refs_5_), channel_id=1, source_target_pairs={{0,1},{1,0},{2,3},{3,2},{4,5},{5,4},{6,7},{7,6},{8,9},{9,8},{10,11... | collective-permute-start | bytes 884744 | tf_op jit(solution)/shard_map/ppermute | solution.py:229
  101.1 4.1 %collective-permute-done.14.refs_4_ = bf16[4,48,768]{2,1,0:T(8,128)(2,1)S(1)} collective-permute-done((bf16[4,48,768]{2,1,0:T(8,128)(2,1)S(1)}, bf16[4,48,768]{2,1,0:T(8,128)(2,1)S(1)}, u32[]{:S(2)}, u32[]{:S(2)}) %collective-permute-start.14) | collective-permute-done | bytes 294944 | tf_op jit(solution)/shard_map/ppermute | solution.py:229
  105.1 1.3 %collective-permute-start.16 = (bf16[4,48,768]{2,1,0:T(8,128)(2,1)S(1)}, bf16[4,48,768]{2,1,0:T(8,128)(2,1)S(1)}, u32[]{:S(2)}, u32[]{:S(2)}) collective-permute-start(bf16[4,48,768]{2,1,0:T(8,128)(2,1)S(1)} %collective-permute-done.14.refs_4_), channel_id=1, source_target_pairs={{0,1},{1,0},{2,3},{3,2},{4,5},{5,4},{6,7},{7,6},{8,9},{9,8},{10,11... | collective-permute-start | bytes 884744 | tf_op jit(solution)/shard_map/ppermute | solution.py:229
  106.5 1.2 %collective-permute-done.16.refs_6_ = bf16[4,48,768]{2,1,0:T(8,128)(2,1)S(1)} collective-permute-done((bf16[4,48,768]{2,1,0:T(8,128)(2,1)S(1)}, bf16[4,48,768]{2,1,0:T(8,128)(2,1)S(1)}, u32[]{:S(2)}, u32[]{:S(2)}) %collective-permute-start.16) | collective-permute-done | bytes 294944 | tf_op jit(solution)/shard_map/ppermute | solution.py:229
  107.7 3.3 %combine.1 = (f32[384,256]{1,0:T(8,128)}, f32[384,256]{1,0:T(8,128)}) custom-call(s32[2]{0:T(128)S(1)} %copy-done.7, f32[32,8,256]{2,1,0:T(8,128)S(1)} %copy-done.3, f32[384,256]{1,0:T(8,128)S(1)} %copy-done.4, f32[384,256]{1,0:T(8,128)S(1)} %copy-done.5, bf16[4,48,768]{2,1,0:T(8,128)(2,1)S(1)} %get-tuple-element.68.refs_0_, ...), custom_call_target="tpu_custom_call" | custom-call | flops 1207959552 | bytes 8388608 | tf_op jit(solution)/shard_map/combine/pallas_call | solution.py:340
  (55 shorter events, 15.9 us)
Async XLA Ops:
  1.7 22.0 %collective-permute-start = (bf16[1024,256]{1,0:T(8,128)(2,1)S(1)}, bf16[1024,256]{1,0:T(8,128)(2,1)S(1)}, u32[]{:S(2)}, u32[]{:S(2)}) collective-permute-start(bf16[1024,256]{1,0:T(8,128)(2,1)S(1)} %slice.13), channel_id=1, source_target_pairs={{0,2},{2,0},{1,3},{3,1},{4,6},{6,4},{5,7},{7,5},{8,10},{10,8},{9,1... | collective-permute-start | bytes 1572872 | tf_op jit(solution)/shard_map/ppermute | solution.py:229
  3.9 29.1 %collective-permute-start.1 = (bf16[1536,256]{1,0:T(8,128)(2,1)}, bf16[1536,256]{1,0:T(8,128)(2,1)S(1)}, u32[]{:S(2)}, u32[]{:S(2)}) collective-permute-start(bf16[1536,256]{1,0:T(8,128)(2,1)} %w0.1), channel_id=1, source_target_pairs={{0,1},{1,0},{2,3},{3,2},{4,5},{5,4},{6,7},{7,6},{8,9},{9,8},{10,11... | collective-permute-start | bytes 2359304 | tf_op jit(solution)/shard_map/ppermute | solution.py:229
  8.5 15.1 %all-to-all-start = ((f32[32,8,256]{2,1,0:T(8,128)}), f32[32,8,256]{2,1,0:T(8,128)S(1)}, u32[]{:S(2)}, u32[]{:S(2)}) async-start(f32[32,8,256]{2,1,0:T(8,128)} %get-tuple-element.42), calls=%async_computation | async-start | bytes 524288 | tf_op jit(solution)/shard_map/all_to_all | solution.py:31
  23.7 7.9 %collective-permute-start.2 = (bf16[512,256]{1,0:T(8,128)(2,1)}, bf16[512,256]{1,0:T(8,128)(2,1)S(1)}, u32[]{:S(2)}, u32[]{:S(2)}) collective-permute-start(bf16[512,256]{1,0:T(8,128)(2,1)} %slice.12), channel_id=1, source_target_pairs={{0,2},{2,0},{1,3},{3,1},{4,6},{6,4},{5,7},{7,5},{8,10},{10,8},{9,1... | collective-permute-start | bytes 786440 | tf_op jit(solution)/shard_map/ppermute | solution.py:229
  28.9 4.9 %collective-permute-start.3 = (bf16[1024,256]{1,0:T(8,128)(2,1)S(1)}, bf16[1024,256]{1,0:T(8,128)(2,1)S(1)}, u32[]{:S(2)}, u32[]{:S(2)}) collective-permute-start(bf16[1024,256]{1,0:T(8,128)(2,1)S(1)} %collective-permute-done.w2), channel_id=1, source_target_pairs={{0,1},{1,0},{2,3},{3,2},{4,5},{5,4},{6,7},{7,6},{8,9},{9,8},{10,11... | collective-permute-start | bytes 1572872 | tf_op jit(solution)/shard_map/ppermute | solution.py:229
  30.1 20.5 %collective-permute-start.5 = (bf16[384,512]{1,0:T(8,128)(2,1)}, bf16[384,512]{1,0:T(8,128)(2,1)S(1)}, u32[]{:S(2)}, u32[]{:S(2)}) collective-permute-start(bf16[384,512]{1,0:T(8,128)(2,1)} %get-tuple-element.63), channel_id=1, source_target_pairs={{0,32},{32,64},{64,96},{96,0},{1,33},{33,65},{65,97},{97,1},{2,34}... | collective-permute-start | bytes 1179656 | tf_op jit(solution)/shard_map/ppermute | solution.py:232
  30.5 20.1 %collective-permute-start.6 = (bf16[384,512]{1,0:T(8,128)(2,1)}, bf16[384,512]{1,0:T(8,128)(2,1)}, u32[]{:S(2)}, u32[]{:S(2)}) collective-permute-start(bf16[384,512]{1,0:T(8,128)(2,1)} %get-tuple-element.64), channel_id=1, source_target_pairs={{0,64},{32,96},{64,0},{96,32},{1,65},{33,97},{65,1},{97,33},{2,66}... | collective-permute-start | bytes 1179656 | tf_op jit(solution)/shard_map/ppermute | solution.py:232
  31.6 19.5 %collective-permute-start.7 = (bf16[384,512]{1,0:T(8,128)(2,1)}, bf16[384,512]{1,0:T(8,128)(2,1)}, u32[]{:S(2)}, u32[]{:S(2)}) collective-permute-start(bf16[384,512]{1,0:T(8,128)(2,1)} %get-tuple-element.65), channel_id=1, source_target_pairs={{0,96},{32,0},{64,32},{96,64},{1,97},{33,1},{65,33},{97,65},{2,98}... | collective-permute-start | bytes 1179656 | tf_op jit(solution)/shard_map/ppermute | solution.py:232
  32.9 2.1 %collective-permute-start.4 = (bf16[512,256]{1,0:T(8,128)(2,1)S(1)}, bf16[512,256]{1,0:T(8,128)(2,1)S(1)}, u32[]{:S(2)}, u32[]{:S(2)}) collective-permute-start(bf16[512,256]{1,0:T(8,128)(2,1)S(1)} %collective-permute-done.2.w2b), channel_id=1, source_target_pairs={{0,1},{1,0},{2,3},{3,2},{4,5},{5,4},{6,7},{7,6},{8,9},{9,8},{10,11... | collective-permute-start | bytes 786440 | tf_op jit(solution)/shard_map/ppermute | solution.py:229
  39.1 27.7 %all-to-all-start.1 = ((bf16[8,48,768]{2,1,0:T(8,128)(2,1)}), bf16[8,48,768]{2,1,0:T(8,128)(2,1)S(1)}, u32[]{:S(2)}, u32[]{:S(2)}) async-start(bf16[8,48,768]{2,1,0:T(8,128)(2,1)} %embed.1), calls=%async_computation.1 | async-start | bytes 1179648 | tf_op jit(solution)/shard_map/all_to_all | solution.py:31
  52.4 18.9 %collective-permute-start.8 = (f16[384,512]{1,0:T(8,128)(2,1)S(1)}, f16[384,512]{1,0:T(8,128)(2,1)S(1)}, u32[]{:S(2)}, u32[]{:S(2)}) collective-permute-start(f16[384,512]{1,0:T(8,128)(2,1)S(1)} %get-tuple-element.82), channel_id=1, source_target_pairs={{0,128},{128,0},{1,129},{129,1},{2,130},{130,2},{3,131},{131,3},{4... | collective-permute-start | bytes 1179656 | tf_op jit(solution)/shard_map/ppermute | solution.py:229
  67.7 22.9 %all-to-all-start.2 = ((bf16[8,48,768]{2,1,0:T(8,128)(2,1)}), bf16[8,48,768]{2,1,0:T(8,128)(2,1)S(1)}, u32[]{:S(2)}, u32[]{:S(2)}) async-start(bf16[8,48,768]{2,1,0:T(8,128)(2,1)} %add_copies.1), calls=%async_computation.2 | async-start | bytes 1179648 | tf_op jit(solution)/shard_map/all_to_all | solution.py:31
  71.4 20.8 %collective-permute-start.10 = (f16[384,512]{1,0:T(8,128)(2,1)S(1)}, f16[384,512]{1,0:T(8,128)(2,1)S(1)}, u32[]{:S(2)}, u32[]{:S(2)}) collective-permute-start(f16[384,512]{1,0:T(8,128)(2,1)S(1)} %get-tuple-element.84), channel_id=1, source_target_pairs={{0,64},{32,96},{64,0},{96,32},{1,65},{33,97},{65,1},{97,33},{2,66}... | collective-permute-start | bytes 1179656 | tf_op jit(solution)/shard_map/ppermute | solution.py:232
  73.7 18.4 %collective-permute-start.11 = (f16[384,512]{1,0:T(8,128)(2,1)S(1)}, f16[384,512]{1,0:T(8,128)(2,1)}, u32[]{:S(2)}, u32[]{:S(2)}) collective-permute-start(f16[384,512]{1,0:T(8,128)(2,1)S(1)} %get-tuple-element.84), channel_id=1, source_target_pairs={{0,96},{32,0},{64,32},{96,64},{1,97},{33,1},{65,33},{97,65},{2,98}... | collective-permute-start | bytes 1179656 | tf_op jit(solution)/shard_map/ppermute | solution.py:232
  74.4 18.2 %collective-permute-start.9 = (f16[384,512]{1,0:T(8,128)(2,1)S(1)}, f16[384,512]{1,0:T(8,128)(2,1)}, u32[]{:S(2)}, u32[]{:S(2)}) collective-permute-start(f16[384,512]{1,0:T(8,128)(2,1)S(1)} %get-tuple-element.84), channel_id=1, source_target_pairs={{0,32},{32,64},{64,96},{96,0},{1,33},{33,65},{65,97},{97,1},{2,34}... | collective-permute-start | bytes 1179656 | tf_op jit(solution)/shard_map/ppermute | solution.py:232
  90.6 8.2 %collective-permute-start.15 = (bf16[4,48,768]{2,1,0:T(8,128)(2,1)S(1)}, bf16[4,48,768]{2,1,0:T(8,128)(2,1)S(1)}, u32[]{:S(2)}, u32[]{:S(2)}) collective-permute-start(bf16[4,48,768]{2,1,0:T(8,128)(2,1)S(1)} %get-tuple-element.69.refs_1_), channel_id=1, source_target_pairs={{0,2},{2,0},{1,3},{3,1},{4,6},{6,4},{5,7},{7,5},{8,10},{10,8},{9,1... | collective-permute-start | bytes 884744 | tf_op jit(solution)/shard_map/ppermute | solution.py:229
  91.6 16.1 %copy-start.3 = (f32[32,8,256]{2,1,0:T(8,128)S(1)}, f32[32,8,256]{2,1,0:T(8,128)}, u32[]{:S(2)}) copy-start(f32[32,8,256]{2,1,0:T(8,128)} %copy-done.1) | copy-start | bytes 786436
  91.6 16.1 %copy-start.4 = (f32[384,256]{1,0:T(8,128)S(1)}, f32[384,256]{1,0:T(8,128)}, u32[]{:S(2)}) copy-start(f32[384,256]{1,0:T(8,128)} %get-tuple-element.50.pa) | copy-start | bytes 1179652
  91.6 16.1 %copy-start.5 = (f32[384,256]{1,0:T(8,128)S(1)}, f32[384,256]{1,0:T(8,128)}, u32[]{:S(2)}) copy-start(f32[384,256]{1,0:T(8,128)} %get-tuple-element.51.pb) | copy-start | bytes 1179652
  91.6 13.5 %collective-permute-start.14 = (bf16[4,48,768]{2,1,0:T(8,128)(2,1)S(1)}, bf16[4,48,768]{2,1,0:T(8,128)(2,1)S(1)}, u32[]{:S(2)}, u32[]{:S(2)}) collective-permute-start(bf16[4,48,768]{2,1,0:T(8,128)(2,1)S(1)} %get-tuple-element.68.refs_0_), channel_id=1, source_target_pairs={{0,2},{2,0},{1,3},{3,1},{4,6},{6,4},{5,7},{7,5},{8,10},{10,8},{9,1... | collective-permute-start | bytes 884744 | tf_op jit(solution)/shard_map/ppermute | solution.py:229
  93.7 12.7 %collective-permute-start.12 = (bf16[4,48,768]{2,1,0:T(8,128)(2,1)S(1)}, bf16[4,48,768]{2,1,0:T(8,128)(2,1)S(1)}, u32[]{:S(2)}, u32[]{:S(2)}) collective-permute-start(bf16[4,48,768]{2,1,0:T(8,128)(2,1)S(1)} %get-tuple-element.68.refs_0_), channel_id=1, source_target_pairs={{0,1},{1,0},{2,3},{3,2},{4,5},{5,4},{6,7},{7,6},{8,9},{9,8},{10,11... | collective-permute-start | bytes 884744 | tf_op jit(solution)/shard_map/ppermute | solution.py:229
  94.5 12.0 %collective-permute-start.13 = (bf16[4,48,768]{2,1,0:T(8,128)(2,1)S(1)}, bf16[4,48,768]{2,1,0:T(8,128)(2,1)S(1)}, u32[]{:S(2)}, u32[]{:S(2)}) collective-permute-start(bf16[4,48,768]{2,1,0:T(8,128)(2,1)S(1)} %get-tuple-element.69.refs_1_), channel_id=1, source_target_pairs={{0,1},{1,0},{2,3},{3,2},{4,5},{5,4},{6,7},{7,6},{8,9},{9,8},{10,11... | collective-permute-start | bytes 884744 | tf_op jit(solution)/shard_map/ppermute | solution.py:229
  98.8 7.7 %collective-permute-start.17 = (bf16[4,48,768]{2,1,0:T(8,128)(2,1)S(1)}, bf16[4,48,768]{2,1,0:T(8,128)(2,1)S(1)}, u32[]{:S(2)}, u32[]{:S(2)}) collective-permute-start(bf16[4,48,768]{2,1,0:T(8,128)(2,1)S(1)} %collective-permute-done.15.refs_5_), channel_id=1, source_target_pairs={{0,1},{1,0},{2,3},{3,2},{4,5},{5,4},{6,7},{7,6},{8,9},{9,8},{10,11... | collective-permute-start | bytes 884744 | tf_op jit(solution)/shard_map/ppermute | solution.py:229
  105.1 2.5 %collective-permute-start.16 = (bf16[4,48,768]{2,1,0:T(8,128)(2,1)S(1)}, bf16[4,48,768]{2,1,0:T(8,128)(2,1)S(1)}, u32[]{:S(2)}, u32[]{:S(2)}) collective-permute-start(bf16[4,48,768]{2,1,0:T(8,128)(2,1)S(1)} %collective-permute-done.14.refs_4_), channel_id=1, source_target_pairs={{0,1},{1,0},{2,3},{3,2},{4,5},{5,4},{6,7},{7,6},{8,9},{9,8},{10,11... | collective-permute-start | bytes 884744 | tf_op jit(solution)/shard_map/ppermute | solution.py:229
  (6 other events, 48.3 us)
